TPU v7x, 32 devices: a whole 2x2x4 slice. The times are simulated.
32 devices in a mesh: dp: 16 (over z, y, core), head: 2 (over x).
Axes of the slice: x: 2, y: 2, z: 4, core: 2. Of those that a mesh axis runs over, the one named last changes fastest.
Arguments:
- media_tokens: bfloat16 [256, 256, 1024], P('dp'), may hold values from -6 to 6
- latents: bfloat16 [256, 64, 1024], P('dp'), may hold values from -6 to 6
- cotangent: bfloat16 [256, 64, 1024], P('dp'), may hold values from -6 to 6
- image_counts: int32 [128], P('dp'), may hold values from 1 to 2, as said below
- media_gain: float32 [1024], replicated, may hold values from 0.1 to 1.9
- media_bias: float32 [1024], replicated, may hold values from -3 to 3
- latent_gain: float32 [1024], replicated, may hold values from 0.1 to 1.9
- latent_bias: float32 [1024], replicated, may hold values from -3 to 3
- ff_gain: float32 [1024], replicated, may hold values from 0.1 to 1.9
- ff_bias: float32 [1024], replicated, may hold values from -3 to 3
- w_query: bfloat16 [1024, 512], P('dp', 'head'), may hold values from -0.1875 to 0.1875
- w_keyval: bfloat16 [1024, 2, 512], P('dp', None, 'head'), may hold values from -0.1875 to 0.1875
- w_attn_out: bfloat16 [512, 1024], P('head', 'dp'), may hold values from -1 to 1
- w_up: bfloat16 [1024, 4096], P('dp', 'head'), may hold values from -0.1875 to 0.1875
- w_down: bfloat16 [4096, 1024], P('head', 'dp'), may hold values from -0.09375 to 0.09375
Outputs:
- latents_out: float32 [256, 64, 1024], P('dp', 'head')
- media_grad: float32 [256, 256, 1024], P('dp', 'head')
- latent_grad: float32 [256, 64, 1024], P('dp', 'head')
- grad_query: float32 [1024, 512], P('dp', 'head')
- grad_keyval: float32 [1024, 2, 512], P('dp', None, 'head')
- grad_attn_out: float32 [512, 1024], P('head', 'dp')
- grad_up: float32 [1024, 4096], P('dp', 'head')
- grad_down: float32 [4096, 1024], P('head', 'dp')
- norm_grads: float32 [6, 1024], replicated
Inputs may be any that keep to these rules, and one draw needn't show every extreme that they name: `image_counts`: samples are stored in order, 8 to each index of dp. The images of a dp index's samples fill its 16 slots from slot 0 on, sample after sample; the other slots of that index are empty. In every draw some sample has 2 images and some dp index has all its slots filled.
All inputs are finite; a program needn't handle non-finite values.
Results may differ from a plain program's by a relative error of at most 0.019.
Values may be sent and summed in bfloat16 or wider, within the bound.
No kernel may reach another device: no remote copies, remote signals or barrier semaphores. Data moves between devices by JAX's collectives and lax.ppermute only.
A program may use at most 192 MiB of HBM per device.

v0:
```python
import math

import jax
import jax.numpy as jnp
from jax import lax
from jax.sharding import PartitionSpec as P

HD = 64


def layer_norm(values, gain, bias):
    centre = values - jnp.mean(values, axis=-1, keepdims=True)
    spread = jnp.mean(centre * centre, axis=-1, keepdims=True)
    return centre * lax.rsqrt(spread + 1e-05) * gain + bias


def norm_back(values, gain, bias, grad):
    result, pull = jax.vjp(layer_norm, values, gain, bias)
    return pull(grad)


def gelu_exact(values):
    return jax.nn.gelu(values, approximate=False)


def row_share(values, count):
    start = lax.axis_index("head") * count
    return lax.dynamic_slice_in_dim(values, start, count, 1)


def local(
    media_tokens,
    latents,
    cotangent,
    image_counts,
    media_gain,
    media_bias,
    latent_gain,
    latent_bias,
    ff_gain,
    ff_bias,
    w_query,
    w_keyval,
    w_attn_out,
    w_up,
    w_down,
):
    images, patches = (media_tokens.shape[0], media_tokens.shape[1])
    lat_rows = latents.shape[1]
    head_count = w_query.shape[1] // HD
    head_groups = lax.axis_size("head")
    patch_share = patches // head_groups
    lat_share = lat_rows // head_groups
    score_scale = 1.0 / math.sqrt(HD)
    live_mask = (jnp.arange(images, dtype=jnp.int32) < jnp.sum(image_counts)).astype(jnp.float32)[
        :, None, None
    ]
    query_all, keyval_all, up_all = (
        lax.all_gather(w_query, "dp", axis=0, tiled=True),
        lax.all_gather(w_keyval, "dp", axis=0, tiled=True),
        lax.all_gather(w_up, "dp", axis=0, tiled=True),
    )
    attn_all, down_all = (
        lax.all_gather(w_attn_out, "dp", axis=1, tiled=True),
        lax.all_gather(w_down, "dp", axis=1, tiled=True),
    )
    media_full = media_tokens.astype(jnp.float32)
    latent_full = latents.astype(jnp.float32)
    normed_media = layer_norm(media_full, media_gain, media_bias).astype(jnp.bfloat16)
    normed_lat = layer_norm(latent_full, latent_gain, latent_bias).astype(jnp.bfloat16)
    sources = jnp.concatenate([normed_media, normed_lat], axis=1)
    src_rows = sources.shape[1]
    query_act = jnp.einsum(
        "ild,dc->ilc", normed_lat, query_all, preferred_element_type=jnp.float32
    ).astype(jnp.bfloat16)
    keyval = jnp.einsum(
        "ird,dkc->ikrc", sources, keyval_all, preferred_element_type=jnp.float32
    ).astype(jnp.bfloat16)
    query_blocks = query_act.reshape(images, lat_rows, head_count, HD)
    key_blocks = keyval[:, 0].reshape(images, src_rows, head_count, HD)
    value_blocks = keyval[:, 1].reshape(images, src_rows, head_count, HD)
    scores = (
        jnp.einsum("ilhe,irhe->ihlr", query_blocks, key_blocks, preferred_element_type=jnp.float32)
        * score_scale
    )
    row_top = jnp.max(scores, axis=-1, keepdims=True)
    exp_terms = jnp.exp(scores - row_top)
    row_total = jnp.sum(exp_terms, axis=-1, keepdims=True)
    probs_low = (exp_terms / row_total).astype(jnp.bfloat16)
    log_total = row_top + jnp.log(row_total)
    mixed_heads = (
        jnp.einsum("ihlr,irhe->ilhe", probs_low, value_blocks, preferred_element_type=jnp.float32)
        .astype(jnp.bfloat16)
        .reshape(images, lat_rows, head_count * HD)
    )
    attn_part = jnp.einsum("ilc,cd->ild", mixed_heads, attn_all, preferred_element_type=jnp.float32)
    middle = latent_full + lax.psum(attn_part.astype(jnp.bfloat16), "head").astype(jnp.float32)
    normed_mid = layer_norm(middle, ff_gain, ff_bias).astype(jnp.bfloat16)
    up_act = jnp.einsum("ild,df->ilf", normed_mid, up_all, preferred_element_type=jnp.float32)
    hidden, gelu_pull = jax.vjp(gelu_exact, up_act)
    hidden_low = hidden.astype(jnp.bfloat16)
    ff_part = jnp.einsum("ilf,fd->ild", hidden_low, down_all, preferred_element_type=jnp.float32)
    final_lat = middle + lax.psum(ff_part.astype(jnp.bfloat16), "head").astype(jnp.float32)
    latent_rows_share = row_share(latent_full, lat_share)
    latents_out = jnp.where(live_mask > 0, row_share(final_lat, lat_share), latent_rows_share)
    grad_final = cotangent.astype(jnp.float32) * live_mask
    final_low = grad_final.astype(jnp.bfloat16)
    grad_down = jnp.einsum("ilf,ild->fd", hidden_low, final_low, preferred_element_type=jnp.float32)
    grad_hidden = jnp.einsum("ild,fd->ilf", final_low, down_all, preferred_element_type=jnp.float32)
    up_low = gelu_pull(grad_hidden)[0].astype(jnp.bfloat16)
    grad_up = jnp.einsum("ild,ilf->df", normed_mid, up_low, preferred_element_type=jnp.float32)
    mid_part = jnp.einsum("ilf,df->ild", up_low, up_all, preferred_element_type=jnp.float32)
    grad_normed_mid = lax.psum(mid_part.astype(jnp.bfloat16), "head").astype(jnp.float32)
    mid_back, ff_gain_grad, ff_bias_grad = norm_back(middle, ff_gain, ff_bias, grad_normed_mid)
    grad_mid = grad_final + mid_back
    mid_low = grad_mid.astype(jnp.bfloat16)
    grad_attn = jnp.einsum("ilc,ild->cd", mixed_heads, mid_low, preferred_element_type=jnp.float32)
    grad_mixed = (
        jnp.einsum("ild,cd->ilc", mid_low, attn_all, preferred_element_type=jnp.float32)
        .astype(jnp.bfloat16)
        .reshape(images, lat_rows, head_count, HD)
    )
    scores_again = (
        jnp.einsum("ilhe,irhe->ihlr", query_blocks, key_blocks, preferred_element_type=jnp.float32)
        * score_scale
    )
    attn_probs = jnp.exp(scores_again - log_total)
    grad_values = jnp.einsum(
        "ihlr,ilhe->irhe", probs_low, grad_mixed, preferred_element_type=jnp.float32
    ).astype(jnp.bfloat16)
    grad_probs = jnp.einsum(
        "ilhe,irhe->ihlr", grad_mixed, value_blocks, preferred_element_type=jnp.float32
    )
    grad_scores = (
        attn_probs * (grad_probs - jnp.sum(attn_probs * grad_probs, axis=-1, keepdims=True))
    ).astype(jnp.bfloat16)
    grad_query_act = (
        (
            jnp.einsum(
                "ihlr,irhe->ilhe", grad_scores, key_blocks, preferred_element_type=jnp.float32
            )
            * score_scale
        )
        .astype(jnp.bfloat16)
        .reshape(images, lat_rows, head_count * HD)
    )
    grad_keys = (
        jnp.einsum("ihlr,ilhe->irhe", grad_scores, query_blocks, preferred_element_type=jnp.float32)
        * score_scale
    ).astype(jnp.bfloat16)
    grad_keyval_act = jnp.stack(
        [
            grad_keys.reshape(images, src_rows, head_count * HD),
            grad_values.reshape(images, src_rows, head_count * HD),
        ],
        axis=1,
    )
    grad_query = jnp.einsum(
        "ild,ilc->dc", normed_lat, grad_query_act, preferred_element_type=jnp.float32
    )
    grad_keyval = jnp.einsum(
        "ird,ikrc->dkc", sources, grad_keyval_act, preferred_element_type=jnp.float32
    )
    lat_part = jnp.einsum(
        "ikrc,dkc->ird",
        grad_keyval_act[:, :, patches:],
        keyval_all,
        preferred_element_type=jnp.float32,
    )
    lat_part = lat_part + jnp.einsum(
        "ilc,dc->ild", grad_query_act, query_all, preferred_element_type=jnp.float32
    )
    media_part = jnp.einsum(
        "ikrc,dkc->ird",
        grad_keyval_act[:, :, :patches],
        keyval_all,
        preferred_element_type=jnp.float32,
    )
    grad_normed_media, grad_normed_lat = (
        lax.psum_scatter(
            media_part.astype(jnp.bfloat16), "head", scatter_dimension=1, tiled=True
        ).astype(jnp.float32),
        lax.psum_scatter(
            lat_part.astype(jnp.bfloat16), "head", scatter_dimension=1, tiled=True
        ).astype(jnp.float32),
    )
    media_share = row_share(media_full, patch_share)
    media_grad, media_gain_grad, media_bias_grad = norm_back(
        media_share, media_gain, media_bias, grad_normed_media
    )
    lat_back, lat_gain_grad, lat_bias_grad = norm_back(
        latent_rows_share, latent_gain, latent_bias, grad_normed_lat
    )
    cot_share = row_share(cotangent.astype(jnp.float32), lat_share)
    latent_grad = jnp.where(live_mask > 0, row_share(grad_mid, lat_share) + lat_back, cot_share)
    gain_terms = jnp.stack(
        [
            media_gain_grad,
            media_bias_grad,
            lat_gain_grad,
            lat_bias_grad,
            ff_gain_grad / head_groups,
            ff_bias_grad / head_groups,
        ]
    )
    norm_grads = lax.psum(gain_terms, ("dp", "head"))
    grad_query, grad_keyval, grad_up = (
        lax.psum_scatter(
            grad_query.astype(jnp.bfloat16), "dp", scatter_dimension=0, tiled=True
        ).astype(jnp.float32),
        lax.psum_scatter(
            grad_keyval.astype(jnp.bfloat16), "dp", scatter_dimension=0, tiled=True
        ).astype(jnp.float32),
        lax.psum_scatter(
            grad_up.astype(jnp.bfloat16), "dp", scatter_dimension=0, tiled=True
        ).astype(jnp.float32),
    )
    grad_attn, grad_down = (
        lax.psum_scatter(
            grad_attn.astype(jnp.bfloat16), "dp", scatter_dimension=1, tiled=True
        ).astype(jnp.float32),
        lax.psum_scatter(
            grad_down.astype(jnp.bfloat16), "dp", scatter_dimension=1, tiled=True
        ).astype(jnp.float32),
    )
    return (
        latents_out,
        media_grad,
        latent_grad,
        grad_query,
        grad_keyval,
        grad_attn,
        grad_up,
        grad_down,
        norm_grads,
    )


def solution(mesh):
    return jax.shard_map(
        local,
        mesh=mesh,
        in_specs=(
            P("dp", None, None),
            P("dp", None, None),
            P("dp", None, None),
            P("dp"),
            P(),
            P(),
            P(),
            P(),
            P(),
            P(),
            P("dp", "head"),
            P("dp", None, "head"),
            P("head", "dp"),
            P("dp", "head"),
            P("head", "dp"),
        ),
        out_specs=(
            P("dp", "head", None),
            P("dp", "head", None),
            P("dp", "head", None),
            P("dp", "head"),
            P("dp", None, "head"),
            P("head", "dp"),
            P("dp", "head"),
            P("head", "dp"),
            P(),
        ),
        check_vma=False,
    )
```

profile of v0, /device:TPU:0, one launch (start us, length us, event | category | flops | bytes accessed | tf_op | source)
XLA Modules:
  0.0 991.0 jit_solution(9586764897184007495)
XLA Ops:
  8.8 1.9 convert_reduce_fusion.3
  10.7 2.3 multiply_reduce_fusion.5
  13.0 4.7 convert_reduce_fusion.1
  18.8 2.8 multiply_reduce_fusion
  21.6 25.3 %all_gather.16 = bf16[1024,256]{1,0:T(8,128)(2,1)S(1)} all-gather(bf16[64,256]{1,0:T(8,128)(2,1)S(1)} %copy-done.29), channel_id=1, replica_groups=mesh['dp'=16,'head'=2] {'dp'}, dimensions={0}, use_global_device_ids=true | all-gather | bytes 557056 | tf_op jit(solution)/shard_map/all_gather | solution.py:59
  52.2 20.5 %all_gather.17 = bf16[256,1024]{0,1:T(8,128)(2,1)} all-gather(bf16[256,64]{0,1:T(8,128)(2,1)S(1)} %copy-done.30), channel_id=1, replica_groups=mesh['dp'=16,'head'=2] {'dp'}, dimensions={1}, use_global_device_ids=true | all-gather | bytes 557056 | tf_op jit(solution)/shard_map/all_gather | solution.py:64
  72.7 8.6 add_convert_fusion
  81.2 8.6 convert_bitcast_fusion
  89.9 2.7 fusion.66
  92.6 4.5 copy.43
  97.1 3.1 multiply_reduce_fusion.3
  101.9 2.6 divide_convert_fusion
  104.4 4.5 copy.42
  109.0 4.1 convolution_convert_fusion.2
  114.1 2.6 convolution_convert_fusion.1
  119.7 58.9 %all-reduce.4.cloned.1.call-done = bf16[16,64,1024]{2,1,0:T(8,128)(2,1)} async-done(((bf16[16,64,1024]{2,1,0:T(8,128)(2,1)}), bf16[16,64,1024]{2,1,0:T(8,128)(2,1)}) %all-reduce.4.cloned.1.call-update) | async-done | bytes 2097168 | tf_op jit(solution)/shard_map/psum | solution.py:97
  178.6 2.4 fusion.64
  181.9 49.7 %all-gather.6.cloned.1.call-done = bf16[1024,2048]{1,0:T(8,128)(2,1)} async-done(((bf16[64,2048]{1,0:T(8,128)(2,1)}), bf16[1024,2048]{1,0:T(8,128)(2,1)}) %all-gather.6.cloned.1.call-update) | async-done | bytes 4194320 | tf_op jit(solution)/shard_map/all_gather | solution.py:61
  231.6 9.4 fusion.28
  240.9 3.2 copy-done.11
  244.1 20.1 %multiply_convert_fusion = (bf16[16,64,2048]{2,1,0:T(8,128)(2,1)}, f32[16,64,2048]{2,1,0:T(8,128)}) fusion(f32[16,64,2048]{2,1,0:T(8,128)S(1)} %get-tuple-element.59, u16[64,2048]{1,0:T(8,128)(2,1)S(1)} %get-tuple-element.32, u16[64,2048]{1,0:T(8,128)(2,1)S(1)} %get-tuple-element.31), kind=kLoop, calls=%fused_computation.24 | loop fusion | flops 146800640 | bytes 21495808 | tf_op jit(solution)/shard_map/convert_element_type | solution.py:101
  264.2 18.6 %all-gather.8.cloned.1.call-done = bf16[2048,1024]{0,1:T(8,128)(2,1)} async-done(((bf16[2048,64]{0,1:T(8,128)(2,1)}), bf16[2048,1024]{0,1:T(8,128)(2,1)}) %all-gather.8.cloned.1.call-update) | async-done | bytes 4194320 | tf_op jit(solution)/shard_map/all_gather | solution.py:65
  282.9 12.8 %add_convert_fusion.1 = bf16[16,64,2048]{2,1,0:T(8,128)(2,1)S(1)} fusion(f32[16,64,2048]{2,1,0:T(8,128)} %get-tuple-element.46, f32[16,64,2048]{2,1,0:T(8,128)} %copy-done.11, bf16[2048,1024]{0,1:T(8,128)(2,1)} %all-gather.8.cloned.1.call-done, f32[16]{0:T(128)S(1)} %compare_convert_fusion, bf16[16,64,1024]{2,1,0:T(8,128)(2,1)} %param.17), kind=kOutput, calls=%fused_computation.23 | convolution fusion | flops 4327473152 | bytes 27263040 | tf_op jit(solution)/shard_map/ild,fd->ilf/dot_general | solution.py:109
  295.8 5.7 fusion.35
  301.5 5.8 fusion.38
  307.4 106.8 %all-reduce.6.cloned.1.call-done = (bf16[16,64,1024]{2,1,0:T(8,128)(2,1)}, bf16[16,64,1024]{2,1,0:T(8,128)(2,1)}) async-done(((bf16[16,64,1024]{2,1,0:T(8,128)(2,1)}, bf16[16,64,1024]{2,1,0:T(8,128)(2,1)}), (bf16[16,64,1024]{2,1,0:T(8,128)(2,1)}, bf16[16,64,1024]{2,1,0:T(8,128)(2,1)})) %all-reduce.6.cloned.1.call-update) | async-done | bytes 4194320 | tf_op jit(solution)/shard_map/psum | solution.py:113
  414.2 4.2 convert_reduce_fusion.2
  418.4 2.8 fusion.16
  421.3 3.3 add_add_fusion.2
  426.8 2.5 fusion.43
  429.4 2.4 copy.65
  431.7 4.9 convolution_convert_fusion
  436.6 4.6 copy.50
  441.2 6.8 multiply_reduce_fusion.2
  451.4 2.7 multiply_convert_fusion.1
  454.1 4.6 copy.49
  459.0 4.2 multiply_convert_fusion.4
  463.2 2.1 fusion.42
  465.5 10.8 %bitcast_convert_fusion.3 = bf16[1024,2,256]{2,0,1:T(8,128)(2,1)} fusion(bf16[16,1,320,256]{3,2,1,0:T(8,128)(2,1)} %copy.50, bf16[16,1,320,256]{3,2,1,0:T(8,128)(2,1)} %copy.49, bf16[16,64,1024]{2,1,0:T(8,128)(2,1)} %copy-done.19, bf16[16,256,1024]{2,1,0:T(8,128)(2,1)} %add_convert_fusion), kind=kOutput, calls=%fused_computation.96 | convolution fusion | flops 5400690688 | bytes 16777216 | tf_op jit(solution)/shard_map/ird,ikrc->dkc/dot_general | solution.py:161
  476.3 9.7 bitcast_convert_fusion.2
  486.6 9.5 bitcast_convert_fusion.1
  496.1 2.9 fusion.45
  499.0 2.7 fusion.20
  501.9 10.5 %bitcast_convert_fusion = bf16[16,256,1024]{2,1,0:T(8,128)(2,1)} fusion(bf16[16,1,320,256]{3,2,1,0:T(8,128)(2,1)} %copy.49, bf16[16,1,320,256]{3,2,1,0:T(8,128)(2,1)} %copy.50, bf16[1024,2,256]{2,0,1:T(8,128)(2,1)} %all-gather.4.cloned.1.call-done), kind=kOutput, calls=%fused_computation | convolution fusion | flops 4301258752 | bytes 14680064 | tf_op jit(solution)/shard_map/ikrc,dkc->ird/dot_general | solution.py:173
  512.5 11.3 %convert_element_type.145 = f32[16,256,1024]{2,1,0:T(8,128)} convert(bf16[16,256,1024]{2,1,0:T(8,128)(2,1)} %param.15) | non-fusion elementwise | flops 4194304 | bytes 25165824 | tf_op jit(solution)/shard_map/convert_element_type | solution.py:67
  523.8 2.6 convert_element_type.144
  526.3 2.5 convert_element_type.160
  528.8 1.8 dynamic-slice_reduce_fusion.1
  530.6 3.9 dynamic-slice_reduce_fusion
  536.8 37.3 %reduce-scatter.12.cloned.1.call-done = bf16[64,256]{1,0:T(8,128)(2,1)} async-done(((bf16[1024,256]{1,0:T(8,128)(2,1)}), bf16[64,256]{1,0:T(8,128)(2,1)}) %reduce-scatter.12.cloned.1.call-update) | async-done | bytes 32784 | tf_op jit(solution)/shard_map/reduce_scatter | solution.py:208
  575.4 59.3 %reduce-scatter.14.cloned.1.call-done = bf16[64,2,256]{2,0,1:T(8,128)(2,1)} async-done(((bf16[1024,2,256]{2,0,1:T(8,128)(2,1)}), bf16[64,2,256]{2,0,1:T(8,128)(2,1)}) %reduce-scatter.14.cloned.1.call-update) | async-done | bytes 65552 | tf_op jit(solution)/shard_map/reduce_scatter | solution.py:211
  636.3 74.1 %reduce-scatter.18.cloned.1.call-done = bf16[64,2048]{1,0:T(8,128)(2,1)} async-done(((bf16[1024,2048]{1,0:T(8,128)(2,1)}), bf16[64,2048]{1,0:T(8,128)(2,1)}) %reduce-scatter.18.cloned.1.call-update) | async-done | bytes 262160 | tf_op jit(solution)/shard_map/reduce_scatter | solution.py:214
  710.4 1.8 convert_element_type.185
  712.2 73.5 %reduce-scatter.20.cloned.1.call-done = bf16[2048,64]{0,1:T(8,128)(2,1)} async-done(((bf16[2048,1024]{0,1:T(8,128)(2,1)}), bf16[2048,64]{0,1:T(8,128)(2,1)}) %reduce-scatter.20.cloned.1.call-update) | async-done | bytes 262160 | tf_op jit(solution)/shard_map/reduce_scatter | solution.py:222
  785.7 1.8 convert_element_type.187
  787.4 32.0 %reduce-scatter.10.cloned.1.call-done = bf16[16,32,1024]{2,1,0:T(8,128)(2,1)} async-done(((bf16[16,64,1024]{2,1,0:T(8,128)(2,1)}), bf16[16,32,1024]{2,1,0:T(8,128)(2,1)}) %reduce-scatter.10.cloned.1.call-update) | async-done | bytes 1048592 | tf_op jit(solution)/shard_map/reduce_scatter | solution.py:183
  819.5 2.9 multiply_reduce_fusion.6
  822.4 3.1 fusion.33
  825.6 5.3 dynamic-slice_select_fusion
  830.9 90.6 %reduce-scatter.8.cloned.1.call-done = bf16[16,128,1024]{2,1,0:T(8,128)(2,1)} async-done(((bf16[16,256,1024]{2,1,0:T(8,128)(2,1)}), bf16[16,128,1024]{2,1,0:T(8,128)(2,1)}) %reduce-scatter.8.cloned.1.call-update) | async-done | bytes 4194320 | tf_op jit(solution)/shard_map/reduce_scatter | solution.py:180
  921.5 7.5 multiply_reduce_fusion.1
  929.0 6.7 fusion.4
  935.8 40.1 %psum.31 = f32[6,1024]{1,0:T(8,128)} all-reduce(f32[6,1024]{1,0:T(8,128)S(1)} %stack.25), channel_id=1, replica_groups=mesh['dp'=16,'head'=2] {'dp','head'}, use_global_device_ids=true, to_apply=%region_36.37 | all-reduce | flops 6144 | bytes 49152 | tf_op jit(solution)/shard_map/psum | solution.py:206
  975.8 8.1 broadcast_add_fusion
  (138 shorter events, 26.6 us)
Async XLA Ops:
  7.2 74.1 %all-gather.4.cloned.1.call-start = ((), (), s32[]{:S(2)}) async-start(), calls=%async_computation.7 | async-start | bytes 1114112 | tf_op jit(solution)/shard_map/all_gather | solution.py:60
  8.7 169.8 %all-reduce.4.cloned.1.call-start = ((), (), s32[]{:S(2)}) async-start(), calls=%async_computation.8 | async-start | bytes 4194304 | tf_op jit(solution)/shard_map/psum | solution.py:97
  13.0 5.8 copy-start.2
  18.8 2.9 copy-start.29
  18.8 28.1 %copy-start = (bf16[16,64,1024]{2,1,0:T(8,128)(2,1)S(1)}, bf16[16,64,1024]{2,1,0:T(8,128)(2,1)}, u32[]{:S(2)}) copy-start(bf16[16,64,1024]{2,1,0:T(8,128)(2,1)} %param.16) | copy-start | bytes 6291460
  18.8 28.1 %copy-start.24 = (f32[1024]{0:T(1024)S(1)}, f32[1024]{0:T(1024)}, u32[]{:S(2)}) copy-start(f32[1024]{0:T(1024)} %param.21) | copy-start | bytes 12292
  18.8 28.1 %copy-start.31 = (f32[1024]{0:T(1024)S(1)}, f32[1024]{0:T(1024)}, u32[]{:S(2)}) copy-start(f32[1024]{0:T(1024)} %param.22) | copy-start | bytes 12292
  46.9 0.9 copy-start.21
  46.9 5.3 copy-start.30
  46.9 25.7 %copy-start.26 = (f32[1024]{0:T(1024)S(1)}, f32[1024]{0:T(1024)}, u32[]{:S(2)}) copy-start(f32[1024]{0:T(1024)} %param.19) | copy-start | bytes 12292
  47.0 25.7 %copy-start.32 = (f32[1024]{0:T(1024)S(1)}, f32[1024]{0:T(1024)}, u32[]{:S(2)}) copy-start(f32[1024]{0:T(1024)} %param.20) | copy-start | bytes 12292
  47.8 1.3 copy-start.19
  100.2 4.3 copy-start.1
  109.0 5.1 copy-start.14
  113.1 1.0 copy-start.16
  113.1 5.2 copy-start.36
  116.7 114.8 %all-gather.6.cloned.1.call-start = ((), (), s32[]{:S(2)}) async-start(), calls=%async_computation.9 | async-start | bytes 4456448 | tf_op jit(solution)/shard_map/all_gather | solution.py:61
  117.5 165.4 %all-gather.8.cloned.1.call-start = ((), (), s32[]{:S(2)}) async-start(), calls=%async_computation.10 | async-start | bytes 4456448 | tf_op jit(solution)/shard_map/all_gather | solution.py:65
  118.1 296.1 %all-reduce.6.cloned.1.call-start = ((), (), s32[]{:S(2)}) async-start(), calls=%async_computation.18 | async-start | bytes 8388608 | tf_op jit(solution)/shard_map/psum | solution.py:113
  119.7 111.9 %copy-start.28 = (f32[1024]{0:T(1024)S(1)}, f32[1024]{0:T(1024)}, u32[]{:S(2)}) copy-start(f32[1024]{0:T(1024)} %param.23) | copy-start | bytes 12292
  119.7 111.9 %copy-start.35 = (f32[1024]{0:T(1024)S(1)}, f32[1024]{0:T(1024)}, u32[]{:S(2)}) copy-start(f32[1024]{0:T(1024)} %param.24) | copy-start | bytes 12292
  178.6 2.4 copy-start.3
  240.9 3.2 copy-start.11
  282.9 12.8 %copy-start.33 = (bf16[1024,2048]{1,0:T(8,128)(2,1)S(1)}, bf16[1024,2048]{1,0:T(8,128)(2,1)}, u32[]{:S(2)}) copy-start(bf16[1024,2048]{1,0:T(8,128)(2,1)} %all-gather.6.cloned.1.call-done) | copy-start | bytes 12582916
  295.7 5.8 copy-start.37
  295.7 5.8 copy-start.18
  295.8 5.8 copy-start.34
  307.3 227.9 %reduce-scatter.16.cloned.1.call-start = ((), (), s32[]{:S(2)}) async-start(), calls=%async_computation.15 | async-start | bytes 557056 | tf_op jit(solution)/shard_map/reduce_scatter | solution.py:219
  414.2 4.2 copy-start.4
  414.2 4.2 copy-start.9
  418.4 2.9 copy-start.12
  421.3 3.3 copy-start.15
  424.6 2.2 copy-start.8
  424.6 2.2 copy-start.17
  441.2 6.8 slice-start
  441.2 6.8 slice-start.1
  449.7 1.7 copy-start.7
  458.8 115.3 %reduce-scatter.12.cloned.1.call-start = ((), (), s32[]{:S(2)}) async-start(), calls=%async_computation.13 | async-start | bytes 557056 | tf_op jit(solution)/shard_map/reduce_scatter | solution.py:208
  459.0 4.2 copy-start.20
  465.4 169.3 %reduce-scatter.14.cloned.1.call-start = ((), (), s32[]{:S(2)}) async-start(), calls=%async_computation.14 | async-start | bytes 1114112 | tf_op jit(solution)/shard_map/reduce_scatter | solution.py:211
  476.3 234.1 %reduce-scatter.18.cloned.1.call-start = ((), (), s32[]{:S(2)}) async-start(), calls=%async_computation.16 | async-start | bytes 4456448 | tf_op jit(solution)/shard_map/reduce_scatter | solution.py:214
  486.1 299.6 %reduce-scatter.20.cloned.1.call-start = ((), (), s32[]{:S(2)}) async-start(), calls=%async_computation.17 | async-start | bytes 4456448 | tf_op jit(solution)/shard_map/reduce_scatter | solution.py:222
  496.1 323.4 %reduce-scatter.10.cloned.1.call-start = ((), (), s32[]{:S(2)}) async-start(), calls=%async_computation.12 | async-start | bytes 3145728 | tf_op jit(solution)/shard_map/reduce_scatter | solution.py:183
  496.1 2.9 copy-start.22
  501.7 419.7 %reduce-scatter.8.cloned.1.call-start = ((), (), s32[]{:S(2)}) async-start(), calls=%async_computation.11 | async-start | bytes 12582912 | tf_op jit(solution)/shard_map/reduce_scatter | solution.py:180
  523.8 2.6 copy-start.13
  530.6 288.9 %copy-start.25 = (f32[1024]{0:T(1024)S(1)}, f32[1024]{0:T(1024)}, u32[]{:S(2)}) copy-start(f32[1024]{0:T(1024)} %param.21) | copy-start | bytes 12292
  535.2 290.3 %copy-start.23 = (bf16[16,64,1024]{2,1,0:T(8,128)(2,1)S(1)}, bf16[16,64,1024]{2,1,0:T(8,128)(2,1)}, u32[]{:S(2)}) copy-start(bf16[16,64,1024]{2,1,0:T(8,128)(2,1)} %get-tuple-element.44) | copy-start | bytes 6291460
  819.5 6.1 copy-start.6
  819.5 6.1 copy-start.10
  825.5 95.9 %copy-start.27 = (f32[1024]{0:T(1024)S(1)}, f32[1024]{0:T(1024)}, u32[]{:S(2)}) copy-start(f32[1024]{0:T(1024)} %param.19) | copy-start | bytes 12292
  921.5 7.6 copy-start.5
Sparse Core Ops, SparseCore 0:
  10.8 41.0 all-gather.3
  116.9 61.6 all-reduce.3
  180.9 50.5 all-gather.5
  233.8 49.0 all-gather.7
  307.5 106.6 all-reduce.5
  458.9 55.7 reduce-scatter.15
  519.2 54.7 reduce-scatter.11
  578.2 56.4 reduce-scatter.13
  639.1 71.2 reduce-scatter.17
  714.1 71.4 reduce-scatter.19
  788.6 30.8 reduce-scatter.9
  822.2 99.2 reduce-scatter.7
where the time goes:
time: 997 us; the launch traced here: 991 us
  waiting for transfers between devices  602 us (60%)
  other arithmetic  125 us (13%)
  matrix products  124 us (12%)
  blocking collectives  85.8 us (9%)
  local copies, waits for them, and re-layouts  37 us (4%)
  between operations  15 us (2%)
    psum x1, waiting for transfers between devices, local(): lax.psum(mid_part.astype(jnp.bfloat16), 'head').astype(jnp.float32)  107 us
    reduce_scatter x1, waiting for transfers between devices, local(): lax.psum_scatter(media_part.astype(jnp.bfloat16), 'head', scatter_dimensi...  90.6 us
    reduce_scatter x1, waiting for transfers between devices, local(): lax.psum_scatter(grad_up.astype(jnp.bfloat16), 'dp', scatter_dimension=0,...  74.1 us
    reduce_scatter x1, waiting for transfers between devices, local(): lax.psum_scatter(grad_down.astype(jnp.bfloat16), 'dp', scatter_dimension=...  73.5 us
    reduce_scatter x1, waiting for transfers between devices, local(): lax.psum_scatter(grad_keyval.astype(jnp.bfloat16), 'dp', scatter_dimensio...  59.3 us
    psum x1, waiting for transfers between devices, local(): lax.psum(attn_part.astype(jnp.bfloat16), 'head').astype(jnp.float32)  58.9 us
    all_gather x1, waiting for transfers between devices, local(): lax.all_gather(w_up, 'dp', axis=0, tiled=True)  49.7 us
    psum x1, blocking collectives, local(): norm_grads = lax.psum(gain_terms, ('dp', 'head'))  40.1 us
  transfers between devices with their start and end apart: 12, of which 10 were waited for; matrix products, arithmetic and copies ran while one was open for 15% of the time, Pallas kernels for 0%

commit v1 on v0

v1 whole, which is shorter than its diff:
```python
import functools

import jax
import jax.numpy as jnp
from jax import lax
from jax.experimental import pallas as pl
from jax.experimental.pallas import tpu as pltpu
from jax.sharding import PartitionSpec as P

HD = 64
HEADS = 8
CHUNKS = 2
EPS = 1e-05
BF = jnp.bfloat16
F32 = jnp.float32
MIB = 1024 * 1024

NN = (((1,), (0,)), ((), ()))
NT = (((1,), (1,)), ((), ()))
TN = (((0,), (0,)), ((), ()))


def dot(left, right, form=NN):
    return lax.dot_general(left, right, form, preferred_element_type=F32)


def struct(shape, dtype):
    return jax.ShapeDtypeStruct(shape, dtype)


def call(kernel, grid, in_specs, out_specs, out_shape, scratch, ids, args, flops, name, vmem=48):
    outs = out_shape if isinstance(out_shape, (list, tuple)) else [out_shape]
    moved = sum(a.size * a.dtype.itemsize for a in args)
    moved += sum(o.size * jnp.dtype(o.dtype).itemsize for o in outs)
    return pl.pallas_call(
        kernel,
        grid_spec=pltpu.PrefetchScalarGridSpec(
            num_scalar_prefetch=1,
            grid=grid,
            in_specs=in_specs,
            out_specs=out_specs,
            scratch_shapes=scratch,
        ),
        out_shape=out_shape,
        compiler_params=pltpu.CompilerParams(
            vmem_limit_bytes=vmem * MIB, dimension_semantics=("arbitrary",) * len(grid)
        ),
        cost_estimate=pl.CostEstimate(
            flops=int(flops), bytes_accessed=int(moved), transcendentals=0
        ),
        name=name,
    )(ids, *args)


def whole(array):
    zeros = (0,) * array.ndim
    return pl.BlockSpec(array.shape, lambda *_: zeros)


def rows_of(block, width):
    return pl.BlockSpec((block, width), lambda i, ids: (i, 0))


def norm_parts(values):
    centre = values - jnp.mean(values, axis=-1, keepdims=True)
    rstd = lax.rsqrt(jnp.mean(centre * centre, axis=-1, keepdims=True) + EPS)
    return centre * rstd, rstd


def norm_back(values, gain, grad):
    xhat, rstd = norm_parts(values)
    scaled = grad * gain
    first = jnp.mean(scaled, axis=-1, keepdims=True)
    second = jnp.mean(scaled * xhat, axis=-1, keepdims=True)
    back = rstd * (scaled - first - xhat * second)
    return (
        back,
        jnp.sum(grad * xhat, axis=0, keepdims=True),
        jnp.sum(grad, axis=0, keepdims=True),
    )


def norm_kernel(
    imgs, lat, share, patch, ids, media, latents, m_gain, m_bias, l_gain, l_bias, src, nlat, keep
):
    start = pl.multiple_of(ids[0] * share, share)
    step = patch + share
    for i in range(imgs):
        xhat, _ = norm_parts(media[i].astype(F32))
        src[i * step : i * step + patch, :] = (xhat * m_gain[...] + m_bias[...]).astype(BF)
        xhat, _ = norm_parts(latents[i].astype(F32))
        normed = xhat * l_gain[...] + l_bias[...]
        nlat[i * lat : (i + 1) * lat, :] = normed.astype(BF)
        keep[...] = normed
        src[i * step + patch : (i + 1) * step, :] = keep[pl.ds(start, share), :].astype(BF)


def assemble(entries, pieces, depth, ids, rows, groups, width, name):
    def kernel(ids_ref, *refs):
        out, sems = refs[len(pieces)], refs[len(pieces) + 1]
        copies = []
        for e, (op, lead, group, s, yf, cf) in enumerate(entries):
            block = lax.rem(ids_ref[1] + s, depth) * 4
            block += lax.rem(ids_ref[2] + yf, 2) * 2 + lax.rem(ids_ref[3] + cf, 2)
            start = pl.multiple_of(block * rows, rows)
            source = refs[op] if lead is None else refs[op].at[lead]
            copies.append(
                pltpu.make_async_copy(source, out.at[group, pl.ds(start, rows), :], sems.at[e])
            )
        for copy in copies:
            copy.start()
        for copy in copies:
            copy.wait()

    return call(
        kernel,
        (1,),
        [pl.BlockSpec(memory_space=pl.ANY)] * len(pieces),
        pl.BlockSpec(memory_space=pl.ANY),
        struct((groups, depth * 4 * rows, width), BF),
        [pltpu.SemaphoreType.DMA((len(entries),))],
        ids,
        pieces,
        0,
        name,
        vmem=4,
    )


def diag_mask(heads, width, dtype):
    row = lax.broadcasted_iota(jnp.int32, (heads * HD, width), 0) // HD
    col = lax.broadcasted_iota(jnp.int32, (heads * HD, width), 1) // HD
    return jnp.where(row == col, 1.0, 0.0).astype(dtype)


def spread(block, heads, mask):
    return jnp.concatenate([block] * heads, axis=0) * mask


def fold(full, heads, lat, mask):
    full = full * mask
    total = full[:lat]
    for h in range(1, heads):
        total = total + full[h * lat : (h + 1) * lat]
    return total


def project_kernel(groups, cw, imgs, step, lat, ids, src, nlat, w, q, kv, stats):
    heads = cw // HD
    for j in range(groups):
        kv[:, j * 2 * cw : (j + 1) * 2 * cw] = dot(src[...], w[j, :, cw : 3 * cw]).astype(BF)
        q[:, j * cw : (j + 1) * cw] = (dot(nlat[...], w[j, :, :cw]) * (HD**-0.5)).astype(BF)
    mask = diag_mask(heads, cw, BF)
    for i in range(imgs):
        for j in range(groups):
            keys = kv[i * step : (i + 1) * step, j * 2 * cw : j * 2 * cw + cw]
            qbd = spread(q[i * lat : (i + 1) * lat, j * cw : (j + 1) * cw], heads, mask)
            score = dot(keys, qbd, NT)
            top = jnp.max(score, axis=0, keepdims=True)
            stats[i, 0:1, j * cw : (j + 1) * cw] = top
            stats[i, 1:2, j * cw : (j + 1) * cw] = jnp.sum(
                jnp.exp(score - top), axis=0, keepdims=True
            )


def send_rows(groups, share, ids, scratch, i, keep, send):
    for s in range(groups):
        start = pl.multiple_of(lax.rem(ids[0] + s, groups) * share, share)
        rows = scratch[pl.ds(start, share), :]
        if s == 0:
            keep[i * share : (i + 1) * share, :] = rows
        else:
            send[s - 1, i * share : (i + 1) * share, :] = rows.astype(BF)


def mix_kernel(groups, cw, imgs, step, lat, share, ids, q, kv, lse, keep, send, scratch):
    heads = cw // HD
    mask, fmask = diag_mask(heads, cw, BF), diag_mask(heads, cw, F32)
    for i in range(imgs):
        for j in range(groups):
            keys = kv[i * step : (i + 1) * step, j * 2 * cw : j * 2 * cw + cw]
            values = kv[i * step : (i + 1) * step, j * 2 * cw + cw : (j + 1) * 2 * cw]
            qbd = spread(q[i * lat : (i + 1) * lat, j * cw : (j + 1) * cw], heads, mask)
            probs = jnp.exp(dot(keys, qbd, NT) - lse[i, 0:1, j * cw : (j + 1) * cw])
            full = dot(probs.astype(BF), values, TN)
            scratch[i, :, j * cw : (j + 1) * cw] = fold(full, heads, lat, fmask)
        send_rows(groups, share, ids, scratch.at[i], i, keep, send)


def back_probs_kernel(
    groups, cw, imgs, step, lat, share, ids, q, kv, lse, grad_keep, *refs
):
    recv, (grad_all, delta, scratch) = refs[: groups - 1], refs[groups - 1 :]
    heads = cw // HD
    mask = diag_mask(heads, cw, BF)
    for i in range(imgs):
        for s in range(groups):
            start = pl.multiple_of(lax.rem(ids[0] + s, groups) * share, share)
            block = grad_keep if s == 0 else recv[s - 1]
            block = lane_roll(block[i * share : (i + 1) * share, :].astype(F32), s, groups, cw)
            scratch[i, pl.ds(start, share), :] = block
        grad_all[i * lat : (i + 1) * lat, :] = scratch[i].astype(BF)
        for j in range(groups):
            keys = kv[i * step : (i + 1) * step, j * 2 * cw : j * 2 * cw + cw]
            values = kv[i * step : (i + 1) * step, j * 2 * cw + cw : (j + 1) * 2 * cw]
            qbd = spread(q[i * lat : (i + 1) * lat, j * cw : (j + 1) * cw], heads, mask)
            gbd = spread(grad_all[i * lat : (i + 1) * lat, j * cw : (j + 1) * cw], heads, mask)
            probs = jnp.exp(dot(keys, qbd, NT) - lse[i, 0:1, j * cw : (j + 1) * cw])
            delta[i, 0:1, j * cw : (j + 1) * cw] = jnp.sum(
                probs * dot(values, gbd, NT), axis=0, keepdims=True
            )


def back_scores_kernel(
    groups, cw, imgs, step, lat, share, ids, q, kv, lse, grad_all, delta, gkv, gq, keep, send, scratch
):
    heads = cw // HD
    mask, fmask = diag_mask(heads, cw, BF), diag_mask(heads, cw, F32)
    for i in range(imgs):
        for j in range(groups):
            keys = kv[i * step : (i + 1) * step, j * 2 * cw : j * 2 * cw + cw]
            values = kv[i * step : (i + 1) * step, j * 2 * cw + cw : (j + 1) * 2 * cw]
            qbd = spread(q[i * lat : (i + 1) * lat, j * cw : (j + 1) * cw], heads, mask)
            gbd = spread(grad_all[i * lat : (i + 1) * lat, j * cw : (j + 1) * cw], heads, mask)
            probs = jnp.exp(dot(keys, qbd, NT) - lse[i, 0:1, j * cw : (j + 1) * cw])
            grad = dot(values, gbd, NT) - delta[i, 0:1, j * cw : (j + 1) * cw]
            grad = (probs * grad).astype(BF)
            gkv[i * step : (i + 1) * step, j * 2 * cw : j * 2 * cw + cw] = dot(grad, qbd).astype(BF)
            gkv[i * step : (i + 1) * step, j * 2 * cw + cw : (j + 1) * 2 * cw] = dot(
                probs.astype(BF), gbd
            ).astype(BF)
            full = dot(grad, keys, TN)
            scratch[i, :, j * cw : (j + 1) * cw] = fold(full, heads, lat, fmask) * (HD**-0.5)
        gq[i * lat : (i + 1) * lat, :] = scratch[i].astype(BF)
        send_rows(groups, share, ids, scratch.at[i], i, keep, send)


def lane_roll(values, s, groups, cw):
    if s == 0:
        return values
    if cw % 128 == 0:
        cut = (groups - s) * cw
        return jnp.concatenate([values[:, cut:], values[:, :cut]], axis=1)
    return pltpu.roll(values, s * cw, 1)


def middle_kernel(groups, cw, ids, keep, *refs):
    recv = refs[: groups - 1]
    latents, w, gain, bias, mixed, middle, normed = refs[groups - 1 :]
    total = keep[...]
    for s in range(1, groups):
        total = total + lane_roll(recv[s - 1][...].astype(F32), s, groups, cw)
    low = total.astype(BF)
    mixed[...] = low
    rows, width = middle.shape
    value = latents[...].astype(F32).reshape(rows, width)
    for j in range(groups):
        value = value + dot(low[:, j * cw : (j + 1) * cw], w[j, :, 3 * cw :], NT)
    middle[...] = value
    xhat, _ = norm_parts(value)
    normed[...] = (xhat * gain[...] + bias[...]).astype(BF)


def gelu_parts(value):
    cdf = 0.5 * (1.0 + lax.erf(value * (0.5**0.5)))
    pdf = jnp.exp(value * value * -0.5) * 0.3989422804014327
    return value * cdf, cdf + value * pdf


def forward_kernel(ids, normed, final, up, down, hidden, up_low, ff, mid, ff_total, mid_total):
    step = pl.program_id(0)

    @pl.when(step == 0)
    def _():
        ff_total[...] = jnp.zeros_like(ff_total)
        mid_total[...] = jnp.zeros_like(mid_total)

    act, slope = gelu_parts(dot(normed[...], up[...]))
    low = act.astype(BF)
    hidden[...] = low
    ff_total[...] += dot(low, down[...], NT)
    low = (dot(final[...], down[...]) * slope).astype(BF)
    up_low[...] = low
    mid_total[...] += dot(low, up[...], NT)

    @pl.when(step == pl.num_programs(0) - 1)
    def _():
        ff[...] = ff_total[...].astype(BF)
        mid[...] = mid_total[...].astype(BF)


def middle_back_kernel(groups, cw, ids, part, *refs):
    recv = refs[: groups - 1]
    middle, final, w, gain, grad_mid, mid_low, grad_mixed, gains = refs[groups - 1 :]
    total = part[...].astype(F32)
    for other in recv:
        total = total + other[...].astype(F32)
    back, gain_grad, bias_grad = norm_back(middle[...], gain[...], total)
    gains[0:1, :] = gain_grad
    gains[1:2, :] = bias_grad
    value = final[...].astype(F32) + back
    grad_mid[...] = value
    low = value.astype(BF)
    mid_low[...] = low
    for j in range(groups):
        grad_mixed[:, j * cw : (j + 1) * cw] = dot(low, w[j, :, 3 * cw :]).astype(BF)


def weight_grad_kernel(terms, rows, ids, *refs):
    left, right = refs[:terms], refs[terms : 2 * terms]
    keep, send, total = refs[2 * terms :]
    value = dot(left[0][...], right[0][...], TN)
    for k in range(1, terms):
        value = value + dot(left[k][...], right[k][...], TN)
    total[...] = value
    for b in range(keep.shape[0]):
        for ref, core in ((keep, ids[3]), (send, 1 - ids[3])):
            start = pl.multiple_of((b * 2 + core) * rows, rows)
            ref[b] = total[pl.ds(start, rows), :].astype(BF)


def weight_grad(ids, left, right, rows, block, name):
    depth, width = left[0].shape[1], right[0].shape[1]
    blocks = depth // rows // 2
    out = struct((blocks, rows, width), BF)
    spec = pl.BlockSpec((blocks, rows, block), lambda i, ids: (0, 0, i))
    return call(
        functools.partial(weight_grad_kernel, len(left), rows),
        (width // block,),
        [whole(a) for a in left]
        + [pl.BlockSpec((a.shape[0], block), lambda i, ids: (0, i)) for a in right],
        [spec, spec],
        [out, out],
        [pltpu.VMEM((depth, block), F32)],
        ids,
        list(left) + list(right),
        2 * sum(a.shape[0] for a in left) * depth * width,
        name,
    )


def source_back_kernel(
    groups, cw, imgs, patch, share, ids, live, gkv, w, media, latents, cot, keep, *refs
):
    recv = refs[: groups - 1]
    grad_mid, m_gain, l_gain, media_grad, latent_grad, gains = refs[groups - 1 :]
    first = pl.program_id(0) * imgs
    step = patch + share
    total = dot(gkv[:, : 2 * cw], w[0, :, cw : 3 * cw], NT)
    for j in range(1, groups):
        total = total + dot(gkv[:, j * 2 * cw : (j + 1) * 2 * cw], w[j, :, cw : 3 * cw], NT)
    query = keep[...]
    for s in range(1, groups):
        query = query + lane_roll(recv[s - 1][...].astype(F32), s, groups, cw)
    query = query.astype(BF)
    lat = dot(query[:, :cw], w[0, :, :cw], NT)
    for j in range(1, groups):
        lat = lat + dot(query[:, j * cw : (j + 1) * cw], w[j, :, :cw], NT)

    @pl.when(pl.program_id(0) == 0)
    def _():
        gains[...] = jnp.zeros_like(gains)

    for i in range(imgs):
        back, gain_grad, bias_grad = norm_back(
            media[i].astype(F32), m_gain[...], total[i * step : i * step + patch]
        )
        media_grad[i] = back
        gains[0:1, :] += gain_grad
        gains[1:2, :] += bias_grad
        rows = slice(i * share, (i + 1) * share)
        back, gain_grad, bias_grad = norm_back(
            latents[i].astype(F32), l_gain[...], total[i * step + patch : (i + 1) * step] + lat[rows]
        )
        gains[2:3, :] += gain_grad
        gains[3:4, :] += bias_grad
        latent_grad[i] = jnp.where(
            live[first + i] > 0, grad_mid[rows, :] + back, cot[i].astype(F32)
        )


def make_local(depth_z, groups):
    dp_size = depth_z * 4

    def from_dp(value, s=0, yf=0, cf=0):
        pairs = []
        for dst in range(dp_size):
            z, y, c = dst // 4, dst // 2 % 2, dst % 2
            pairs.append(((z + s) % depth_z * 4 + (y ^ yf) * 2 + (c ^ cf), dst))
        return lax.ppermute(value, "dp", pairs)

    def from_head(value, s):
        return lax.ppermute(value, "head", [((x + s) % groups, x) for x in range(groups)])

    def to_head(value, s):
        return lax.ppermute(value, "head", [(x, (x + s) % groups) for x in range(groups)])

    def plane(value, sx, yf, back):
        pairs = []
        for dst in range(dp_size):
            for x in range(groups):
                other = (dst ^ (2 * yf)) * groups + (x + sx) % groups
                mine = dst * groups + x
                pairs.append((mine, other) if back else (other, mine))
        return lax.ppermute(value, ("dp", "head"), pairs)

    def local(
        media_tokens,
        latents,
        cotangent,
        image_counts,
        media_gain,
        media_bias,
        latent_gain,
        latent_bias,
        ff_gain,
        ff_bias,
        w_query,
        w_keyval,
        w_attn_out,
        w_up,
        w_down,
    ):
        images, patches, width = media_tokens.shape
        lat = latents.shape[1]
        rows, cw = w_query.shape
        units = w_up.shape[1]
        patch, share = patches // groups, lat // groups
        step = patch + share
        heads_w = cw * groups
        me = lax.axis_index("head").astype(jnp.int32)
        place = lax.axis_index("dp").astype(jnp.int32)
        z, y, c = place // 4, place // 2 % 2, place % 2
        ids = jnp.stack([me, z, y, c])
        live = (jnp.arange(images, dtype=jnp.int32) < jnp.sum(image_counts)).astype(jnp.int32)
        gains = [
            g.reshape(1, width)
            for g in (media_gain, media_bias, latent_gain, latent_bias, ff_gain, ff_bias)
        ]

        attn_shard = jnp.concatenate([w_query, w_keyval[:, 0], w_keyval[:, 1], w_attn_out.T], axis=1)
        ff_shard = jnp.concatenate([w_up, w_down.T], axis=1)
        line = jnp.stack([attn_shard] + [from_dp(attn_shard, s) for s in range(1, depth_z)])
        pieces, entries = [], []
        for sx in range(groups):
            for yf in range(2):
                part = line if sx == yf == 0 else plane(line, sx, yf, False)
                for cf, piece in ((0, part), (1, from_dp(part, cf=1))):
                    for s in range(depth_z):
                        entries.append((len(pieces), s, sx, s, yf, cf))
                    pieces.append(piece)
        w_attn = assemble(entries, pieces, depth_z, ids, rows, groups, 4 * cw, "place_attn")
        pieces, entries = [], []
        for s in range(depth_z):
            part = ff_shard if s == 0 else from_dp(ff_shard, s)
            for yf, row in ((0, part), (1, from_dp(part, yf=1))):
                for cf, piece in ((0, row), (1, from_dp(row, cf=1))):
                    entries.append((len(pieces), None, 0, s, yf, cf))
                    pieces.append(piece)
        w_ff = assemble(entries, pieces, depth_z, ids, rows, 1, 2 * units, "place_ff")[0]

        imgs = 2
        media4 = media_tokens.reshape(images, groups, patch, width)
        lat4 = latents.reshape(images, groups, share, width)
        cot4 = cotangent.reshape(images, groups, share, width)
        src, nlat = call(
            functools.partial(norm_kernel, imgs, lat, share, patch),
            (images // imgs,),
            [
                pl.BlockSpec((imgs, None, patch, width), lambda i, ids: (i, ids[0], 0, 0)),
                pl.BlockSpec((imgs, lat, width), lambda i, ids: (i, 0, 0)),
            ]
            + [whole(gains[0])] * 4,
            [rows_of(imgs * step, width), rows_of(imgs * lat, width)],
            [struct((images * step, width), BF), struct((images * lat, width), BF)],
            [pltpu.VMEM((lat, width), F32)],
            ids,
            [media4, latents] + gains[:4],
            images * step * width * 12,
            "input_norms",
        )
        final4 = jnp.stack(
            [
                lax.dynamic_index_in_dim(cot4, (me + s) % groups, 1, keepdims=False)
                for s in range(groups)
            ]
        ) * live.astype(BF).reshape(1, images, 1, 1)

        imgs = 4
        attn_macs = images * step * lat * heads_w
        q, kv, stats = call(
            functools.partial(project_kernel, groups, cw, imgs, step, lat),
            (images // imgs,),
            [rows_of(imgs * step, width), rows_of(imgs * lat, width), whole(w_attn)],
            [
                rows_of(imgs * lat, heads_w),
                rows_of(imgs * step, 2 * heads_w),
                pl.BlockSpec((imgs, 2, heads_w), lambda i, ids: (i, 0, 0)),
            ],
            [
                struct((images * lat, heads_w), BF),
                struct((images * step, 2 * heads_w), BF),
                struct((images, 2, heads_w), F32),
            ],
            [],
            ids,
            [src, nlat, w_attn],
            2 * images * (step * width * 2 * heads_w + lat * width * heads_w) + 8 * attn_macs,
            "project",
        )
        tops, sums = [stats[:, :1]], [stats[:, 1:]]
        for s in range(1, groups):
            other = jnp.roll(from_head(stats, s), s * cw, axis=2)
            tops.append(other[:, :1])
            sums.append(other[:, 1:])
        top = functools.reduce(jnp.maximum, tops)
        lse = top + jnp.log(sum(t * jnp.exp(m - top) for m, t in zip(tops, sums)))

        part = images // CHUNKS
        count = part // imgs
        own = part * share
        lat_block = part * lat

        def chunk_rows(ch, size):
            return pl.BlockSpec((imgs * size[0], size[1]), lambda i, ids: (i + ch * count, 0))

        def chunk_images(ch):
            return pl.BlockSpec((imgs, 1, heads_w), lambda i, ids: (i + ch * count, 0, 0))

        def attn_specs(ch):
            return [
                chunk_rows(ch, (lat, heads_w)),
                chunk_rows(ch, (step, 2 * heads_w)),
                chunk_images(ch),
            ]

        row_sends = [
            rows_of(imgs * share, heads_w),
            pl.BlockSpec((groups - 1, imgs * share, heads_w), lambda i, ids: (0, i, 0)),
        ]
        row_outs = [struct((own, heads_w), F32), struct((groups - 1, own, heads_w), BF)]
        share_spec = pl.BlockSpec
        mixed, middle, normed, final, hidden, up_low, ff_sum, mid_sum = ([] for _ in range(8))
        for ch in range(CHUNKS):
            keep, send = call(
                functools.partial(mix_kernel, groups, cw, imgs, step, lat, share),
                (count,),
                attn_specs(ch),
                row_sends,
                row_outs,
                [pltpu.VMEM((imgs, lat, heads_w), F32)],
                ids,
                [q, kv, lse],
                8 * attn_macs / CHUNKS,
                f"mix{ch}",
            )
            recv = [to_head(send[s - 1], s) for s in range(groups - 1, 0, -1)]
            lat_spec = share_spec(
                (part, None, share, width), lambda i, ids, ch=ch: (ch, ids[0], 0, 0)
            )
            outs = call(
                functools.partial(middle_kernel, groups, cw),
                (1,),
                [whole(keep)]
                + [whole(r) for r in recv]
                + [lat_spec, whole(w_attn), whole(gains[4]), whole(gains[5])],
                [rows_of(own, heads_w), rows_of(own, width), rows_of(own, width)],
                [struct((own, heads_w), BF), struct((own, width), F32), struct((own, width), BF)],
                [],
                ids,
                [keep] + recv + [lat4, w_attn, gains[4], gains[5]],
                2 * own * heads_w * width,
                f"middle{ch}",
            )
            mixed.append(outs[0])
            middle.append(outs[1])
            normed.append(
                jnp.concatenate([outs[2]] + [from_head(outs[2], s) for s in range(1, groups)])
            )
            final.append(final4[:, ch * part : (ch + 1) * part].reshape(groups * own, width))
        block = min(512, units)
        full = groups * own
        for ch in range(CHUNKS):
            outs = call(
                forward_kernel,
                (units // block,),
                [
                    whole(normed[ch]),
                    whole(final[ch]),
                    pl.BlockSpec((width, block), lambda i, ids: (0, i)),
                    pl.BlockSpec((width, block), lambda i, ids: (0, i + units // block)),
                ],
                [
                    pl.BlockSpec((full, block), lambda i, ids: (0, i)),
                    pl.BlockSpec((full, block), lambda i, ids: (0, i)),
                    pl.BlockSpec((full, width), lambda i, ids: (0, 0)),
                    pl.BlockSpec((full, width), lambda i, ids: (0, 0)),
                ],
                [
                    struct((full, units), BF),
                    struct((full, units), BF),
                    struct((full, width), BF),
                    struct((full, width), BF),
                ],
                [pltpu.VMEM((full, width), F32)] * 2,
                ids,
                [normed[ch], final[ch], w_ff, w_ff],
                8 * full * width * units,
                f"feed_forward{ch}",
            )
            hidden.append(outs[0])
            up_low.append(outs[1])
            for total, terms in ((outs[2], ff_sum), (outs[3], mid_sum)):
                total = total.reshape(groups, own, width)
                terms.append(
                    [total[0]] + [to_head(total[s], s) for s in range(groups - 1, 0, -1)]
                )

        down_parts = weight_grad(ids, final, hidden, rows, block, "grad_down")
        up_parts = weight_grad(ids, normed, up_low, rows, block, "grad_up")

        mid_low, grad_mid, gain_terms, grad_mixed = [], [], [], []
        for ch in range(CHUNKS):
            outs = call(
                functools.partial(middle_back_kernel, groups, cw),
                (1,),
                [whole(t) for t in mid_sum[ch]]
                + [whole(middle[ch]), pl.BlockSpec((own, width), lambda i, ids: (0, 0))]
                + [whole(w_attn), whole(gains[4])],
                [
                    rows_of(own, width),
                    rows_of(own, width),
                    rows_of(own, heads_w),
                    pl.BlockSpec((2, width), lambda i, ids: (0, 0)),
                ],
                [
                    struct((own, width), F32),
                    struct((own, width), BF),
                    struct((own, heads_w), BF),
                    struct((2, width), F32),
                ],
                [],
                ids,
                mid_sum[ch] + [middle[ch], final[ch], w_attn, gains[4]],
                2 * own * heads_w * width,
                f"middle_back{ch}",
            )
            grad_mid.append(outs[0])
            mid_low.append(outs[1])
            grad_mixed.append([outs[2]] + [from_head(outs[2], s) for s in range(1, groups)])
            gain_terms.append(outs[3])
        out_parts = weight_grad(ids, mid_low, mixed, rows, heads_w, "grad_attn_out")

        grad_all, delta = [], []
        for ch in range(CHUNKS):
            outs = call(
                functools.partial(back_probs_kernel, groups, cw, imgs, step, lat, share),
                (count,),
                attn_specs(ch) + [rows_of(imgs * share, heads_w)] * groups,
                [
                    rows_of(imgs * lat, heads_w),
                    pl.BlockSpec((imgs, 1, heads_w), lambda i, ids: (i, 0, 0)),
                ],
                [struct((lat_block, heads_w), BF), struct((part, 1, heads_w), F32)],
                [pltpu.VMEM((imgs, lat, heads_w), F32)],
                ids,
                [q, kv, lse] + grad_mixed[ch],
                8 * attn_macs / CHUNKS,
                f"back_probs{ch}",
            )
            grad_all.append(outs[0])
            total = outs[1]
            for s in range(1, groups):
                total = total + jnp.roll(from_head(outs[1], s), s * cw, axis=2)
            delta.append(total)
        gkv, gq, query_terms = [], [], []
        for ch in range(CHUNKS):
            outs = call(
                functools.partial(back_scores_kernel, groups, cw, imgs, step, lat, share),
                (count,),
                attn_specs(ch)
                + [
                    rows_of(imgs * lat, heads_w),
                    pl.BlockSpec((imgs, 1, heads_w), lambda i, ids: (i, 0, 0)),
                ],
                [rows_of(imgs * step, 2 * heads_w), rows_of(imgs * lat, heads_w)] + row_sends,
                [struct((part * step, 2 * heads_w), BF), struct((lat_block, heads_w), BF)]
                + row_outs,
                [pltpu.VMEM((imgs, lat, heads_w), F32)],
                ids,
                [q, kv, lse, grad_all[ch], delta[ch]],
                20 * attn_macs / CHUNKS,
                f"back_scores{ch}",
            )
            gkv.append(outs[0])
            gq.append(outs[1])
            query_terms.append(
                [outs[2]] + [to_head(outs[3][s - 1], s) for s in range(groups - 1, 0, -1)]
            )
        src_chunks = [src[ch * part * step : (ch + 1) * part * step] for ch in range(CHUNKS)]
        nlat_chunks = [nlat[ch * lat_block : (ch + 1) * lat_block] for ch in range(CHUNKS)]
        kv_parts = weight_grad(ids, src_chunks, gkv, rows, min(512, 2 * heads_w), "grad_keyval")
        q_parts = weight_grad(ids, nlat_chunks, gq, rows, heads_w, "grad_query")

        imgs = min(4, part)
        count = part // imgs
        media_grad, latent_grad = [], []
        for ch in range(CHUNKS):

            def share_rows(size, ch=ch):
                return pl.BlockSpec(
                    (imgs, None, size, width), lambda i, ids, live: (i + ch * count, ids[0], 0, 0)
                )

            def own_rows(block, size):
                return pl.BlockSpec((block, size), lambda i, ids, live: (i, 0))

            def fixed(array):
                zeros = (0,) * array.ndim
                return pl.BlockSpec(array.shape, lambda *_: zeros)

            args = [gkv[ch], w_attn, media4, lat4, cot4] + query_terms[ch]
            args += [grad_mid[ch], gains[0], gains[2]]
            outs = pl.pallas_call(
                functools.partial(source_back_kernel, groups, cw, imgs, patch, share),
                grid_spec=pltpu.PrefetchScalarGridSpec(
                    num_scalar_prefetch=2,
                    grid=(count,),
                    in_specs=[own_rows(imgs * step, 2 * heads_w), fixed(w_attn)]
                    + [share_rows(patch), share_rows(share), share_rows(share)]
                    + [own_rows(imgs * share, heads_w)] * groups
                    + [own_rows(imgs * share, width), fixed(gains[0]), fixed(gains[2])],
                    out_specs=[
                        pl.BlockSpec((imgs, patch, width), lambda i, ids, live: (i, 0, 0)),
                        pl.BlockSpec((imgs, share, width), lambda i, ids, live: (i, 0, 0)),
                        pl.BlockSpec((4, width), lambda i, ids, live: (0, 0)),
                    ],
                ),
                out_shape=[
                    struct((part, patch, width), F32),
                    struct((part, share, width), F32),
                    struct((4, width), F32),
                ],
                compiler_params=pltpu.CompilerParams(
                    vmem_limit_bytes=48 * MIB, dimension_semantics=("arbitrary",)
                ),
                cost_estimate=pl.CostEstimate(
                    flops=2 * part * step * width * 2 * heads_w,
                    bytes_accessed=part * step * width * 8,
                    transcendentals=0,
                ),
                name=f"source_back{ch}",
            )(ids, live[ch * part : (ch + 1) * part], *args)
            media_grad.append(outs[0])
            latent_grad.append(outs[1])
            gain_terms[ch] = jnp.concatenate([outs[2], gain_terms[ch]])

        def pick(block, index):
            return lax.dynamic_index_in_dim(block, index, 0, keepdims=False).astype(F32)

        def scatter_plane(keep, send):
            recv = from_dp(send, cf=1)
            grid = [a.reshape((depth_z, 2) + a.shape[1:]) for a in (keep, recv)]

            def at(yy, zz):
                return sum(pick(pick(a, zz), yy) for a in grid)

            away = jnp.stack([at(1 - y, k) for k in range(depth_z)]).astype(BF)
            near = from_dp(away, yf=1)
            total = at(y, z) + pick(near, z)
            for s in range(1, depth_z):
                block = (at(y, (z + s) % depth_z) + pick(near, (z + s) % depth_z)).astype(BF)
                total = total + from_dp(block, depth_z - s).astype(F32)
            return total

        def scatter_all(keep, send, cols):
            recv = from_dp(send, cf=1)
            grid = [a.reshape((depth_z, 2) + a.shape[1:]) for a in (keep, recv)]

            def at(sx, yy):
                lanes = slice(sx * cols, (sx + 1) * cols)
                return sum(
                    lax.dynamic_index_in_dim(a[..., lanes], yy, 1, keepdims=False).astype(F32)
                    for a in grid
                )

            terms = []
            for sx in range(groups):
                for yf in range(2):
                    if sx or yf:
                        terms.append(plane(at(sx, y ^ yf).astype(BF), sx, yf, True))
            base = at(0, y)

            def sum_at(zz):
                return pick(base, zz) + sum(pick(t, zz) for t in terms)

            total = sum_at(z)
            for s in range(1, depth_z):
                block = sum_at((z + s) % depth_z).astype(BF)
                total = total + from_dp(block, depth_z - s).astype(F32)
            return total

        grad_down = scatter_plane(*down_parts).T
        grad_up = scatter_plane(*up_parts)
        grad_attn = scatter_all(*out_parts, cw).T
        grad_keyval = scatter_all(*kv_parts, 2 * cw).reshape(rows, 2, cw)
        grad_query = scatter_all(*q_parts, cw)

        total = sum(gain_terms)
        total = total + from_dp(total, cf=1)
        around = [total]
        for sx in range(groups):
            for yf in range(2):
                if sx or yf:
                    around.append(plane(total, sx, yf, False))
        total = sum(around)
        norm_grads = total + sum(from_dp(total, s) for s in range(1, depth_z))

        final_lat = jnp.concatenate(
            [
                mid + sum(t.astype(F32) for t in terms)
                for mid, terms in zip(middle, ff_sum)
            ]
        ).reshape(images, share, width)
        lat_own = lax.dynamic_index_in_dim(lat4, me, 1, keepdims=False).astype(F32)
        latents_out = jnp.where(live[:, None, None] > 0, final_lat, lat_own)
        return (
            latents_out,
            jnp.concatenate(media_grad),
            jnp.concatenate(latent_grad),
            grad_query,
            grad_keyval,
            grad_attn,
            grad_up,
            grad_down,
            norm_grads,
        )

    return local


def solution(mesh):
    return jax.shard_map(
        make_local(mesh.shape["dp"] // 4, mesh.shape["head"]),
        mesh=mesh,
        in_specs=(
            P("dp", None, None),
            P("dp", None, None),
            P("dp", None, None),
            P("dp"),
            P(),
            P(),
            P(),
            P(),
            P(),
            P(),
            P("dp", "head"),
            P("dp", None, "head"),
            P("head", "dp"),
            P("dp", "head"),
            P("head", "dp"),
        ),
        out_specs=(
            P("dp", "head", None),
            P("dp", "head", None),
            P("dp", "head", None),
            P("dp", "head"),
            P("dp", None, "head"),
            P("head", "dp"),
            P("dp", "head"),
            P("head", "dp"),
            P(),
        ),
        check_vma=False,
    )
```

time: 997 us -> 451 us (0.45)
  waiting for transfers between devices: 602 us -> 108 us
  Pallas kernels: 0 us -> 160 us
  matrix products: 124 us -> 0 us
  other arithmetic: 125 us -> 31.6 us
  starting transfers between devices: 1.53 us -> 92.9 us
  blocking collectives: 85.8 us -> 0 us
  local copies, waits for them, and re-layouts: 37 us -> 52.2 us
  between operations: 15 us -> 2.27 us
    reduce_scatter x7 -> x0, waiting for transfers between devices: 367 us -> none  [the longest x1 90.6 us: local(): lax.psum_scatter(media_part.astype(jnp.bfloat16), 'head', scatter_dimensi...]
    psum x2 -> x0, waiting for transfers between devices: 166 us -> none  [the longest x1 107 us: local(): lax.psum(mid_part.astype(jnp.bfloat16), 'head').astype(jnp.float32)]
    pallas_call x0 -> x23, Pallas kernels: none -> 160 us  [the longest x21 134 us: call(): pl.pallas_call(kernel, grid_spec=pltpu.PrefetchScalarGridSpec(num_scalar_...]
    dot_general x22 -> x0, matrix products: 124 us -> none  [the longest x1 12.8 us: local(): jnp.einsum('ild,fd->ilf', final_low, down_all, preferred_element_type=jnp...]
    ppermute x0 -> x78, waiting for transfers between devices: none -> 108 us  [the longest x48 45.5 us: from_dp(): return lax.ppermute(value, 'dp', pairs)]
    ppermute x0 -> x78, starting transfers between devices: none -> 92.9 us  [the longest x48 63.3 us: from_dp(): return lax.ppermute(value, 'dp', pairs)]
    all_gather x3 -> x0, waiting for transfers between devices: 68.3 us -> none  [the longest x1 49.7 us: local(): lax.all_gather(w_up, 'dp', axis=0, tiled=True)]
    reduce_sum x15 -> x0, other arithmetic: 49.6 us -> none  [the longest x4 16.8 us: layer_norm(): return centre * lax.rsqrt(spread + 1e-05) * gain + bias]
  transfers between devices with their start and end apart: 12 -> 78, of which waited for: 10 -> 25; matrix products, arithmetic and copies ran while one was open for 15% -> 12% of each run, Pallas kernels for 0% -> 33%
where the time goes in v1:
time: 451 us; the launch traced here: 447 us
  Pallas kernels  160 us (35%)
  waiting for transfers between devices  108 us (24%)
  starting transfers between devices  92.9 us (21%)
  local copies, waits for them, and re-layouts  52.2 us (12%)
  other arithmetic  31.6 us (7%)
    pallas_call x21, Pallas kernels, call(): pl.pallas_call(kernel, grid_spec=pltpu.PrefetchScalarGridSpec(num_scalar_...  134 us
    ppermute x48, starting transfers between devices, from_dp(): return lax.ppermute(value, 'dp', pairs)  63.3 us
    ppermute x48, waiting for transfers between devices, from_dp(): return lax.ppermute(value, 'dp', pairs)  45.5 us
    ppermute x15, waiting for transfers between devices, plane(): return lax.ppermute(value, ('dp', 'head'), pairs)  42.6 us
    unnamed x156, local copies, waits for them, and re-layouts  26.9 us
    pallas_call x2, Pallas kernels, local(): pl.pallas_call(functools.partial(source_back_kernel, groups, cw, imgs, pa...  25.9 us
    ppermute x8, waiting for transfers between devices, to_head(): lax.ppermute(value, 'head', [(x, (x + s) % groups) for x in range(groups)])  19.9 us
    ppermute x15, starting transfers between devices, plane(): return lax.ppermute(value, ('dp', 'head'), pairs)  13.8 us
  transfers between devices with their start and end apart: 78, of which 25 were waited for; matrix products, arithmetic and copies ran while one was open for 12% of the time, Pallas kernels for 33%

profile of v1, /device:TPU:0, one launch (start us, length us, event | category | flops | bytes accessed | tf_op | source)
XLA Modules:
  0.0 447.2 jit_solution(12457166174984135499)
XLA Ops:
  2.7 4.1 collective-permute-start.1
  8.8 5.9 %collective-permute-done.1 = bf16[64,1024]{1,0:T(8,128)(2,1)S(1)} collective-permute-done((bf16[64,1024]{1,0:T(8,128)(2,1)S(1)}, bf16[64,1024]{1,0:T(8,128)(2,1)S(1)}, u32[]{:S(2)}, u32[]{:S(2)}) %collective-permute-start.1) | collective-permute-done | bytes 131104 | tf_op jit(solution)/shard_map/ppermute | solution.py:390
  14.7 2.4 collective-permute-done.2
  17.2 2.5 collective-permute-start.8
  21.6 2.4 collective-permute-start.24
  24.0 9.3 %input_norms.1 = (bf16[2560,1024]{1,0:T(8,128)(2,1)}, bf16[1024,1024]{1,0:T(8,128)(2,1)S(1)}) custom-call(s32[4]{0:T(128)S(1)} %pad_add_fusion.ids.ids_ref, bf16[16,2,128,1024]{3,2,1,0:T(8,128)(2,1)} %bitcast.314, bf16[16,64,1024]{2,1,0:T(8,128)(2,1)S(1)} %copy-done.1, f32[1,1024]{1,0:T(1,128)S(1)} %bitcast.301, f32[1,1024]{1,0:T(1,128)S(1)} %bitcast.309, ...), custom_call_target="tpu_custom_call" | custom-call | flops 31457280 | bytes 17842176 | tf_op jit(solution)/shard_map/input_norms/pallas_call | solution.py:35
  35.2 7.1 %collective-permute-done.6.refs_4_ = bf16[4,64,1024]{2,1,0:T(8,128)(2,1)} collective-permute-done((bf16[4,64,1024]{2,1,0:T(8,128)(2,1)S(1)}, bf16[4,64,1024]{2,1,0:T(8,128)(2,1)}, u32[]{:S(2)}, u32[]{:S(2)}) %collective-permute-start.6) | collective-permute-done | bytes 524320 | tf_op jit(solution)/shard_map/ppermute | solution.py:405
  42.8 5.4 %fusion.53 = (bf16[1280,1024]{1,0:T(8,128)(2,1)}, bf16[1280,1024]{1,0:T(8,128)(2,1)}) fusion(bf16[2560,1024]{1,0:T(8,128)(2,1)} %get-tuple-element.68.src), kind=kLoop, calls=%fused_computation.128 | loop fusion | bytes 10485760 | tf_op jit(solution)/shard_map/slice | solution.py:700
  48.2 3.0 fusion.58
  51.3 5.4 %collective-permute-start.20 = (bf16[64,4096]{1,0:T(8,128)(2,1)}, bf16[64,4096]{1,0:T(8,128)(2,1)}, u32[]{:S(2)}, u32[]{:S(2)}) collective-permute-start(bf16[64,4096]{1,0:T(8,128)(2,1)} %pad_maximum_fusion.6.refs_0_), channel_id=1, source_target_pairs={{16,0},{18,2},{20,4},{22,6},{24,8},{26,10},{28,12},{30,14},{0,16},... | collective-permute-start | bytes 1572872 | tf_op jit(solution)/shard_map/ppermute | solution.py:390
  58.5 3.6 place_attn.1.w.refs_2_.refs_3_
  62.1 2.0 copy-done
  64.1 12.9 %project.1 = (bf16[1024,512]{1,0:T(8,128)(2,1)S(1)}, bf16[2560,1024]{1,0:T(8,128)(2,1)}, f32[16,2,512]{2,1,0:T(2,128)S(1)}) custom-call(s32[4]{0:T(128)S(1)} %pad_add_fusion.ids.ids_ref, bf16[2560,1024]{1,0:T(8,128)(2,1)} %get-tuple-element.68.src, bf16[1024,1024]{1,0:T(8,128)(2,1)S(1)} %copy-done.14, bf16[2,1024,1024]{2,1,0:T(8,128)(2,1)} %copy-done), custom_call_target="tpu_custom_call" | custom-call | flops 7113539584 | bytes 17891328 | tf_op jit(solution)/shard_map/project/pallas_call | solution.py:35
  83.0 4.5 %mix1.1 = (f32[256,512]{1,0:T(8,128)S(1)}, bf16[1,256,512]{2,1,0:T(8,128)(2,1)S(1)}) custom-call(s32[4]{0:T(128)S(1)} %pad_add_fusion.ids.ids_ref, bf16[1024,512]{1,0:T(8,128)(2,1)S(1)} %get-tuple-element.70.q, bf16[2560,1024]{1,0:T(8,128)(2,1)} %get-tuple-element.71.kv, f32[16,1,512]{2,1,0:T(1,128)S(1)} %log_add_fusion.lse), custom_call_target="tpu_custom_call" | custom-call | flops 335544320 | bytes 7110656 | tf_op jit(solution)/shard_map/mix1/pallas_call | solution.py:35
  89.7 6.2 %collective-permute-done.26.refs_14_ = bf16[64,4096]{1,0:T(8,128)(2,1)} collective-permute-done((bf16[64,4096]{1,0:T(8,128)(2,1)}, bf16[64,4096]{1,0:T(8,128)(2,1)}, u32[]{:S(2)}, u32[]{:S(2)}) %collective-permute-start.26) | collective-permute-done | bytes 524320 | tf_op jit(solution)/shard_map/ppermute | solution.py:390
  98.2 4.4 mix0.1
  102.7 1.9 collective-permute-done.29.refs_0_
  107.6 4.3 middle1.1
  115.0 2.9 collective-permute-done.18.refs_6_
  121.6 3.5 middle0.1
  128.8 3.5 place_ff.1
  132.3 3.4 copy-done.2
  139.0 13.5 %feed_forward1.1 = (bf16[512,2048]{1,0:T(8,128)(2,1)}, bf16[512,2048]{1,0:T(8,128)(2,1)}, bf16[512,1024]{1,0:T(8,128)(2,1)S(1)}, bf16[512,1024]{1,0:T(8,128)(2,1)S(1)}) custom-call(s32[4]{0:T(128)S(1)} %pad_add_fusion.ids.ids_ref, bf16[512,1024]{1,0:T(8,128)(2,1)S(1)} %copy-done.37, bf16[512,1024]{1,0:T(8,128)(2,1)S(1)} %bitcast.288, ...), custom_call_target="tpu_custom_call" | custom-call | flops 8589934592 | bytes 25165824 | tf_op jit(solution)/shard_map/feed_forward1/pallas_call | solution.py:35
  154.4 13.7 %feed_forward0.1 = (bf16[512,2048]{1,0:T(8,128)(2,1)}, bf16[512,2048]{1,0:T(8,128)(2,1)}, bf16[512,1024]{1,0:T(8,128)(2,1)S(1)}, bf16[512,1024]{1,0:T(8,128)(2,1)S(1)}) custom-call(s32[4]{0:T(128)S(1)} %pad_add_fusion.ids.ids_ref, bf16[512,1024]{1,0:T(8,128)(2,1)S(1)} %constant_dynamic-update-slice_fusion.normed.refs_0_, bf16[512,1024]{1,0:T(8,128)(2,1)S(1)} %bitcast.291, ...), custom_call_target="tpu_custom_call" | custom-call | flops 8589934592 | bytes 25165824 | tf_op jit(solution)/shard_map/feed_forward0/pallas_call | solution.py:35
  174.1 8.4 %grad_down.1 = (bf16[8,64,2048]{2,1,0:T(8,128)(2,1)S(1)}, bf16[8,64,2048]{2,1,0:T(8,128)(2,1)}) custom-call(s32[4]{0:T(128)S(1)} %pad_add_fusion.ids.ids_ref, bf16[512,1024]{1,0:T(8,128)(2,1)S(1)} %bitcast.292, bf16[512,1024]{1,0:T(8,128)(2,1)S(1)} %bitcast.289, bf16[512,2048]{1,0:T(8,128)(2,1)} %get-tuple-element.119.refs_2_, ...), custom_call_target="tpu_custom_call" | custom-call | flops 4294967296 | bytes 10485760 | tf_op jit(solution)/shard_map/grad_down/pallas_call | solution.py:35
  185.6 8.5 %grad_up.1 = (bf16[8,64,2048]{2,1,0:T(8,128)(2,1)S(1)}, bf16[8,64,2048]{2,1,0:T(8,128)(2,1)}) custom-call(s32[4]{0:T(128)S(1)} %pad_add_fusion.ids.ids_ref, bf16[512,1024]{1,0:T(8,128)(2,1)S(1)} %copy-done.35, bf16[512,1024]{1,0:T(8,128)(2,1)S(1)} %copy-done.38, bf16[512,2048]{1,0:T(8,128)(2,1)} %get-tuple-element.115.refs_2_, ...), custom_call_target="tpu_custom_call" | custom-call | flops 4294967296 | bytes 10485760 | tf_op jit(solution)/shard_map/grad_up/pallas_call | solution.py:35
  196.1 11.3 %collective-permute-done.32.refs_0_ = bf16[256,1024]{1,0:T(8,128)(2,1)S(1)} collective-permute-done((bf16[256,1024]{1,0:T(8,128)(2,1)}, bf16[256,1024]{1,0:T(8,128)(2,1)S(1)}, u32[]{:S(2)}, u32[]{:S(2)}) %collective-permute-start.32) | collective-permute-done | bytes 524320 | tf_op jit(solution)/shard_map/ppermute | solution.py:396
  207.4 4.0 middle_back0.1
  212.0 6.7 %collective-permute-done.36.refs_0_ = bf16[256,1024]{1,0:T(8,128)(2,1)S(1)} collective-permute-done((bf16[256,1024]{1,0:T(8,128)(2,1)S(1)}, bf16[256,1024]{1,0:T(8,128)(2,1)S(1)}, u32[]{:S(2)}, u32[]{:S(2)}) %collective-permute-start.36) | collective-permute-done | bytes 524320 | tf_op jit(solution)/shard_map/ppermute | solution.py:396
  218.6 4.0 middle_back1.1
  224.3 2.2 grad_attn_out.1
  231.8 3.5 back_probs1.1
  236.9 3.5 back_probs0.1
  241.1 8.2 %back_scores1.1 = (bf16[1280,1024]{1,0:T(8,128)(2,1)S(1)}, bf16[512,512]{1,0:T(8,128)(2,1)S(1)}, f32[256,512]{1,0:T(8,128)S(1)}, bf16[1,256,512]{2,1,0:T(8,128)(2,1)}) custom-call(s32[4]{0:T(128)S(1)} %pad_add_fusion.ids.ids_ref, bf16[1024,512]{1,0:T(8,128)(2,1)S(1)} %get-tuple-element.70.q, bf16[2560,1024]{1,0:T(8,128)(2,1)} %get-tuple-element.71.kv, ...), custom_call_target="tpu_custom_call" | custom-call | flops 838860800 | bytes 10797056 | tf_op jit(solution)/shard_map/back_scores1/pallas_call | solution.py:35
  253.2 7.5 %back_scores0.1 = (bf16[1280,1024]{1,0:T(8,128)(2,1)S(1)}, bf16[512,512]{1,0:T(8,128)(2,1)S(1)}, f32[256,512]{1,0:T(8,128)S(1)}, bf16[1,256,512]{2,1,0:T(8,128)(2,1)S(1)}) custom-call(s32[4]{0:T(128)S(1)} %pad_add_fusion.ids.ids_ref, bf16[1024,512]{1,0:T(8,128)(2,1)S(1)} %get-tuple-element.70.q, bf16[2560,1024]{1,0:T(8,128)(2,1)} %get-tuple-element.71.kv, ...), custom_call_target="tpu_custom_call" | custom-call | flops 838860800 | bytes 10797056 | tf_op jit(solution)/shard_map/back_scores0/pallas_call | solution.py:35
  263.5 1.9 grad_query.1
  265.5 9.3 %grad_keyval.1 = (bf16[8,64,1024]{2,1,0:T(8,128)(2,1)S(1)}, bf16[8,64,1024]{2,1,0:T(8,128)(2,1)S(1)}) custom-call(s32[4]{0:T(128)S(1)} %pad_add_fusion.ids.ids_ref, bf16[1280,1024]{1,0:T(8,128)(2,1)S(1)} %copy-done.10, bf16[1280,1024]{1,0:T(8,128)(2,1)} %get-tuple-element.133.refs_1_, bf16[1280,1024]{1,0:T(8,128)(2,1)} %copy-done.12, ...), custom_call_target="tpu_custom_call" | custom-call | flops 5368709120 | bytes 12582912 | tf_op jit(solution)/shard_map/grad_keyval/pallas_call | solution.py:35
  278.5 12.6 %source_back0.1 = (f32[8,128,1024]{2,1,0:T(8,128)}, f32[8,32,1024]{2,1,0:T(8,128)S(1)}, f32[4,1024]{1,0:T(4,128)S(1)}) custom-call(s32[4]{0:T(128)S(1)} %pad_add_fusion.ids.ids_ref, s32[8]{0:T(128)S(1)} %get-tuple-element.202.live, bf16[1280,1024]{1,0:T(8,128)(2,1)} %copy-done.12, bf16[2,1024,1024]{2,1,0:T(8,128)(2,1)} %copy-done, ...), custom_call_target="tpu_custom_call" | custom-call | flops 2684354560 | bytes 10485760 | tf_op jit(solution)/shard_map/source_back0/pallas_call | solution.py:724
  291.1 13.3 %source_back1.1 = (f32[8,128,1024]{2,1,0:T(8,128)}, f32[8,32,1024]{2,1,0:T(8,128)S(1)}, f32[4,1024]{1,0:T(4,128)S(1)}) custom-call(s32[4]{0:T(128)S(1)} %pad_add_fusion.ids.ids_ref, s32[8]{0:T(128)S(1)} %get-tuple-element.203.live, bf16[1280,1024]{1,0:T(8,128)(2,1)} %copy-done.11, bf16[2,1024,1024]{2,1,0:T(8,128)(2,1)} %copy-done, ...), custom_call_target="tpu_custom_call" | custom-call | flops 2684354560 | bytes 10485760 | tf_op jit(solution)/shard_map/source_back1/pallas_call | solution.py:724
  305.0 7.2 %pad_maximum_fusion = f32[16,128,1024]{2,1,0:T(8,128)} fusion(f32[8,128,1024]{2,1,0:T(8,128)} %get-tuple-element.100, f32[8,128,1024]{2,1,0:T(8,128)S(1)} %copy-done.57), kind=kLoop, calls=%fused_computation | loop fusion | flops 2097152 | bytes 16777216 | tf_op jit(solution)/shard_map/concatenate | solution.py:829
  312.2 2.1 collective-permute-start.74
  319.0 9.0 %collective-permute-start.77 = (f32[6,1024]{1,0:T(8,128)S(1)}, f32[6,1024]{1,0:T(8,128)S(1)}, u32[]{:S(2)}, u32[]{:S(2)}) collective-permute-start(f32[6,1024]{1,0:T(8,128)S(1)} %add_add_fusion.3), channel_id=1, source_target_pairs={{24,0},{26,2},{28,4},{30,6},{0,8},{2,10},{4,12},{6,14},{8,16},{10,... | collective-permute-start | bytes 73736 | tf_op jit(solution)/shard_map/ppermute | solution.py:390
  327.9 3.4 collective-permute-start.76
  336.3 2.4 collective-permute-done.55
  340.0 3.0 collective-permute-done.57
  346.7 2.3 collective-permute-done.43
  348.9 2.2 collective-permute-start.60
  355.9 2.5 collective-permute-start.67
  359.7 2.5 collective-permute-start.46
  369.2 2.4 collective-permute-done.50
  371.6 1.9 collective-permute-done.49
  373.5 20.2 %collective-permute-done.48 = bf16[4,64,512]{2,1,0:T(8,128)(2,1)S(1)} collective-permute-done((bf16[4,64,512]{2,1,0:T(8,128)(2,1)S(1)}, bf16[4,64,512]{2,1,0:T(8,128)(2,1)S(1)}, u32[]{:S(2)}, u32[]{:S(2)}) %collective-permute-start.48) | collective-permute-done | bytes 262176 | tf_op jit(solution)/shard_map/ppermute | solution.py:405
  393.8 2.0 collective-permute-start.51
  395.8 1.9 collective-permute-start.53
  397.7 2.7 fusion.17
  400.4 2.0 collective-permute-start.68
  402.4 1.8 collective-permute-start.70
  406.2 6.0 %collective-permute-done.62 = bf16[4,64,2048]{2,1,0:T(8,128)(2,1)} collective-permute-done((bf16[4,64,2048]{2,1,0:T(8,128)(2,1)S(1)}, bf16[4,64,2048]{2,1,0:T(8,128)(2,1)}, u32[]{:S(2)}, u32[]{:S(2)}) %collective-permute-start.62) | collective-permute-done | bytes 1048608 | tf_op jit(solution)/shard_map/ppermute | solution.py:390
  413.8 2.6 collective-permute-start.63
  417.7 5.7 %collective-permute-start.64 = (bf16[64,2048]{1,0:T(8,128)(2,1)S(1)}, bf16[64,2048]{1,0:T(8,128)(2,1)S(1)}, u32[]{:S(2)}, u32[]{:S(2)}) collective-permute-start(bf16[64,2048]{1,0:T(8,128)(2,1)S(1)} %get-tuple-element.132), channel_id=1, source_target_pairs={{16,0},{18,2},{20,4},{22,6},{24,8},{26,10},{28,12},{30,14},{0,16},... | collective-permute-start | bytes 786440 | tf_op jit(solution)/shard_map/ppermute | solution.py:390
  423.5 13.0 %collective-permute-done.69 = bf16[64,2048]{1,0:T(8,128)(2,1)} collective-permute-done((bf16[64,2048]{1,0:T(8,128)(2,1)}, bf16[64,2048]{1,0:T(8,128)(2,1)}, u32[]{:S(2)}, u32[]{:S(2)}) %collective-permute-start.69) | collective-permute-done | bytes 262176 | tf_op jit(solution)/shard_map/ppermute | solution.py:390
  436.5 2.3 fusion.6
  438.8 5.9 %collective-permute-done.64 = bf16[64,2048]{1,0:T(8,128)(2,1)S(1)} collective-permute-done((bf16[64,2048]{1,0:T(8,128)(2,1)S(1)}, bf16[64,2048]{1,0:T(8,128)(2,1)S(1)}, u32[]{:S(2)}, u32[]{:S(2)}) %collective-permute-start.64) | collective-permute-done | bytes 262176 | tf_op jit(solution)/shard_map/ppermute | solution.py:390
  444.7 2.1 fusion.11
  (347 shorter events, 103.3 us)
Async XLA Ops:
  2.7 12.1 %collective-permute-start.1 = (bf16[64,1024]{1,0:T(8,128)(2,1)S(1)}, bf16[64,1024]{1,0:T(8,128)(2,1)S(1)}, u32[]{:S(2)}, u32[]{:S(2)}) collective-permute-start(bf16[64,1024]{1,0:T(8,128)(2,1)S(1)} %get-tuple-element.193), channel_id=1, source_target_pairs={{16,0},{18,2},{20,4},{22,6},{24,8},{26,10},{28,12},{30,14},{0,16},... | collective-permute-start | bytes 393224 | tf_op jit(solution)/shard_map/ppermute | solution.py:390
  6.8 8.0 %collective-permute-start = (bf16[64,1024]{1,0:T(8,128)(2,1)S(1)}, bf16[64,1024]{1,0:T(8,128)(2,1)S(1)}, u32[]{:S(2)}, u32[]{:S(2)}) collective-permute-start(bf16[64,1024]{1,0:T(8,128)(2,1)S(1)} %get-tuple-element.193), channel_id=1, source_target_pairs={{8,0},{10,2},{12,4},{14,6},{16,8},{18,10},{20,12},{22,14},{24,16},... | collective-permute-start | bytes 393224 | tf_op jit(solution)/shard_map/ppermute | solution.py:390
  8.1 9.0 %collective-permute-start.2 = (bf16[64,1024]{1,0:T(8,128)(2,1)S(1)}, bf16[64,1024]{1,0:T(8,128)(2,1)S(1)}, u32[]{:S(2)}, u32[]{:S(2)}) collective-permute-start(bf16[64,1024]{1,0:T(8,128)(2,1)S(1)} %get-tuple-element.193), channel_id=1, source_target_pairs={{24,0},{26,2},{28,4},{30,6},{0,8},{2,10},{4,12},{6,14},{8,16},{10,... | collective-permute-start | bytes 393224 | tf_op jit(solution)/shard_map/ppermute | solution.py:390
  17.2 17.5 %collective-permute-start.8 = (bf16[4,64,1024]{2,1,0:T(8,128)(2,1)S(1)}, bf16[4,64,1024]{2,1,0:T(8,128)(2,1)S(1)}, u32[]{:S(2)}, u32[]{:S(2)}) collective-permute-start(bf16[4,64,1024]{2,1,0:T(8,128)(2,1)S(1)} %pad_maximum_fusion.5.refs_0_), channel_id=1, source_target_pairs={{5,0},{4,1},{7,2},{6,3},{1,4},{0,5},{3,6},{2,7},{13,8},{12,9},{15,... | collective-permute-start | bytes 1572872 | tf_op jit(solution)/shard_map/ppermute | solution.py:405
  19.7 22.6 %collective-permute-start.6 = (bf16[4,64,1024]{2,1,0:T(8,128)(2,1)S(1)}, bf16[4,64,1024]{2,1,0:T(8,128)(2,1)}, u32[]{:S(2)}, u32[]{:S(2)}) collective-permute-start(bf16[4,64,1024]{2,1,0:T(8,128)(2,1)S(1)} %pad_maximum_fusion.5.refs_0_), channel_id=1, source_target_pairs={{1,0},{0,1},{3,2},{2,3},{5,4},{4,5},{7,6},{6,7},{9,8},{8,9},{11,10... | collective-permute-start | bytes 1572872 | tf_op jit(solution)/shard_map/ppermute | solution.py:405
  20.2 22.1 %collective-permute-start.4 = (bf16[4,64,1024]{2,1,0:T(8,128)(2,1)S(1)}, bf16[4,64,1024]{2,1,0:T(8,128)(2,1)}, u32[]{:S(2)}, u32[]{:S(2)}) collective-permute-start(bf16[4,64,1024]{2,1,0:T(8,128)(2,1)S(1)} %pad_maximum_fusion.5.refs_0_), channel_id=1, source_target_pairs={{4,0},{5,1},{6,2},{7,3},{0,4},{1,5},{2,6},{3,7},{12,8},{13,9},{14,... | collective-permute-start | bytes 1572872 | tf_op jit(solution)/shard_map/ppermute | solution.py:405
  21.6 59.2 %collective-permute-start.24 = (bf16[64,4096]{1,0:T(8,128)(2,1)}, bf16[64,4096]{1,0:T(8,128)(2,1)}, u32[]{:S(2)}, u32[]{:S(2)}) collective-permute-start(bf16[64,4096]{1,0:T(8,128)(2,1)} %pad_maximum_fusion.6.refs_0_), channel_id=1, source_target_pairs={{24,0},{26,2},{28,4},{30,6},{0,8},{2,10},{4,12},{6,14},{8,16},{10,... | collective-permute-start | bytes 1572872 | tf_op jit(solution)/shard_map/ppermute | solution.py:390
  34.7 16.6 %collective-permute-start.3 = (bf16[4,64,1024]{2,1,0:T(8,128)(2,1)S(1)}, bf16[4,64,1024]{2,1,0:T(8,128)(2,1)}, u32[]{:S(2)}, u32[]{:S(2)}) collective-permute-start(bf16[4,64,1024]{2,1,0:T(8,128)(2,1)S(1)} %pad_maximum_fusion.5.refs_0_), channel_id=1, source_target_pairs={{2,0},{0,2},{6,4},{4,6},{10,8},{8,10},{14,12},{12,14},{18,16},{16,... | collective-permute-start | bytes 1572872 | tf_op jit(solution)/shard_map/ppermute | solution.py:390
  34.7 21.9 %collective-permute-start.9 = (bf16[4,64,1024]{2,1,0:T(8,128)(2,1)S(1)}, bf16[4,64,1024]{2,1,0:T(8,128)(2,1)}, u32[]{:S(2)}, u32[]{:S(2)}) collective-permute-start(bf16[4,64,1024]{2,1,0:T(8,128)(2,1)S(1)} %collective-permute-done.8.refs_6_), channel_id=1, source_target_pairs={{2,0},{0,2},{6,4},{4,6},{10,8},{8,10},{14,12},{12,14},{18,16},{16,... | collective-permute-start | bytes 1572872 | tf_op jit(solution)/shard_map/ppermute | solution.py:390
  42.3 15.2 %collective-permute-start.7 = (bf16[4,64,1024]{2,1,0:T(8,128)(2,1)}, bf16[4,64,1024]{2,1,0:T(8,128)(2,1)}, u32[]{:S(2)}, u32[]{:S(2)}) collective-permute-start(bf16[4,64,1024]{2,1,0:T(8,128)(2,1)} %collective-permute-done.6.refs_4_), channel_id=1, source_target_pairs={{2,0},{0,2},{6,4},{4,6},{10,8},{8,10},{14,12},{12,14},{18,16},{16,... | collective-permute-start | bytes 1572872 | tf_op jit(solution)/shard_map/ppermute | solution.py:390
  42.3 16.1 %collective-permute-start.5 = (bf16[4,64,1024]{2,1,0:T(8,128)(2,1)}, bf16[4,64,1024]{2,1,0:T(8,128)(2,1)}, u32[]{:S(2)}, u32[]{:S(2)}) collective-permute-start(bf16[4,64,1024]{2,1,0:T(8,128)(2,1)} %collective-permute-done.4.refs_2_), channel_id=1, source_target_pairs={{2,0},{0,2},{6,4},{4,6},{10,8},{8,10},{14,12},{12,14},{18,16},{16,... | collective-permute-start | bytes 1572872 | tf_op jit(solution)/shard_map/ppermute | solution.py:390
  51.3 29.5 %collective-permute-start.20 = (bf16[64,4096]{1,0:T(8,128)(2,1)}, bf16[64,4096]{1,0:T(8,128)(2,1)}, u32[]{:S(2)}, u32[]{:S(2)}) collective-permute-start(bf16[64,4096]{1,0:T(8,128)(2,1)} %pad_maximum_fusion.6.refs_0_), channel_id=1, source_target_pairs={{16,0},{18,2},{20,4},{22,6},{24,8},{26,10},{28,12},{30,14},{0,16},... | collective-permute-start | bytes 1572872 | tf_op jit(solution)/shard_map/ppermute | solution.py:390
  56.7 30.8 %collective-permute-start.16 = (bf16[64,4096]{1,0:T(8,128)(2,1)}, bf16[64,4096]{1,0:T(8,128)(2,1)}, u32[]{:S(2)}, u32[]{:S(2)}) collective-permute-start(bf16[64,4096]{1,0:T(8,128)(2,1)} %pad_maximum_fusion.6.refs_0_), channel_id=1, source_target_pairs={{8,0},{10,2},{12,4},{14,6},{16,8},{18,10},{20,12},{22,14},{24,16},... | collective-permute-start | bytes 1572872 | tf_op jit(solution)/shard_map/ppermute | solution.py:390
  57.5 30.9 %collective-permute-start.14 = (bf16[64,4096]{1,0:T(8,128)(2,1)}, bf16[64,4096]{1,0:T(8,128)(2,1)}, u32[]{:S(2)}, u32[]{:S(2)}) collective-permute-start(bf16[64,4096]{1,0:T(8,128)(2,1)} %pad_maximum_fusion.6.refs_0_), channel_id=1, source_target_pairs={{4,0},{6,2},{0,4},{2,6},{12,8},{14,10},{8,12},{10,14},{20,16},{22,... | collective-permute-start | bytes 1572872 | tf_op jit(solution)/shard_map/ppermute | solution.py:390
  80.7 7.8 %collective-permute-start.13 = (bf16[64,4096]{1,0:T(8,128)(2,1)}, bf16[64,4096]{1,0:T(8,128)(2,1)S(1)}, u32[]{:S(2)}, u32[]{:S(2)}) collective-permute-start(bf16[64,4096]{1,0:T(8,128)(2,1)} %pad_maximum_fusion.6.refs_0_), channel_id=1, source_target_pairs={{2,0},{0,2},{6,4},{4,6},{10,8},{8,10},{14,12},{12,14},{18,16},{16,... | collective-permute-start | bytes 1572872 | tf_op jit(solution)/shard_map/ppermute | solution.py:390
  80.7 15.1 %collective-permute-start.26 = (bf16[64,4096]{1,0:T(8,128)(2,1)}, bf16[64,4096]{1,0:T(8,128)(2,1)}, u32[]{:S(2)}, u32[]{:S(2)}) collective-permute-start(bf16[64,4096]{1,0:T(8,128)(2,1)} %collective-permute-done.24.refs_12_), channel_id=1, source_target_pairs={{4,0},{6,2},{0,4},{2,6},{12,8},{14,10},{8,12},{10,14},{20,16},{22,... | collective-permute-start | bytes 1572872 | tf_op jit(solution)/shard_map/ppermute | solution.py:390
  81.9 13.9 %collective-permute-start.25 = (bf16[64,4096]{1,0:T(8,128)(2,1)}, bf16[64,4096]{1,0:T(8,128)(2,1)S(1)}, u32[]{:S(2)}, u32[]{:S(2)}) collective-permute-start(bf16[64,4096]{1,0:T(8,128)(2,1)} %collective-permute-done.24.refs_12_), channel_id=1, source_target_pairs={{2,0},{0,2},{6,4},{4,6},{10,8},{8,10},{14,12},{12,14},{18,16},{16,... | collective-permute-start | bytes 1572872 | tf_op jit(solution)/shard_map/ppermute | solution.py:390
  87.5 26.1 %collective-permute-start.22 = (bf16[64,4096]{1,0:T(8,128)(2,1)}, bf16[64,4096]{1,0:T(8,128)(2,1)}, u32[]{:S(2)}, u32[]{:S(2)}) collective-permute-start(bf16[64,4096]{1,0:T(8,128)(2,1)} %collective-permute-done.20.refs_8_), channel_id=1, source_target_pairs={{4,0},{6,2},{0,4},{2,6},{12,8},{14,10},{8,12},{10,14},{20,16},{22,... | collective-permute-start | bytes 1572872 | tf_op jit(solution)/shard_map/ppermute | solution.py:390
  88.4 25.2 %collective-permute-start.21 = (bf16[64,4096]{1,0:T(8,128)(2,1)}, bf16[64,4096]{1,0:T(8,128)(2,1)S(1)}, u32[]{:S(2)}, u32[]{:S(2)}) collective-permute-start(bf16[64,4096]{1,0:T(8,128)(2,1)} %collective-permute-done.20.refs_8_), channel_id=1, source_target_pairs={{2,0},{0,2},{6,4},{4,6},{10,8},{8,10},{14,12},{12,14},{18,16},{16,... | collective-permute-start | bytes 1572872 | tf_op jit(solution)/shard_map/ppermute | solution.py:390
  88.5 29.3 %collective-permute-start.18 = (bf16[64,4096]{1,0:T(8,128)(2,1)}, bf16[64,4096]{1,0:T(8,128)(2,1)}, u32[]{:S(2)}, u32[]{:S(2)}) collective-permute-start(bf16[64,4096]{1,0:T(8,128)(2,1)} %collective-permute-done.16.refs_4_), channel_id=1, source_target_pairs={{4,0},{6,2},{0,4},{2,6},{12,8},{14,10},{8,12},{10,14},{20,16},{22,... | collective-permute-start | bytes 1572872 | tf_op jit(solution)/shard_map/ppermute | solution.py:390
  95.9 22.0 %collective-permute-start.17 = (bf16[64,4096]{1,0:T(8,128)(2,1)}, bf16[64,4096]{1,0:T(8,128)(2,1)S(1)}, u32[]{:S(2)}, u32[]{:S(2)}) collective-permute-start(bf16[64,4096]{1,0:T(8,128)(2,1)} %collective-permute-done.16.refs_4_), channel_id=1, source_target_pairs={{2,0},{0,2},{6,4},{4,6},{10,8},{8,10},{14,12},{12,14},{18,16},{16,... | collective-permute-start | bytes 1572872 | tf_op jit(solution)/shard_map/ppermute | solution.py:390
  95.9 8.7 %collective-permute-start.29 = (bf16[256,512]{1,0:T(8,128)(2,1)S(1)}, bf16[256,512]{1,0:T(8,128)(2,1)S(1)}, u32[]{:S(2)}, u32[]{:S(2)}) collective-permute-start(bf16[256,512]{1,0:T(8,128)(2,1)S(1)} %bitcast.313), channel_id=1, source_target_pairs={{0,1},{1,0},{2,3},{3,2},{4,5},{5,4},{6,7},{7,6},{8,9},{9,8},{10,11... | collective-permute-start | bytes 786440 | tf_op jit(solution)/shard_map/ppermute | solution.py:396
  104.6 14.6 %collective-permute-start.11 = (bf16[256,512]{1,0:T(8,128)(2,1)S(1)}, bf16[256,512]{1,0:T(8,128)(2,1)S(1)}, u32[]{:S(2)}, u32[]{:S(2)}) collective-permute-start(bf16[256,512]{1,0:T(8,128)(2,1)S(1)} %bitcast.312), channel_id=1, source_target_pairs={{0,1},{1,0},{2,3},{3,2},{4,5},{5,4},{6,7},{7,6},{8,9},{9,8},{10,11... | collective-permute-start | bytes 786440 | tf_op jit(solution)/shard_map/ppermute | solution.py:396
  113.6 13.6 %collective-permute-start.15 = (bf16[64,4096]{1,0:T(8,128)(2,1)}, bf16[64,4096]{1,0:T(8,128)(2,1)}, u32[]{:S(2)}, u32[]{:S(2)}) collective-permute-start(bf16[64,4096]{1,0:T(8,128)(2,1)} %collective-permute-done.14.refs_2_), channel_id=1, source_target_pairs={{2,0},{0,2},{6,4},{4,6},{10,8},{8,10},{14,12},{12,14},{18,16},{16,... | collective-permute-start | bytes 1572872 | tf_op jit(solution)/shard_map/ppermute | solution.py:390
  114.5 14.2 %collective-permute-start.27 = (bf16[64,4096]{1,0:T(8,128)(2,1)}, bf16[64,4096]{1,0:T(8,128)(2,1)}, u32[]{:S(2)}, u32[]{:S(2)}) collective-permute-start(bf16[64,4096]{1,0:T(8,128)(2,1)} %collective-permute-done.26.refs_14_), channel_id=1, source_target_pairs={{2,0},{0,2},{6,4},{4,6},{10,8},{8,10},{14,12},{12,14},{18,16},{16,... | collective-permute-start | bytes 1572872 | tf_op jit(solution)/shard_map/ppermute | solution.py:390
  117.9 10.8 %collective-permute-start.23 = (bf16[64,4096]{1,0:T(8,128)(2,1)}, bf16[64,4096]{1,0:T(8,128)(2,1)}, u32[]{:S(2)}, u32[]{:S(2)}) collective-permute-start(bf16[64,4096]{1,0:T(8,128)(2,1)} %collective-permute-done.22.refs_10_), channel_id=1, source_target_pairs={{2,0},{0,2},{6,4},{4,6},{10,8},{8,10},{14,12},{12,14},{18,16},{16,... | collective-permute-start | bytes 1572872 | tf_op jit(solution)/shard_map/ppermute | solution.py:390
  118.7 10.0 %collective-permute-start.19 = (bf16[64,4096]{1,0:T(8,128)(2,1)}, bf16[64,4096]{1,0:T(8,128)(2,1)}, u32[]{:S(2)}, u32[]{:S(2)}) collective-permute-start(bf16[64,4096]{1,0:T(8,128)(2,1)} %collective-permute-done.18.refs_6_), channel_id=1, source_target_pairs={{2,0},{0,2},{6,4},{4,6},{10,8},{8,10},{14,12},{12,14},{18,16},{16,... | collective-permute-start | bytes 1572872 | tf_op jit(solution)/shard_map/ppermute | solution.py:390
  119.2 16.5 %collective-permute-start.30 = (bf16[256,1024]{1,0:T(8,128)(2,1)}, bf16[256,1024]{1,0:T(8,128)(2,1)}, u32[]{:S(2)}, u32[]{:S(2)}) collective-permute-start(bf16[256,1024]{1,0:T(8,128)(2,1)} %get-tuple-element.81), channel_id=1, source_target_pairs={{1,0},{0,1},{3,2},{2,3},{5,4},{4,5},{7,6},{6,7},{9,8},{8,9},{11,10... | collective-permute-start | bytes 1572872 | tf_op jit(solution)/shard_map/ppermute | solution.py:393
  127.2 25.4 %collective-permute-start.12 = (bf16[256,1024]{1,0:T(8,128)(2,1)S(1)}, bf16[256,1024]{1,0:T(8,128)(2,1)S(1)}, u32[]{:S(2)}, u32[]{:S(2)}) collective-permute-start(bf16[256,1024]{1,0:T(8,128)(2,1)S(1)} %get-tuple-element.76), channel_id=1, source_target_pairs={{1,0},{0,1},{3,2},{2,3},{5,4},{4,5},{7,6},{6,7},{9,8},{8,9},{11,10... | collective-permute-start | bytes 1572872 | tf_op jit(solution)/shard_map/ppermute | solution.py:393
  170.0 56.5 %collective-permute-start.28 = (bf16[256,1024]{1,0:T(8,128)(2,1)S(1)}, bf16[256,1024]{1,0:T(8,128)(2,1)}, u32[]{:S(2)}, u32[]{:S(2)}) collective-permute-start(bf16[256,1024]{1,0:T(8,128)(2,1)S(1)} %slice.186), channel_id=1, source_target_pairs={{0,1},{1,0},{2,3},{3,2},{4,5},{5,4},{6,7},{7,6},{8,9},{9,8},{10,11... | collective-permute-start | bytes 1572872 | tf_op jit(solution)/shard_map/ppermute | solution.py:396
  170.6 57.2 %collective-permute-start.31 = (bf16[256,1024]{1,0:T(8,128)(2,1)}, bf16[256,1024]{1,0:T(8,128)(2,1)}, u32[]{:S(2)}, u32[]{:S(2)}) collective-permute-start(bf16[256,1024]{1,0:T(8,128)(2,1)} %slice.189), channel_id=1, source_target_pairs={{0,1},{1,0},{2,3},{3,2},{4,5},{5,4},{6,7},{7,6},{8,9},{9,8},{10,11... | collective-permute-start | bytes 1572872 | tf_op jit(solution)/shard_map/ppermute | solution.py:396
  172.1 35.3 %collective-permute-start.32 = (bf16[256,1024]{1,0:T(8,128)(2,1)}, bf16[256,1024]{1,0:T(8,128)(2,1)S(1)}, u32[]{:S(2)}, u32[]{:S(2)}) collective-permute-start(bf16[256,1024]{1,0:T(8,128)(2,1)} %get-tuple-element.166), channel_id=1, source_target_pairs={{0,1},{1,0},{2,3},{3,2},{4,5},{5,4},{6,7},{7,6},{8,9},{9,8},{10,11... | collective-permute-start | bytes 1572872 | tf_op jit(solution)/shard_map/ppermute | solution.py:396
  172.7 46.0 %collective-permute-start.36 = (bf16[256,1024]{1,0:T(8,128)(2,1)S(1)}, bf16[256,1024]{1,0:T(8,128)(2,1)S(1)}, u32[]{:S(2)}, u32[]{:S(2)}) collective-permute-start(bf16[256,1024]{1,0:T(8,128)(2,1)S(1)} %get-tuple-element.168), channel_id=1, source_target_pairs={{0,1},{1,0},{2,3},{3,2},{4,5},{5,4},{6,7},{7,6},{8,9},{9,8},{10,11... | collective-permute-start | bytes 1572872 | tf_op jit(solution)/shard_map/ppermute | solution.py:396
  196.1 156.7 %collective-permute-start.66 = (bf16[8,64,2048]{2,1,0:T(8,128)(2,1)}, bf16[8,64,2048]{2,1,0:T(8,128)(2,1)}, u32[]{:S(2)}, u32[]{:S(2)}) collective-permute-start(bf16[8,64,2048]{2,1,0:T(8,128)(2,1)} %get-tuple-element.122), channel_id=1, source_target_pairs={{2,0},{0,2},{6,4},{4,6},{10,8},{8,10},{14,12},{12,14},{18,16},{16,... | collective-permute-start | bytes 6291464 | tf_op jit(solution)/shard_map/ppermute | solution.py:390
  211.4 25.5 %collective-permute-start.33 = (bf16[256,512]{1,0:T(8,128)(2,1)S(1)}, bf16[256,512]{1,0:T(8,128)(2,1)S(1)}, u32[]{:S(2)}, u32[]{:S(2)}) collective-permute-start(bf16[256,512]{1,0:T(8,128)(2,1)S(1)} %get-tuple-element.84.grad_keep), channel_id=1, source_target_pairs={{1,0},{0,1},{3,2},{2,3},{5,4},{4,5},{7,6},{6,7},{9,8},{8,9},{11,10... | collective-permute-start | bytes 786440 | tf_op jit(solution)/shard_map/ppermute | solution.py:393
  222.6 9.2 %collective-permute-start.37 = (bf16[256,512]{1,0:T(8,128)(2,1)S(1)}, bf16[256,512]{1,0:T(8,128)(2,1)S(1)}, u32[]{:S(2)}, u32[]{:S(2)}) collective-permute-start(bf16[256,512]{1,0:T(8,128)(2,1)S(1)} %get-tuple-element.93.grad_keep), channel_id=1, source_target_pairs={{1,0},{0,1},{3,2},{2,3},{5,4},{4,5},{7,6},{6,7},{9,8},{8,9},{11,10... | collective-permute-start | bytes 786440 | tf_op jit(solution)/shard_map/ppermute | solution.py:393
  226.5 49.4 %collective-permute-start.54 = (bf16[8,64,512]{2,1,0:T(8,128)(2,1)}, bf16[8,64,512]{2,1,0:T(8,128)(2,1)}, u32[]{:S(2)}, u32[]{:S(2)}) collective-permute-start(bf16[8,64,512]{2,1,0:T(8,128)(2,1)} %get-tuple-element.114), channel_id=1, source_target_pairs={{2,0},{0,2},{6,4},{4,6},{10,8},{8,10},{14,12},{12,14},{18,16},{16,... | collective-permute-start | bytes 1572872 | tf_op jit(solution)/shard_map/ppermute | solution.py:390
  240.4 12.7 %collective-permute-start.34 = (f32[8,1,512]{2,1,0:T(1,128)S(1)}, f32[8,1,512]{2,1,0:T(1,128)S(1)}, u32[]{:S(2)}, u32[]{:S(2)}) collective-permute-start(f32[8,1,512]{2,1,0:T(1,128)S(1)} %get-tuple-element.86), channel_id=1, source_target_pairs={{1,0},{0,1},{3,2},{2,3},{5,4},{4,5},{7,6},{6,7},{9,8},{8,9},{11,10... | collective-permute-start | bytes 49160 | tf_op jit(solution)/shard_map/ppermute | solution.py:393
  251.6 39.5 %collective-permute-start.39 = (bf16[256,512]{1,0:T(8,128)(2,1)}, bf16[256,512]{1,0:T(8,128)(2,1)S(1)}, u32[]{:S(2)}, u32[]{:S(2)}) collective-permute-start(bf16[256,512]{1,0:T(8,128)(2,1)} %bitcast.31), channel_id=1, source_target_pairs={{0,1},{1,0},{2,3},{3,2},{4,5},{5,4},{6,7},{7,6},{8,9},{9,8},{10,11... | collective-permute-start | bytes 786440 | tf_op jit(solution)/shard_map/ppermute | solution.py:396
  263.0 15.6 %collective-permute-start.35 = (bf16[256,512]{1,0:T(8,128)(2,1)S(1)}, bf16[256,512]{1,0:T(8,128)(2,1)S(1)}, u32[]{:S(2)}, u32[]{:S(2)}) collective-permute-start(bf16[256,512]{1,0:T(8,128)(2,1)S(1)} %bitcast.311), channel_id=1, source_target_pairs={{0,1},{1,0},{2,3},{3,2},{4,5},{5,4},{6,7},{7,6},{8,9},{9,8},{10,11... | collective-permute-start | bytes 786440 | tf_op jit(solution)/shard_map/ppermute | solution.py:396
  265.4 65.9 %collective-permute-start.40 = (bf16[8,64,512]{2,1,0:T(8,128)(2,1)S(1)}, bf16[8,64,512]{2,1,0:T(8,128)(2,1)}, u32[]{:S(2)}, u32[]{:S(2)}) collective-permute-start(bf16[8,64,512]{2,1,0:T(8,128)(2,1)S(1)} %get-tuple-element.106), channel_id=1, source_target_pairs={{2,0},{0,2},{6,4},{4,6},{10,8},{8,10},{14,12},{12,14},{18,16},{16,... | collective-permute-start | bytes 1572872 | tf_op jit(solution)/shard_map/ppermute | solution.py:390
  304.4 7.7 %collective-permute-start.71 = (f32[6,1024]{1,0:T(8,128)S(1)}, f32[6,1024]{1,0:T(8,128)S(1)}, u32[]{:S(2)}, u32[]{:S(2)}) collective-permute-start(f32[6,1024]{1,0:T(8,128)S(1)} %maximum_add_fusion), channel_id=1, source_target_pairs={{2,0},{0,2},{6,4},{4,6},{10,8},{8,10},{14,12},{12,14},{18,16},{16,... | collective-permute-start | bytes 73736 | tf_op jit(solution)/shard_map/ppermute | solution.py:390
  317.2 34.0 %collective-permute-start.47 = (bf16[8,64,1024]{2,1,0:T(8,128)(2,1)S(1)}, bf16[8,64,1024]{2,1,0:T(8,128)(2,1)S(1)}, u32[]{:S(2)}, u32[]{:S(2)}) collective-permute-start(bf16[8,64,1024]{2,1,0:T(8,128)(2,1)S(1)} %get-tuple-element.108), channel_id=1, source_target_pairs={{2,0},{0,2},{6,4},{4,6},{10,8},{8,10},{14,12},{12,14},{18,16},{16,... | collective-permute-start | bytes 3145736 | tf_op jit(solution)/shard_map/ppermute | solution.py:390
  319.0 13.7 %collective-permute-start.77 = (f32[6,1024]{1,0:T(8,128)S(1)}, f32[6,1024]{1,0:T(8,128)S(1)}, u32[]{:S(2)}, u32[]{:S(2)}) collective-permute-start(f32[6,1024]{1,0:T(8,128)S(1)} %add_add_fusion.3), channel_id=1, source_target_pairs={{24,0},{26,2},{28,4},{30,6},{0,8},{2,10},{4,12},{6,14},{8,16},{10,... | collective-permute-start | bytes 73736 | tf_op jit(solution)/shard_map/ppermute | solution.py:390
  335.3 7.8 %collective-permute-start.57 = (bf16[4,64,256]{2,1,0:T(8,128)(2,1)S(1)}, bf16[4,64,256]{2,1,0:T(8,128)(2,1)S(1)}, u32[]{:S(2)}, u32[]{:S(2)}) collective-permute-start(bf16[4,64,256]{2,1,0:T(8,128)(2,1)S(1)} %get-tuple-element.179), channel_id=1, source_target_pairs={{0,5},{1,4},{2,7},{3,6},{4,1},{5,0},{6,3},{7,2},{8,13},{9,12},{10,... | collective-permute-start | bytes 393224 | tf_op jit(solution)/shard_map/ppermute | solution.py:405
  345.5 10.4 %collective-permute-start.61 = (bf16[8,64,2048]{2,1,0:T(8,128)(2,1)S(1)}, bf16[8,64,2048]{2,1,0:T(8,128)(2,1)S(1)}, u32[]{:S(2)}, u32[]{:S(2)}) collective-permute-start(bf16[8,64,2048]{2,1,0:T(8,128)(2,1)S(1)} %copy-done.75), channel_id=1, source_target_pairs={{2,0},{0,2},{6,4},{4,6},{10,8},{8,10},{14,12},{12,14},{18,16},{16,... | collective-permute-start | bytes 6291464 | tf_op jit(solution)/shard_map/ppermute | solution.py:390
  345.5 14.2 %collective-permute-start.58 = (bf16[64,256]{1,0:T(8,128)(2,1)S(1)}, bf16[64,256]{1,0:T(8,128)(2,1)S(1)}, u32[]{:S(2)}, u32[]{:S(2)}) collective-permute-start(bf16[64,256]{1,0:T(8,128)(2,1)S(1)} %get-tuple-element.170), channel_id=1, source_target_pairs={{24,0},{26,2},{28,4},{30,6},{0,8},{2,10},{4,12},{6,14},{8,16},{10,... | collective-permute-start | bytes 98312 | tf_op jit(solution)/shard_map/ppermute | solution.py:390
  348.9 13.3 %collective-permute-start.60 = (bf16[64,256]{1,0:T(8,128)(2,1)S(1)}, bf16[64,256]{1,0:T(8,128)(2,1)S(1)}, u32[]{:S(2)}, u32[]{:S(2)}) collective-permute-start(bf16[64,256]{1,0:T(8,128)(2,1)S(1)} %get-tuple-element.171), channel_id=1, source_target_pairs={{8,0},{10,2},{12,4},{14,6},{16,8},{18,10},{20,12},{22,14},{24,16},... | collective-permute-start | bytes 98312 | tf_op jit(solution)/shard_map/ppermute | solution.py:390
  351.2 11.2 %collective-permute-start.59 = (bf16[64,256]{1,0:T(8,128)(2,1)S(1)}, bf16[64,256]{1,0:T(8,128)(2,1)S(1)}, u32[]{:S(2)}, u32[]{:S(2)}) collective-permute-start(bf16[64,256]{1,0:T(8,128)(2,1)S(1)} %get-tuple-element.172), channel_id=1, source_target_pairs={{16,0},{18,2},{20,4},{22,6},{24,8},{26,10},{28,12},{30,14},{0,16},... | collective-permute-start | bytes 98312 | tf_op jit(solution)/shard_map/ppermute | solution.py:390
  352.8 10.4 %collective-permute-start.44 = (bf16[64,256]{1,0:T(8,128)(2,1)S(1)}, bf16[64,256]{1,0:T(8,128)(2,1)S(1)}, u32[]{:S(2)}, u32[]{:S(2)}) collective-permute-start(bf16[64,256]{1,0:T(8,128)(2,1)S(1)} %get-tuple-element.173), channel_id=1, source_target_pairs={{24,0},{26,2},{28,4},{30,6},{0,8},{2,10},{4,12},{6,14},{8,16},{10,... | collective-permute-start | bytes 98312 | tf_op jit(solution)/shard_map/ppermute | solution.py:390
  355.9 41.8 %collective-permute-start.67 = (bf16[4,64,2048]{2,1,0:T(8,128)(2,1)S(1)}, bf16[4,64,2048]{2,1,0:T(8,128)(2,1)S(1)}, u32[]{:S(2)}, u32[]{:S(2)}) collective-permute-start(bf16[4,64,2048]{2,1,0:T(8,128)(2,1)S(1)} %pad_maximum_fusion.4), channel_id=1, source_target_pairs={{4,0},{6,2},{0,4},{2,6},{12,8},{14,10},{8,12},{10,14},{20,16},{22,... | collective-permute-start | bytes 3145736 | tf_op jit(solution)/shard_map/ppermute | solution.py:390
  362.5 9.1 %collective-permute-start.50 = (bf16[4,64,512]{2,1,0:T(8,128)(2,1)S(1)}, bf16[4,64,512]{2,1,0:T(8,128)(2,1)S(1)}, u32[]{:S(2)}, u32[]{:S(2)}) collective-permute-start(bf16[4,64,512]{2,1,0:T(8,128)(2,1)S(1)} %fusion.20), channel_id=1, source_target_pairs={{0,5},{1,4},{2,7},{3,6},{4,1},{5,0},{6,3},{7,2},{8,13},{9,12},{10,... | collective-permute-start | bytes 786440 | tf_op jit(solution)/shard_map/ppermute | solution.py:405
  363.1 10.3 %collective-permute-start.49 = (bf16[4,64,512]{2,1,0:T(8,128)(2,1)S(1)}, bf16[4,64,512]{2,1,0:T(8,128)(2,1)S(1)}, u32[]{:S(2)}, u32[]{:S(2)}) collective-permute-start(bf16[4,64,512]{2,1,0:T(8,128)(2,1)S(1)} %fusion.13), channel_id=1, source_target_pairs={{0,1},{1,0},{2,3},{3,2},{4,5},{5,4},{6,7},{7,6},{8,9},{9,8},{10,11... | collective-permute-start | bytes 786440 | tf_op jit(solution)/shard_map/ppermute | solution.py:405
  364.9 28.8 %collective-permute-start.48 = (bf16[4,64,512]{2,1,0:T(8,128)(2,1)S(1)}, bf16[4,64,512]{2,1,0:T(8,128)(2,1)S(1)}, u32[]{:S(2)}, u32[]{:S(2)}) collective-permute-start(bf16[4,64,512]{2,1,0:T(8,128)(2,1)S(1)} %get-tuple-element.160), channel_id=1, source_target_pairs={{0,4},{1,5},{2,6},{3,7},{4,0},{5,1},{6,2},{7,3},{8,12},{9,13},{10,... | collective-permute-start | bytes 786440 | tf_op jit(solution)/shard_map/ppermute | solution.py:405
  367.0 45.2 %collective-permute-start.62 = (bf16[4,64,2048]{2,1,0:T(8,128)(2,1)S(1)}, bf16[4,64,2048]{2,1,0:T(8,128)(2,1)}, u32[]{:S(2)}, u32[]{:S(2)}) collective-permute-start(bf16[4,64,2048]{2,1,0:T(8,128)(2,1)S(1)} %pad_maximum_fusion.3), channel_id=1, source_target_pairs={{4,0},{6,2},{0,4},{2,6},{12,8},{14,10},{8,12},{10,14},{20,16},{22,... | collective-permute-start | bytes 3145736 | tf_op jit(solution)/shard_map/ppermute | solution.py:390
  393.8 8.6 %collective-permute-start.51 = (bf16[64,512]{1,0:T(8,128)(2,1)S(1)}, bf16[64,512]{1,0:T(8,128)(2,1)S(1)}, u32[]{:S(2)}, u32[]{:S(2)}) collective-permute-start(bf16[64,512]{1,0:T(8,128)(2,1)S(1)} %get-tuple-element.157), channel_id=1, source_target_pairs={{24,0},{26,2},{28,4},{30,6},{0,8},{2,10},{4,12},{6,14},{8,16},{10,... | collective-permute-start | bytes 196616 | tf_op jit(solution)/shard_map/ppermute | solution.py:390
  395.8 8.4 %collective-permute-start.53 = (bf16[64,512]{1,0:T(8,128)(2,1)S(1)}, bf16[64,512]{1,0:T(8,128)(2,1)S(1)}, u32[]{:S(2)}, u32[]{:S(2)}) collective-permute-start(bf16[64,512]{1,0:T(8,128)(2,1)S(1)} %get-tuple-element.158), channel_id=1, source_target_pairs={{8,0},{10,2},{12,4},{14,6},{16,8},{18,10},{20,12},{22,14},{24,16},... | collective-permute-start | bytes 196616 | tf_op jit(solution)/shard_map/ppermute | solution.py:390
  397.7 7.7 %collective-permute-start.52 = (bf16[64,512]{1,0:T(8,128)(2,1)S(1)}, bf16[64,512]{1,0:T(8,128)(2,1)S(1)}, u32[]{:S(2)}, u32[]{:S(2)}) collective-permute-start(bf16[64,512]{1,0:T(8,128)(2,1)S(1)} %get-tuple-element.159), channel_id=1, source_target_pairs={{16,0},{18,2},{20,4},{22,6},{24,8},{26,10},{28,12},{30,14},{0,16},... | collective-permute-start | bytes 196616 | tf_op jit(solution)/shard_map/ppermute | solution.py:390
  400.4 17.3 %collective-permute-start.68 = (bf16[64,2048]{1,0:T(8,128)(2,1)}, bf16[64,2048]{1,0:T(8,128)(2,1)S(1)}, u32[]{:S(2)}, u32[]{:S(2)}) collective-permute-start(bf16[64,2048]{1,0:T(8,128)(2,1)} %get-tuple-element.127), channel_id=1, source_target_pairs={{24,0},{26,2},{28,4},{30,6},{0,8},{2,10},{4,12},{6,14},{8,16},{10,... | collective-permute-start | bytes 786440 | tf_op jit(solution)/shard_map/ppermute | solution.py:390
  402.4 21.0 %collective-permute-start.70 = (bf16[64,2048]{1,0:T(8,128)(2,1)}, bf16[64,2048]{1,0:T(8,128)(2,1)}, u32[]{:S(2)}, u32[]{:S(2)}) collective-permute-start(bf16[64,2048]{1,0:T(8,128)(2,1)} %get-tuple-element.128), channel_id=1, source_target_pairs={{8,0},{10,2},{12,4},{14,6},{16,8},{18,10},{20,12},{22,14},{24,16},... | collective-permute-start | bytes 786440 | tf_op jit(solution)/shard_map/ppermute | solution.py:390
  404.3 32.2 %collective-permute-start.69 = (bf16[64,2048]{1,0:T(8,128)(2,1)}, bf16[64,2048]{1,0:T(8,128)(2,1)}, u32[]{:S(2)}, u32[]{:S(2)}) collective-permute-start(bf16[64,2048]{1,0:T(8,128)(2,1)} %get-tuple-element.129), channel_id=1, source_target_pairs={{16,0},{18,2},{20,4},{22,6},{24,8},{26,10},{28,12},{30,14},{0,16},... | collective-permute-start | bytes 786440 | tf_op jit(solution)/shard_map/ppermute | solution.py:390
  413.8 24.9 %collective-permute-start.63 = (bf16[64,2048]{1,0:T(8,128)(2,1)S(1)}, bf16[64,2048]{1,0:T(8,128)(2,1)S(1)}, u32[]{:S(2)}, u32[]{:S(2)}) collective-permute-start(bf16[64,2048]{1,0:T(8,128)(2,1)S(1)} %get-tuple-element.130), channel_id=1, source_target_pairs={{24,0},{26,2},{28,4},{30,6},{0,8},{2,10},{4,12},{6,14},{8,16},{10,... | collective-permute-start | bytes 786440 | tf_op jit(solution)/shard_map/ppermute | solution.py:390
  416.4 22.4 %collective-permute-start.65 = (bf16[64,2048]{1,0:T(8,128)(2,1)S(1)}, bf16[64,2048]{1,0:T(8,128)(2,1)S(1)}, u32[]{:S(2)}, u32[]{:S(2)}) collective-permute-start(bf16[64,2048]{1,0:T(8,128)(2,1)S(1)} %get-tuple-element.131), channel_id=1, source_target_pairs={{8,0},{10,2},{12,4},{14,6},{16,8},{18,10},{20,12},{22,14},{24,16},... | collective-permute-start | bytes 786440 | tf_op jit(solution)/shard_map/ppermute | solution.py:390
  417.7 27.0 %collective-permute-start.64 = (bf16[64,2048]{1,0:T(8,128)(2,1)S(1)}, bf16[64,2048]{1,0:T(8,128)(2,1)S(1)}, u32[]{:S(2)}, u32[]{:S(2)}) collective-permute-start(bf16[64,2048]{1,0:T(8,128)(2,1)S(1)} %get-tuple-element.132), channel_id=1, source_target_pairs={{16,0},{18,2},{20,4},{22,6},{24,8},{26,10},{28,12},{30,14},{0,16},... | collective-permute-start | bytes 786440 | tf_op jit(solution)/shard_map/ppermute | solution.py:390
  (91 other events, 880.3 us)

commit v2 on v1

v2 whole, which is shorter than its diff:
```python
import functools

import jax
import jax.numpy as jnp
from jax import lax
from jax.experimental import pallas as pl
from jax.experimental.pallas import tpu as pltpu
from jax.sharding import PartitionSpec as P

HD = 64
HEADS = 8
CHUNKS = 2
EPS = 1e-05
BF = jnp.bfloat16
F32 = jnp.float32
MIB = 1024 * 1024
VMEM = 56
COST = 1
COST = 50

NN = (((1,), (0,)), ((), ()))
NT = (((1,), (1,)), ((), ()))
TN = (((0,), (0,)), ((), ()))


def dot(left, right, form=NN):
    return lax.dot_general(left, right, form, preferred_element_type=F32)


def struct(shape, dtype):
    return jax.ShapeDtypeStruct(shape, dtype)


def call(kernel, grid, in_specs, out_specs, out_shape, scratch, ids, args, flops, name, alias=None):
    scalars = ids if isinstance(ids, (list, tuple)) else [ids]
    moved = sum(a.size * a.dtype.itemsize for a in args if a.ndim < 4)
    moved += sum(o.size * jnp.dtype(o.dtype).itemsize for o in out_shape)
    return pl.pallas_call(
        kernel,
        grid_spec=pltpu.PrefetchScalarGridSpec(
            num_scalar_prefetch=len(scalars),
            grid=grid,
            in_specs=in_specs,
            out_specs=out_specs,
            scratch_shapes=scratch,
        ),
        out_shape=out_shape,
        input_output_aliases={len(scalars) + k: v for k, v in (alias or {}).items()},
        compiler_params=pltpu.CompilerParams(
            vmem_limit_bytes=VMEM * MIB, dimension_semantics=("arbitrary",) * len(grid)
        ),
        cost_estimate=pl.CostEstimate(
            flops=int(flops) // COST, bytes_accessed=int(moved) // COST, transcendentals=0
        ),
        name=name,
    )(*scalars, *args)


def whole(array):
    zeros = (0,) * array.ndim
    return pl.BlockSpec(array.shape, lambda *_: zeros)


def rows_of(block, width, first=0):
    return pl.BlockSpec((block, width), lambda i, *_: (i + first, 0))


def fixed_rows(block, width, at=0):
    return pl.BlockSpec((block, width), lambda *_: (at, 0))


def images_of(block, rows, width, first=0):
    return pl.BlockSpec((block, rows, width), lambda i, *_: (i + first, 0, 0))


def third(array, width, at):
    if width % 128:
        return whole(array)
    return pl.BlockSpec(array.shape[:2] + (width,), lambda *_: (0, 0, at))


def columns(ref, group, width, at):
    if ref.shape[2] == width:
        return ref[group]
    return ref[group, :, at * width : (at + 1) * width]


def anywhere():
    return pl.BlockSpec(memory_space=pl.ANY)


def tie(values, *first):
    flat, tree = jax.tree.flatten(values)
    out = lax.optimization_barrier(tuple(flat) + tuple(jax.tree.leaves(first)))
    return jax.tree.unflatten(tree, out[: len(flat)])


def norm_parts(values):
    centre = values - jnp.mean(values, axis=-1, keepdims=True)
    rstd = lax.rsqrt(jnp.mean(centre * centre, axis=-1, keepdims=True) + EPS)
    return centre * rstd, rstd


def norm_back(values, gain, grad):
    xhat, rstd = norm_parts(values)
    scaled = grad * gain
    first = jnp.mean(scaled, axis=-1, keepdims=True)
    second = jnp.mean(scaled * xhat, axis=-1, keepdims=True)
    return rstd * (scaled - first - xhat * second), grad * xhat


def fold_rows(value):
    return jnp.sum(value.reshape(value.shape[0] // 8, 8, value.shape[1]), axis=0)


def norm_kernel(
    imgs, lat, share, patch, ids, media, latents, m_gain, m_bias, l_gain, l_bias, src, nlat, keep
):
    start = pl.multiple_of(ids[0] * share, share)
    step = patch + share
    for i in range(imgs):
        xhat, _ = norm_parts(media[i].astype(F32))
        src[i * step : i * step + patch, :] = (xhat * m_gain[...] + m_bias[...]).astype(BF)
        xhat, _ = norm_parts(latents[i].astype(F32))
        normed = xhat * l_gain[...] + l_bias[...]
        nlat[i * lat : (i + 1) * lat, :] = normed.astype(BF)
        keep[...] = normed
        src[i * step + patch : (i + 1) * step, :] = keep[pl.ds(start, share), :].astype(BF)


def assemble(entries, pieces, depth, ids, rows, groups, width, name):
    def kernel(ids_ref, *refs):
        out, sems = refs[len(pieces)], refs[len(pieces) + 1]
        copies = []
        for e, (op, lead, group, s, yf, cf) in enumerate(entries):
            block = lax.rem(ids_ref[1] + s, depth) * 4
            block += lax.rem(ids_ref[2] + yf, 2) * 2 + lax.rem(ids_ref[3] + cf, 2)
            start = pl.multiple_of(block * rows, rows)
            source = refs[op] if lead is None else refs[op].at[lead]
            copies.append(
                pltpu.make_async_copy(source, out.at[group, pl.ds(start, rows), :], sems.at[e])
            )
        for copy in copies:
            copy.start()
        for copy in copies:
            copy.wait()

    return call(
        kernel,
        (1,),
        [anywhere()] * len(pieces),
        [pl.BlockSpec((groups, depth * 4 * rows, width), lambda *_: (0, 0, 0))],
        [struct((groups, depth * 4 * rows, width), BF)],
        [pltpu.SemaphoreType.DMA((len(entries),))],
        ids,
        pieces,
        0,
        name,
    )[0]


def diag_mask(heads, width, dtype):
    row = lax.broadcasted_iota(jnp.int32, (heads * HD, width), 0) // HD
    col = lax.broadcasted_iota(jnp.int32, (heads * HD, width), 1) // HD
    return jnp.where(row == col, 1.0, 0.0).astype(dtype)


def spread(block, heads, mask):
    return jnp.concatenate([block] * heads, axis=0) * mask


def fold(full, heads, lat, mask):
    full = full * mask
    total = full[:lat]
    for h in range(1, heads):
        total = total + full[h * lat : (h + 1) * lat]
    return total


def lane_roll(values, s, groups, cw):
    if s == 0:
        return values
    if cw % 128 == 0:
        cut = (groups - s) * cw
        return jnp.concatenate([values[:, cut:], values[:, :cut]], axis=1)
    return pltpu.roll(values, s * cw, 1)


def project_kernel(groups, cw, imgs, step, lat, ids, src, nlat, w, q, k, stats):
    heads = cw // HD
    for j in range(groups):
        k[:, j * cw : (j + 1) * cw] = dot(src[...], w[j, :, cw:]).astype(BF)
        q[:, j * cw : (j + 1) * cw] = (dot(nlat[...], w[j, :, :cw]) * (HD**-0.5)).astype(BF)
    mask = diag_mask(heads, cw, BF)
    for i in range(imgs):
        for j in range(groups):
            cols = slice(j * cw, (j + 1) * cw)
            qbd = spread(q[i * lat : (i + 1) * lat, cols], heads, mask)
            score = dot(k[i * step : (i + 1) * step, cols], qbd, NT)
            top = jnp.max(score, axis=0, keepdims=True)
            stats[i, 0:1, cols] = top
            stats[i, 1:2, cols] = jnp.sum(jnp.exp(score - top), axis=0, keepdims=True)


def values_kernel(groups, cw, ids, src, w, v):
    for j in range(groups):
        v[:, j * cw : (j + 1) * cw] = dot(src[...], columns(w, j, cw, 0)).astype(BF)


def send_rows(groups, share, ids, scratch, i, keep, send):
    for s in range(groups):
        start = pl.multiple_of(lax.rem(ids[0] + s, groups) * share, share)
        rows = scratch[pl.ds(start, share), :]
        if s == 0:
            keep[i * share : (i + 1) * share, :] = rows
        else:
            send[s - 1, i * share : (i + 1) * share, :] = rows.astype(BF)


def mix_kernel(groups, cw, imgs, step, lat, share, ids, q, k, v, lse, keep, send, scratch):
    heads = cw // HD
    mask, fmask = diag_mask(heads, cw, BF), diag_mask(heads, cw, F32)
    for i in range(imgs):
        rows = slice(i * step, (i + 1) * step)
        for j in range(groups):
            cols = slice(j * cw, (j + 1) * cw)
            qbd = spread(q[i * lat : (i + 1) * lat, cols], heads, mask)
            probs = jnp.exp(dot(k[rows, cols], qbd, NT) - lse[i, 0:1, cols])
            full = dot(probs.astype(BF), v[rows, cols], TN)
            scratch[i, :, cols] = fold(full, heads, lat, fmask)
        send_rows(groups, share, ids, scratch.at[i], i, keep, send)


def back_probs_kernel(groups, cw, imgs, step, lat, share, first, ids, q, k, v, lse, grad_keep, *refs):
    recv, refs = refs[: groups - 1], refs[groups - 1 :]
    gv, grad_all, delta, scratch = refs if first else refs[1:]
    heads = cw // HD
    mask = diag_mask(heads, cw, BF)
    for i in range(imgs):
        for s in range(groups):
            start = pl.multiple_of(lax.rem(ids[0] + s, groups) * share, share)
            block = grad_keep if s == 0 else recv[s - 1]
            block = lane_roll(block[i * share : (i + 1) * share, :].astype(F32), s, groups, cw)
            scratch[i, pl.ds(start, share), :] = block
        grad_all[i * lat : (i + 1) * lat, :] = scratch[i].astype(BF)
        rows = slice(i * step, (i + 1) * step)
        for j in range(groups):
            cols = slice(j * cw, (j + 1) * cw)
            qbd = spread(q[i * lat : (i + 1) * lat, cols], heads, mask)
            gbd = spread(grad_all[i * lat : (i + 1) * lat, cols], heads, mask)
            probs = jnp.exp(dot(k[rows, cols], qbd, NT) - lse[i, 0:1, cols])
            delta[i, 0:1, cols] = jnp.sum(probs * dot(v[rows, cols], gbd, NT), axis=0, keepdims=True)
            gv[rows, cols] = dot(probs.astype(BF), gbd).astype(BF)


def back_scores_kernel(
    groups, cw, imgs, step, lat, share, first, ids, q, k, v, lse, grad_all, delta, *refs
):
    gk, gq, keep, send, scratch = refs if first else refs[2:]
    heads = cw // HD
    mask, fmask = diag_mask(heads, cw, BF), diag_mask(heads, cw, F32)
    for i in range(imgs):
        rows = slice(i * step, (i + 1) * step)
        for j in range(groups):
            cols = slice(j * cw, (j + 1) * cw)
            qbd = spread(q[i * lat : (i + 1) * lat, cols], heads, mask)
            gbd = spread(grad_all[i * lat : (i + 1) * lat, cols], heads, mask)
            probs = jnp.exp(dot(k[rows, cols], qbd, NT) - lse[i, 0:1, cols])
            grad = dot(v[rows, cols], gbd, NT) - delta[i, 0:1, cols]
            grad = (probs * grad).astype(BF)
            gk[rows, cols] = dot(grad, qbd).astype(BF)
            full = dot(grad, k[rows, cols], TN)
            scratch[i, :, cols] = fold(full, heads, lat, fmask) * (HD**-0.5)
        gq[i * lat : (i + 1) * lat, :] = scratch[i].astype(BF)
        send_rows(groups, share, ids, scratch.at[i], i, keep, send)


def middle_kernel(groups, cw, ids, keep, *refs):
    recv = refs[: groups - 1]
    latents, w, gain, bias, mixed, middle, normed = refs[groups - 1 :]
    total = keep[...]
    for s in range(1, groups):
        total = total + lane_roll(recv[s - 1][...].astype(F32), s, groups, cw)
    low = total.astype(BF)
    mixed[...] = low
    value = latents[...].astype(F32).reshape(middle.shape)
    for j in range(groups):
        value = value + dot(low[:, j * cw : (j + 1) * cw], columns(w, j, cw, 1), NT)
    middle[...] = value
    xhat, _ = norm_parts(value)
    normed[...] = (xhat * gain[...] + bias[...]).astype(BF)


def gelu_parts(value):
    cdf = 0.5 * (1.0 + lax.erf(value * (0.5**0.5)))
    pdf = jnp.exp(value * value * -0.5) * 0.3989422804014327
    return value * cdf, cdf + value * pdf


def forward_kernel(terms, ids, *refs):
    normed, final = refs[:terms], refs[terms : 2 * terms]
    up, down, hidden, up_low, ff, mid, normed_all, final_all, ff_total, mid_total = refs[2 * terms :]
    step = pl.program_id(0)

    @pl.when(step == 0)
    def _():
        at = 0
        for left, right in zip(normed, final):
            normed_all[at : at + left.shape[0], :] = left[...]
            final_all[at : at + left.shape[0], :] = right[...]
            at += left.shape[0]

    act, slope = gelu_parts(dot(normed_all[...], up[...]))
    low = act.astype(BF)
    hidden[...] = low
    ff_part = dot(low, down[...], NT)
    low = (dot(final_all[...], down[...]) * slope).astype(BF)
    up_low[...] = low
    mid_part = dot(low, up[...], NT)
    last = pl.num_programs(0) - 1

    @pl.when(step == 0)
    def _():
        ff_total[...] = ff_part
        mid_total[...] = mid_part

    @pl.when(step > 0)
    def _():
        ff_total[...] += ff_part
        mid_total[...] += mid_part

    @pl.when(step == last)
    def _():
        ff[...] = ff_total[...].astype(BF)
        mid[...] = mid_total[...].astype(BF)


def middle_back_kernel(groups, cw, ids, part, *refs):
    recv = refs[: groups - 1]
    middle, final, w, gain, grad_mid, mid_low, grad_mixed, gains = refs[groups - 1 :]
    total = part[...].astype(F32)
    for other in recv:
        total = total + other[...].astype(F32)
    back, terms = norm_back(middle[...], gain[...], total)
    gains[0:1, :] = jnp.sum(terms, axis=0, keepdims=True)
    gains[1:2, :] = jnp.sum(total, axis=0, keepdims=True)
    value = final[...].astype(F32) + back
    grad_mid[...] = value
    low = value.astype(BF)
    mid_low[...] = low
    for j in range(groups):
        grad_mixed[:, j * cw : (j + 1) * cw] = dot(low, columns(w, j, cw, 1)).astype(BF)


def weight_grad_kernel(plan, rows, split, ids, *refs):
    count = sum(n + m for n, m, _ in plan)
    if split:
        keep, send, total, turned = refs[count:]
    else:
        out, turned = refs[count:]
    first = step = 0
    for n, m, steps in plan:
        left, right = refs[first : first + n], refs[first + n : first + n + m]
        first += n + m
        size = sum(a.shape[0] for a in left)

        @pl.when(pl.program_id(0) == step)
        def _(left=left):
            at = 0
            for a in left:
                turned[:, at : at + a.shape[0]] = a[...].T
                at += a.shape[0]

        @pl.when((pl.program_id(0) >= step) & (pl.program_id(0) < step + steps))
        def _(right=right):
            at, value = 0, None
            for a in right:
                term = dot(turned[:, at : at + a.shape[0]], a[...])
                value = term if value is None else value + term
                at += a.shape[0]
            if split:
                total[...] = value
            else:
                out[...] = value.astype(BF)

        step += steps
    if not split:
        return
    for b in range(keep.shape[0]):
        for ref, core in ((keep, ids[3]), (send, 1 - ids[3])):
            start = pl.multiple_of((b * 2 + core) * rows, rows)
            ref[b] = total[pl.ds(start, rows), :].astype(BF)


def weight_grad(ids, results, rows, depth, block, name, split=True):
    plan, specs, args, step, most, flops = [], [], [], 0, 0, 0
    for left, right in results:
        width = right[0][0].shape[1]
        steps = width // block
        size = 0
        for array, spec in left:
            args.append(array)
            specs.append(spec)
        for array, count, at in right:

            def place(i, *_, at=at, step=step, steps=steps):
                return at, jnp.clip(i - step, 0, steps - 1)

            args.append(array)
            specs.append(pl.BlockSpec((count, block), place))
            size += count
        plan.append((len(left), len(right), steps))
        step += steps
        most = max(most, size)
        flops += 2 * size * depth * width
    blocks = depth // rows // 2
    turned = pltpu.VMEM((depth, most), BF)
    if split:
        outs = [struct((blocks, rows, step * block), BF)] * 2
        out_specs = [pl.BlockSpec((blocks, rows, block), lambda i, *_: (0, 0, i))] * 2
        scratch = [pltpu.VMEM((depth, block), F32), turned]
    else:
        outs = [struct((depth, step * block), BF)]
        out_specs = [pl.BlockSpec((depth, block), lambda i, *_: (0, i))]
        scratch = [turned]
    return call(
        functools.partial(weight_grad_kernel, plan, rows, split),
        (step,),
        specs,
        out_specs,
        outs,
        scratch,
        ids,
        args,
        flops,
        name,
    )


def source_back_kernel(
    groups, cw, imgs, patch, share, first, ids, live, gk, gv, wk, wv, media, latents, cot, keep, *refs
):
    recv, refs = refs[: groups - 1], refs[groups - 1 :]
    grad_mid, m_gain, l_gain = refs[:3]
    refs = refs[3:] if first == 0 else refs[5:]
    media_grad, latent_grad, gains, total, lat_total, query = refs
    base = (pl.program_id(0) + first) * imgs
    step = patch + share
    value = dot(gk[:, :cw], wk[0, :, cw:], NT) + dot(gv[:, :cw], columns(wv, 0, cw, 0), NT)
    for j in range(1, groups):
        cols = slice(j * cw, (j + 1) * cw)
        value = value + dot(gk[:, cols], wk[j, :, cw:], NT)
        value = value + dot(gv[:, cols], columns(wv, j, cw, 0), NT)
    total[...] = value
    asked = keep[...]
    for s in range(1, groups):
        asked = asked + lane_roll(recv[s - 1][...].astype(F32), s, groups, cw)
    query[...] = asked.astype(BF)
    value = dot(query[:, :cw], wk[0, :, :cw], NT)
    for j in range(1, groups):
        value = value + dot(query[:, j * cw : (j + 1) * cw], wk[j, :, :cw], NT)
    lat_total[...] = value

    @pl.when(pl.program_id(0) == 0)
    def _():
        gains[...] = jnp.zeros_like(gains)

    sums = [0.0] * 4
    for i in range(imgs):
        grad = total[i * step : i * step + patch, :]
        back, terms = norm_back(media[i].astype(F32), m_gain[...], grad)
        media_grad[i] = back
        sums[0] += fold_rows(terms)
        sums[1] += fold_rows(grad)
        rows = slice(i * share, (i + 1) * share)
        grad = total[i * step + patch : (i + 1) * step, :] + lat_total[rows, :]
        back, terms = norm_back(latents[i].astype(F32), l_gain[...], grad)
        sums[2] += fold_rows(terms)
        sums[3] += fold_rows(grad)
        latent_grad[i] = jnp.where(
            live[base + i] > 0, grad_mid[rows, :] + back, cot[i].astype(F32)
        )
    for k in range(4):
        gains[k : k + 1, :] += jnp.sum(sums[k], axis=0, keepdims=True)


def make_local(depth_z, groups):
    dp_size = depth_z * 4

    def from_dp(value, s=0, yf=0, cf=0):
        pairs = []
        for dst in range(dp_size):
            z, y, c = dst // 4, dst // 2 % 2, dst % 2
            pairs.append(((z + s) % depth_z * 4 + (y ^ yf) * 2 + (c ^ cf), dst))
        return lax.ppermute(value, "dp", pairs)

    def from_head(value, s):
        return lax.ppermute(value, "head", [((x + s) % groups, x) for x in range(groups)])

    def to_head(value, s):
        return lax.ppermute(value, "head", [(x, (x + s) % groups) for x in range(groups)])

    def plane(value, sx, yf, back, cf=0):
        pairs = []
        for dst in range(dp_size):
            for x in range(groups):
                other = (dst ^ (2 * yf + cf)) * groups + (x + sx) % groups
                mine = dst * groups + x
                pairs.append((mine, other) if back else (other, mine))
        return lax.ppermute(value, ("dp", "head"), pairs)

    others = [(sx, yf) for sx in range(groups) for yf in range(2) if sx or yf]

    def local(
        media_tokens,
        latents,
        cotangent,
        image_counts,
        media_gain,
        media_bias,
        latent_gain,
        latent_bias,
        ff_gain,
        ff_bias,
        w_query,
        w_keyval,
        w_attn_out,
        w_up,
        w_down,
    ):
        images, patches, width = media_tokens.shape
        lat = latents.shape[1]
        rows, cw = w_query.shape
        units = w_up.shape[1]
        patch, share = patches // groups, lat // groups
        step = patch + share
        heads_w = cw * groups
        me = lax.axis_index("head").astype(jnp.int32)
        place = lax.axis_index("dp").astype(jnp.int32)
        z, y, c = place // 4, place // 2 % 2, place % 2
        ids = jnp.stack([me, z, y, c])
        live = (jnp.arange(images, dtype=jnp.int32) < jnp.sum(image_counts)).astype(jnp.int32)
        gains = [
            g.reshape(1, width)
            for g in (media_gain, media_bias, latent_gain, latent_bias, ff_gain, ff_bias)
        ]
        media4 = media_tokens.reshape(images, groups, patch, width)
        lat4 = latents.reshape(images, groups, share, width)
        cot4 = cotangent.reshape(images, groups, share, width)

        shard_qk = jnp.concatenate([w_query, w_keyval[:, 0]], axis=1)
        shard_vo = jnp.concatenate([w_keyval[:, 1], w_attn_out.T], axis=1)
        got_qk = [from_dp(shard_qk, s) for s in range(1, depth_z)]
        shard_vo = tie(shard_vo, shard_qk)
        got_vo = [from_dp(shard_vo, s) for s in range(1, depth_z)]
        w_up_all = lax.all_gather(w_up, "dp", axis=0, tiled=True)
        w_down_all = lax.all_gather(w_down.T, "dp", axis=0, tiled=True)

        def spread_line(line):
            return {(0, 0): line} | {at: plane(line, *at, False) for at in others}

        def cores(parts):
            pieces, entries = [], []
            for (sx, yf), part in parts.items():
                for cf, piece in ((0, part), (1, from_dp(part, cf=1))):
                    for s in range(depth_z):
                        entries.append((len(pieces), s, sx, s, yf, cf))
                    pieces.append(piece)
            return entries, pieces

        line_qk = jnp.stack([shard_qk] + got_qk)
        parts_qk = spread_line(line_qk)
        imgs = 2
        src, nlat = call(
            functools.partial(norm_kernel, imgs, lat, share, patch),
            (images // imgs,),
            [
                pl.BlockSpec((imgs, None, patch, width), lambda i, ids: (i, ids[0], 0, 0)),
                images_of(imgs, lat, width),
            ]
            + [whole(gains[0])] * 4,
            [rows_of(imgs * step, width), rows_of(imgs * lat, width)],
            [struct((images * step, width), BF), struct((images * lat, width), BF)],
            [pltpu.VMEM((lat, width), F32)],
            tie(ids, line_qk),
            [media4, latents] + gains[:4],
            images * step * width * 12,
            "input_norms",
        )

        line_vo = jnp.stack([shard_vo] + tie(got_vo, line_qk))
        parts_vo = spread_line(line_vo)
        w_qk = assemble(*cores(parts_qk), depth_z, ids, rows, groups, 2 * cw, "place_qk")
        final4 = jnp.stack(
            [
                lax.dynamic_index_in_dim(cot4, (me + s) % groups, 1, keepdims=False)
                for s in range(groups)
            ]
        ) * live.astype(BF).reshape(1, images, 1, 1)
        final4 = final4.reshape(groups, images * share, width)

        imgs = 4
        attn_macs = images * step * lat * heads_w
        q, k, stats = call(
            functools.partial(project_kernel, groups, cw, imgs, step, lat),
            (images // imgs,),
            [rows_of(imgs * step, width), rows_of(imgs * lat, width), whole(w_qk)],
            [
                rows_of(imgs * lat, heads_w),
                rows_of(imgs * step, heads_w),
                images_of(imgs, 2, heads_w),
            ],
            [
                struct((images * lat, heads_w), BF),
                struct((images * step, heads_w), BF),
                struct((images, 2, heads_w), F32),
            ],
            [],
            ids,
            [src, nlat, w_qk],
            2 * images * (step * width * heads_w + lat * width * heads_w) + 8 * attn_macs,
            "project",
        )
        tops, sums = [stats[:, :1]], [stats[:, 1:]]
        for s in range(1, groups):
            other = jnp.roll(from_head(stats, s), s * cw, axis=2)
            tops.append(other[:, :1])
            sums.append(other[:, 1:])
        w_vo = assemble(*cores(parts_vo), depth_z, tie(ids, q), rows, groups, 2 * cw, "place_vo")
        v = call(
            functools.partial(values_kernel, groups, cw),
            (images // imgs,),
            [rows_of(imgs * step, width), third(w_vo, cw, 0)],
            [rows_of(imgs * step, heads_w)],
            [struct((images * step, heads_w), BF)],
            [],
            ids,
            [src, w_vo],
            2 * images * step * width * heads_w,
            "values",
        )[0]
        top = functools.reduce(jnp.maximum, tops)
        lse = top + jnp.log(sum(t * jnp.exp(m - top) for m, t in zip(tops, sums)))

        part = images // CHUNKS
        imgs = min(imgs, part)
        count = part // imgs
        own = part * share

        def attn_specs(ch):
            return [
                rows_of(imgs * lat, heads_w, ch * count),
                rows_of(imgs * step, heads_w, ch * count),
                rows_of(imgs * step, heads_w, ch * count),
                images_of(imgs, 1, heads_w, ch * count),
            ]

        row_sends = [
            rows_of(imgs * share, heads_w),
            pl.BlockSpec((groups - 1, imgs * share, heads_w), lambda i, ids: (0, i, 0)),
        ]
        row_outs = [struct((own, heads_w), F32), struct((groups - 1, own, heads_w), BF)]

        def exchanged(keep, send):
            return [keep] + [to_head(send[s - 1], s) for s in range(groups - 1, 0, -1)]

        mixes, mixed, middle, normed = [], [], [], []
        for ch in range(CHUNKS):
            keep, send = call(
                functools.partial(mix_kernel, groups, cw, imgs, step, lat, share),
                (count,),
                attn_specs(ch),
                row_sends,
                row_outs,
                [pltpu.VMEM((imgs, lat, heads_w), F32)],
                tie(ids, [a[0] for a in mixes]),
                [q, k, v, lse],
                8 * attn_macs / CHUNKS,
                f"mix{ch}",
            )
            mixes.append(exchanged(keep, send))
        for ch in range(CHUNKS):
            lat_spec = pl.BlockSpec(
                (part, None, share, width), lambda i, ids, ch=ch: (ch, ids[0], 0, 0)
            )
            outs = call(
                functools.partial(middle_kernel, groups, cw),
                (1,),
                [whole(a) for a in mixes[ch]]
                + [lat_spec, third(w_vo, cw, 1), whole(gains[4]), whole(gains[5])],
                [fixed_rows(own, heads_w), fixed_rows(own, width), fixed_rows(own, width)],
                [struct((own, heads_w), BF), struct((own, width), F32), struct((own, width), BF)],
                [],
                tie(ids, [a[0] for a in normed]),
                mixes[ch] + [lat4, w_vo, gains[4], gains[5]],
                2 * own * heads_w * width,
                f"middle{ch}",
            )
            mixed.append(outs[0])
            middle.append(outs[1])
            normed.append([outs[2]] + [from_head(outs[2], s) for s in range(1, groups)])
        block = min(512, units)

        def feed_forward(terms, ids, name):
            size = len(terms) * own
            return call(
                functools.partial(forward_kernel, len(terms)),
                (units // block,),
                [whole(a) for a, _ in terms]
                + [spec for _, spec in terms]
                + [
                    pl.BlockSpec((width, block), lambda i, ids: (0, i)),
                    pl.BlockSpec((width, block), lambda i, ids: (0, i)),
                ],
                [pl.BlockSpec((size, block), lambda i, ids: (0, i))] * 2
                + [fixed_rows(size, width)] * 2,
                [struct((size, units), BF)] * 2 + [struct((size, width), BF)] * 2,
                [pltpu.VMEM((size, width), BF)] * 2 + [pltpu.VMEM((size, width), F32)] * 2,
                ids,
                [a for a, _ in terms] + [final4] * len(terms) + [w_up_all, w_down_all],
                8 * size * width * units,
                name,
            )

        def final_rows(s, ch):
            return pl.BlockSpec((None, own, width), lambda *_: (s, ch, 0))

        own_ff = feed_forward(
            [(normed[ch][0], final_rows(0, ch)) for ch in range(CHUNKS)],
            tie(ids, normed[-1][0]),
            "feed_forward_own",
        )
        away_ff, ff_back, mid_back = [], [], []
        for ch in range(CHUNKS):
            outs = feed_forward(
                [(normed[ch][s], final_rows(s, ch)) for s in range(1, groups)],
                tie(ids, (away_ff or [own_ff])[-1]),
                f"feed_forward_away{ch}",
            )
            away_ff.append(outs[:2])
            sends = [a.reshape(groups - 1, own, width) for a in outs[2:]]
            mid_back.append(
                [to_head(sends[1][s - 1], s) for s in range(groups - 1, 0, -1)]
            )
            ff_back.append(sends[0])

        def ff_terms(lefts, which):
            rights = [(own_ff[which], CHUNKS * own, 0)]
            rights += [(a[which], (groups - 1) * own, 0) for a in away_ff]
            return [(lefts, rights)]

        finals = [(final4, pl.BlockSpec((None, CHUNKS * own, width), lambda *_: (0, 0, 0)))]
        finals += [(final4, final_rows(s, ch)) for ch in range(CHUNKS) for s in range(1, groups)]
        norms = [normed[ch][0] for ch in range(CHUNKS)]
        norms += [normed[ch][s] for ch in range(CHUNKS) for s in range(1, groups)]
        norms = [(a, whole(a)) for a in norms]
        down_part = weight_grad(
            tie(ids, away_ff), ff_terms(finals, 0), rows, width, block, "grad_down", False
        )[0]
        up_part = weight_grad(
            tie(ids, down_part), ff_terms(norms, 1), rows, width, block, "grad_up", False
        )[0]
        grad_down = lax.psum_scatter(down_part, "dp", scatter_dimension=0, tiled=True)
        grad_up = lax.psum_scatter(up_part, "dp", scatter_dimension=0, tiled=True)
        ff_back = tie(ff_back, mid_back)
        ff_back = [[to_head(a[s - 1], s) for s in range(groups - 1, 0, -1)] for a in ff_back]

        def pick(block, index, axis=0):
            return lax.dynamic_index_in_dim(block, index, axis, keepdims=False).astype(F32)

        def lanes(block, cols):
            if len(cols) == 1 and cols[0] == slice(0, block.shape[-1]):
                return block
            return jnp.concatenate([block[..., c] for c in cols], axis=-1)

        class Sum:
            def __init__(self, parts, cols):
                self.cols = cols
                self.routes = others
                self.grid = [a.reshape((depth_z, 2) + a.shape[1:]) for a in (parts[0], from_dp(parts[1], cf=1))]

            def at(self, sx, yy):
                return sum(pick(lanes(a, self.cols[sx]), yy, 1) for a in self.grid)

            def second(self):
                self.away = [self.at(sx, y ^ yf).astype(BF) for sx, yf in self.routes]
                return self.away

            def sent(self):
                self.near = [plane(a, *to, True) for a, to in zip(self.away, self.routes)]

            def third(self):
                base = self.at(0, y)

                def block(zz):
                    return pick(base, zz) + sum(pick(a, zz) for a in self.near)

                self.mine = block
                self.away = [block((z + s) % depth_z).astype(BF) for s in range(1, depth_z)]
                return self.away

            def last(self, late=()):
                got = [from_dp(a, depth_z - s) for s, a in zip(range(1, depth_z), self.away)]
                got = tie(got, late)
                return self.mine(z) + sum(a.astype(F32) for a in got)

        def groups_of(*starts):
            return [[slice(a + sx * cw, a + (sx + 1) * cw) for a in starts] for sx in range(groups)]

        grad_mid, mid_low, gain_terms, grad_mixed = [], [], [], []
        for ch in range(CHUNKS):
            outs = call(
                functools.partial(middle_back_kernel, groups, cw),
                (1,),
                [fixed_rows(own, width, ch)]
                + [whole(t) for t in mid_back[ch]]
                + [whole(middle[ch]), final_rows(0, ch), third(w_vo, cw, 1), whole(gains[4])],
                [
                    fixed_rows(own, width),
                    fixed_rows(own, width),
                    fixed_rows(own, heads_w),
                    fixed_rows(2, width),
                ],
                [
                    struct((own, width), F32),
                    struct((own, width), BF),
                    struct((own, heads_w), BF),
                    struct((2, width), F32),
                ],
                [],
                tie(ids, up_part, mid_low),
                [own_ff[3]] + mid_back[ch] + [middle[ch], final4, w_vo, gains[4]],
                2 * own * heads_w * width,
                f"middle_back{ch}",
            )
            grad_mid.append(outs[0])
            mid_low.append(outs[1])
            grad_mixed.append([outs[2]] + [from_head(outs[2], s) for s in range(1, groups)])
            gain_terms.append(outs[3])
        whole_of = lambda arrays: [(a, whole(a)) for a in arrays]
        full_of = lambda arrays: [(a, a.shape[0], 0) for a in arrays]
        out_parts = weight_grad(
            tie(ids, mid_low), [(whole_of(mid_low), full_of(mixed))], rows, width, heads_w, "grad_attn_out"
        )
        sum_out = Sum(out_parts, groups_of(0))

        grad_all, delta, gv = [], [], None
        for ch in range(CHUNKS):
            first = gv is None
            before = [out_parts[0]] if first else sum_out.second()
            outs = call(
                functools.partial(back_probs_kernel, groups, cw, imgs, step, lat, share, first),
                (count,),
                attn_specs(ch)
                + [rows_of(imgs * share, heads_w)] * groups
                + ([] if first else [anywhere()]),
                [
                    rows_of(imgs * step, heads_w, ch * count),
                    rows_of(imgs * lat, heads_w),
                    images_of(imgs, 1, heads_w),
                ],
                [
                    struct((images * step, heads_w), BF),
                    struct((part * lat, heads_w), BF),
                    struct((part, 1, heads_w), F32),
                ],
                [pltpu.VMEM((imgs, lat, heads_w), F32)],
                tie(ids, before),
                [q, k, v, lse] + grad_mixed[ch] + ([] if first else [gv]),
                12 * attn_macs / CHUNKS,
                f"back_probs{ch}",
                None if first else {4 + groups: 0},
            )
            gv = outs[0]
            grad_all.append(outs[1])
            delta.append([outs[2]] + [from_head(outs[2], s) for s in range(1, groups)])
        sum_out.sent()
        source = lambda block: [(src, whole(src))]
        value_parts = weight_grad(
            tie(ids, gv), [(source(src), [(gv, images * step, 0)])], rows, width, heads_w, "grad_values"
        )
        sum_value = Sum(value_parts, groups_of(0))
        gk = gq = None
        query_terms = []
        for ch in range(CHUNKS):
            first = gk is None
            total = sum(jnp.roll(a, s * cw, axis=2) for s, a in enumerate(delta[ch]))
            before = [value_parts[0]] if first else [gk, sum_value.second()]
            outs = call(
                functools.partial(back_scores_kernel, groups, cw, imgs, step, lat, share, first),
                (count,),
                attn_specs(ch)
                + [rows_of(imgs * lat, heads_w), images_of(imgs, 1, heads_w)]
                + ([] if first else [anywhere()] * 2),
                [
                    rows_of(imgs * step, heads_w, ch * count),
                    rows_of(imgs * lat, heads_w, ch * count),
                ]
                + row_sends,
                [struct((images * step, heads_w), BF), struct((images * lat, heads_w), BF)]
                + row_outs,
                [pltpu.VMEM((imgs, lat, heads_w), F32)],
                tie(ids, before),
                [q, k, v, lse, grad_all[ch], total] + ([] if first else [gk, gq]),
                16 * attn_macs / CHUNKS,
                f"back_scores{ch}",
                None if first else {6: 0, 7: 1},
            )
            gk, gq = outs[:2]
            query_terms.append(exchanged(*outs[2:]))
        sum_value.sent()
        key_parts = weight_grad(
            tie(ids, gk, sum_out.third()),
            [
                (source(src), [(gk, images * step, 0)]),
                ([(nlat, whole(nlat))], [(gq, images * lat, 0)]),
            ],
            rows,
            width,
            heads_w,
            "grad_query_keys",
        )
        sum_key = Sum(key_parts, groups_of(0, heads_w))

        ff_back = tie(ff_back, key_parts[0])
        final_lat = [mid + sum(t.astype(F32) for t in terms) for mid, terms in zip(middle, ff_back)]
        final_lat = jnp.concatenate(final_lat) + own_ff[2].astype(F32)
        final_lat = final_lat.reshape(images, share, width)
        lat_own = lax.dynamic_index_in_dim(lat4, me, 1, keepdims=False).astype(F32)
        latents_out = jnp.where(live[:, None, None] > 0, final_lat, lat_own)

        media_grad = latent_grad = None
        imgs = min(4, part)
        count = part // imgs
        for ch in range(CHUNKS):
            first = media_grad is None

            def share_rows(size, ch=ch):
                return pl.BlockSpec(
                    (imgs, None, size, width), lambda i, ids, live: (i + ch * count, ids[0], 0, 0)
                )

            before = [sum_key.second(), latents_out, sum_value.third()] if first else [media_grad]
            outs = call(
                functools.partial(
                    source_back_kernel, groups, cw, imgs, patch, share, ch * count
                ),
                (count,),
                [rows_of(imgs * step, heads_w, ch * count)] * 2
                + [whole(w_qk), third(w_vo, cw, 0)]
                + [share_rows(patch), share_rows(share), share_rows(share)]
                + [rows_of(imgs * share, heads_w)] * groups
                + [rows_of(imgs * share, width), whole(gains[0]), whole(gains[2])]
                + ([] if first else [anywhere()] * 2),
                [
                    images_of(imgs, patch, width, ch * count),
                    images_of(imgs, share, width, ch * count),
                    fixed_rows(4, width),
                ],
                [
                    struct((images, patch, width), F32),
                    struct((images, share, width), F32),
                    struct((4, width), F32),
                ],
                [
                    pltpu.VMEM((imgs * step, width), F32),
                    pltpu.VMEM((imgs * share, width), F32),
                    pltpu.VMEM((imgs * share, heads_w), BF),
                ],
                [tie(ids, before), live],
                [gk, gv, w_qk, w_vo, media4, lat4, cot4]
                + query_terms[ch]
                + [grad_mid[ch], gains[0], gains[2]]
                + ([] if first else [media_grad, latent_grad]),
                2 * part * step * width * 2 * heads_w,
                f"source_back{ch}",
                None if first else {10 + groups: 0, 11 + groups: 1},
            )
            media_grad, latent_grad = outs[:2]
            gain_terms[ch] = jnp.concatenate([outs[2], gain_terms[ch]])
            if first:
                sum_key.sent()
        sum_key.third()
        query_key = sum_key.last()
        grad_value = sum_value.last(media_grad)
        grad_attn = sum_out.last(media_grad)

        total = sum(gain_terms)
        near = [from_dp(total, cf=1)] + [plane(total, *at, False) for at in others]
        near += [plane(total, *at, False, 1) for at in others]
        total = total + sum(near)
        norm_grads = total + sum(from_dp(total, s) for s in range(1, depth_z))

        return (
            latents_out,
            media_grad,
            latent_grad,
            query_key[:, cw:],
            jnp.stack([query_key[:, :cw], grad_value], axis=1),
            grad_attn.T,
            grad_up.astype(F32),
            grad_down.T.astype(F32),
            norm_grads,
        )

    return local


def solution(mesh):
    return jax.shard_map(
        make_local(mesh.shape["dp"] // 4, mesh.shape["head"]),
        mesh=mesh,
        in_specs=(
            P("dp", None, None),
            P("dp", None, None),
            P("dp", None, None),
            P("dp"),
            P(),
            P(),
            P(),
            P(),
            P(),
            P(),
            P("dp", "head"),
            P("dp", None, "head"),
            P("head", "dp"),
            P("dp", "head"),
            P("head", "dp"),
        ),
        out_specs=(
            P("dp", "head", None),
            P("dp", "head", None),
            P("dp", "head", None),
            P("dp", "head"),
            P("dp", None, "head"),
            P("head", "dp"),
            P("dp", "head"),
            P("head", "dp"),
            P(),
        ),
        check_vma=False,
    )
```

time: 451 us -> 384 us (0.85)
  waiting for transfers between devices: 108 us -> 56 us
  Pallas kernels: 160 us -> 201 us
  local copies, waits for them, and re-layouts: 52.2 us -> 14.8 us
  starting transfers between devices: 92.9 us -> 74.8 us
  other arithmetic: 31.6 us -> 18.5 us
  between operations: 2.27 us -> 14.7 us
    pallas_call x21 -> x25, Pallas kernels: 134 us -> 201 us  [call(): pl.pallas_call(kernel, grid_spec=pltpu.PrefetchScalarGridSpec(num_scalar_...]
    ppermute x48 -> x30, waiting for transfers between devices: 45.5 us -> 11.7 us  [from_dp(): return lax.ppermute(value, 'dp', pairs)]
    ppermute x48 -> x30, starting transfers between devices: 63.3 us -> 31.6 us  [from_dp(): return lax.ppermute(value, 'dp', pairs)]
    pallas_call x2 -> x0, Pallas kernels: 25.9 us -> none  [local(): pl.pallas_call(functools.partial(source_back_kernel, groups, cw, imgs, pa...]
    unnamed x156 -> x87, local copies, waits for them, and re-layouts: 26.9 us -> 11.2 us
    slice x17 -> x9, local copies, waits for them, and re-layouts: 17.2 us -> 2.47 us  [the longest x6 1.43 us: lanes(): return jnp.concatenate([block[..., c] for c in cols], axis=-1)]
    ppermute x15 -> x21, starting transfers between devices: 13.8 us -> 27.8 us  [plane(): return lax.ppermute(value, ('dp', 'head'), pairs)]
    ppermute x8, waiting for transfers between devices: 19.9 us -> 6.37 us  [to_head(): lax.ppermute(value, 'head', [(x, (x + s) % groups) for x in range(groups)])]
  transfers between devices with their start and end apart: 78 -> 70, of which waited for: 25 -> 19; matrix products, arithmetic and copies ran while one was open for 12% -> 6% of each run, Pallas kernels for 33% -> 48%
where the time goes in v2:
time: 384 us; the launch traced here: 379 us
  Pallas kernels  201 us (52%)
  starting transfers between devices  74.8 us (19%)
  waiting for transfers between devices  56 us (15%)
  other arithmetic  18.5 us (5%)
  local copies, waits for them, and re-layouts  14.8 us (4%)
  between operations  14.7 us (4%)
    pallas_call x25, Pallas kernels, call(): pl.pallas_call(kernel, grid_spec=pltpu.PrefetchScalarGridSpec(num_scalar_...  201 us
    ppermute x21, waiting for transfers between devices, plane(): return lax.ppermute(value, ('dp', 'head'), pairs)  33.3 us
    ppermute x30, starting transfers between devices, from_dp(): return lax.ppermute(value, 'dp', pairs)  31.6 us
    ppermute x21, starting transfers between devices, plane(): return lax.ppermute(value, ('dp', 'head'), pairs)  27.8 us
    ppermute x30, waiting for transfers between devices, from_dp(): return lax.ppermute(value, 'dp', pairs)  11.7 us
    unnamed x87, local copies, waits for them, and re-layouts  11.2 us
    ppermute x8, starting transfers between devices, to_head(): lax.ppermute(value, 'head', [(x, (x + s) % groups) for x in range(groups)])  7.78 us
  transfers between devices with their start and end apart: 70, of which 19 were waited for; matrix products, arithmetic and copies ran while one was open for 6% of the time, Pallas kernels for 48%

profile of v2, /device:TPU:0, one launch (start us, length us, event | category | flops | bytes accessed | tf_op | source)
XLA Modules:
  0.0 379.4 jit_solution(14323541607167588279)
XLA Ops:
  10.5 3.1 collective-permute-start.2
  13.6 2.6 collective-permute-start.1
  19.3 2.8 collective-permute-start.10
  22.2 2.5 collective-permute-done.12
  24.7 3.8 collective-permute-done.11
  28.6 3.4 collective-permute-start.18
  34.1 1.9 collective-permute-start.4
  36.0 3.2 collective-permute-done.18.refs_6_
  39.2 2.1 collective-permute-start.14
  41.3 4.1 %collective-permute-done.16.refs_4_ = bf16[4,64,512]{2,1,0:T(8,128)(2,1)S(1)} collective-permute-done((bf16[4,64,512]{2,1,0:T(8,128)(2,1)S(1)}, bf16[4,64,512]{2,1,0:T(8,128)(2,1)S(1)}, u32[]{:S(2)}, u32[]{:S(2)}) %collective-permute-start.16) | collective-permute-done | bytes 262176 | tf_op jit(solution)/shard_map/ppermute | solution.py:510
  45.4 5.0 %collective-permute-done.8.refs_6_ = bf16[4,64,512]{2,1,0:T(8,128)(2,1)S(1)} collective-permute-done((bf16[4,64,512]{2,1,0:T(8,128)(2,1)S(1)}, bf16[4,64,512]{2,1,0:T(8,128)(2,1)S(1)}, u32[]{:S(2)}, u32[]{:S(2)}) %collective-permute-start.8) | collective-permute-done | bytes 262176 | tf_op jit(solution)/shard_map/ppermute | solution.py:510
  50.5 2.3 collective-permute-done.6.refs_4_
  53.3 8.1 %collective-permute-done.14.refs_2_ = bf16[4,64,512]{2,1,0:T(8,128)(2,1)S(1)} collective-permute-done((bf16[4,64,512]{2,1,0:T(8,128)(2,1)S(1)}, bf16[4,64,512]{2,1,0:T(8,128)(2,1)S(1)}, u32[]{:S(2)}, u32[]{:S(2)}) %collective-permute-start.14) | collective-permute-done | bytes 262176 | tf_op jit(solution)/shard_map/ppermute | solution.py:510
  63.7 10.0 %input_norms.1 = (bf16[2560,1024]{1,0:T(8,128)(2,1)}, bf16[1024,1024]{1,0:T(8,128)(2,1)}) custom-call(s32[4]{0:T(128)} %pad_add_fusion.ids.ids_ref, bf16[16,2,128,1024]{3,2,1,0:T(8,128)(2,1)} %bitcast.214, bf16[16,64,1024]{2,1,0:T(8,128)(2,1)} %latents.1, f32[1,1024]{1,0:T(1,128)} %bitcast.246, f32[1,1024]{1,0:T(1,128)} %bitcast.255, f32[1,1024]{1,0:T(1,128)} %bitcast.249, ...), custom_call_target="tpu_custom_call" | custom-call | flops 629145 | bytes 189071 | tf_op jit(solution)/shard_map/input_norms/pallas_call | solution.py:38
  73.8 4.0 %place_qk.1.w.wk = bf16[2,1024,512]{2,1,0:T(8,128)(2,1)} custom-call(s32[4]{0:T(128)} %pad_add_fusion.ids.ids_ref, bf16[4,64,512]{2,1,0:T(8,128)(2,1)} %copy-done.8, bf16[4,64,512]{2,1,0:T(8,128)(2,1)} %copy-done.23, bf16[4,64,512]{2,1,0:T(8,128)(2,1)} %copy-done.21, bf16[4,64,512]{2,1,0:T(8,128)(2,1)} %collective-permute-done.5.refs_3_, ...), custom_call_target="tpu_custom_call" | custom-call | bytes 83886 | tf_op jit(solution)/shard_map/place_qk/pallas_call | solution.py:38
  77.8 9.8 %project.1 = (bf16[1024,512]{1,0:T(8,128)(2,1)}, bf16[2560,512]{1,0:T(8,128)(2,1)}, f32[16,2,512]{2,1,0:T(2,128)}) custom-call(s32[4]{0:T(128)} %pad_add_fusion.ids.ids_ref, bf16[2560,1024]{1,0:T(8,128)(2,1)} %get-tuple-element.108.src.refs_0_, bf16[1024,1024]{1,0:T(8,128)(2,1)} %get-tuple-element.109.nlat.refs_2_, bf16[2,1024,512]{2,1,0:T(8,128)(2,1)} %place_qk.1.w.wk), custom_call_target="tpu_custom_call" | custom-call | flops 88583696 | bytes 263454 | tf_op jit(solution)/shard_map/project/pallas_call | solution.py:38
  87.6 1.4 collective-permute-start.20
  89.8 3.9 %place_vo.1.w.refs_2_.refs_3_.wv = bf16[2,1024,512]{2,1,0:T(8,128)(2,1)} custom-call(s32[4]{0:T(128)} %pad_add_fusion.ids.ids_ref, bf16[4,64,512]{2,1,0:T(8,128)(2,1)} %copy-done.7, bf16[4,64,512]{2,1,0:T(8,128)(2,1)} %copy-done.22, bf16[4,64,512]{2,1,0:T(8,128)(2,1)} %copy-done.17, bf16[4,64,512]{2,1,0:T(8,128)(2,1)} %collective-permute-done.15.refs_3_, ...), custom_call_target="tpu_custom_call" | custom-call | bytes 83886 | tf_op jit(solution)/shard_map/place_vo/pallas_call | solution.py:38
  93.8 7.5 %values.1.v = bf16[2560,512]{1,0:T(8,128)(2,1)} custom-call(s32[4]{0:T(128)} %pad_add_fusion.ids.ids_ref, bf16[2560,1024]{1,0:T(8,128)(2,1)} %get-tuple-element.108.src.refs_0_, bf16[2,1024,512]{2,1,0:T(8,128)(2,1)} %place_vo.1.w.refs_2_.refs_3_.wv), custom_call_target="tpu_custom_call" | custom-call | flops 53687092 | bytes 199229 | tf_op jit(solution)/shard_map/values/pallas_call | solution.py:38
  102.1 5.3 %mix0.1 = (f32[256,512]{1,0:T(8,128)}, bf16[1,256,512]{2,1,0:T(8,128)(2,1)}) custom-call(s32[4]{0:T(128)} %pad_add_fusion.ids.ids_ref, bf16[1024,512]{1,0:T(8,128)(2,1)} %get-tuple-element.110.q, bf16[2560,512]{1,0:T(8,128)(2,1)} %get-tuple-element.111.k, bf16[2560,512]{1,0:T(8,128)(2,1)} %values.1.v, f32[16,1,512]{2,1,0:T(1,128)} %log_add_fusion.lse), custom_call_target="tpu_custom_call" | custom-call | flops 6710886 | bytes 142213 | tf_op jit(solution)/shard_map/mix0/pallas_call | solution.py:38
  108.1 5.5 %mix1.1 = (f32[256,512]{1,0:T(8,128)}, bf16[1,256,512]{2,1,0:T(8,128)(2,1)}) custom-call(s32[4]{0:T(128)} %pad_add_fusion.ids.ids_ref, bf16[1024,512]{1,0:T(8,128)(2,1)} %get-tuple-element.110.q, bf16[2560,512]{1,0:T(8,128)(2,1)} %get-tuple-element.111.k, bf16[2560,512]{1,0:T(8,128)(2,1)} %values.1.v, f32[16,1,512]{2,1,0:T(1,128)} %log_add_fusion.lse), custom_call_target="tpu_custom_call" | custom-call | flops 6710886 | bytes 142213 | tf_op jit(solution)/shard_map/mix1/pallas_call | solution.py:38
  113.6 1.4 collective-permute-start.22
  116.4 4.0 %middle0.1 = (bf16[256,512]{1,0:T(8,128)(2,1)}, f32[256,1024]{1,0:T(8,128)}, bf16[256,1024]{1,0:T(8,128)(2,1)}) custom-call(s32[4]{0:T(128)} %pad_add_fusion.ids.ids_ref, f32[256,512]{1,0:T(8,128)} %get-tuple-element.118.keep, bf16[256,512]{1,0:T(8,128)(2,1)} %copy-done.30, bf16[16,2,32,1024]{3,2,1,0:T(8,128)(2,1)} %bitcast.217, ...), custom_call_target="tpu_custom_call" | custom-call | flops 5368709 | bytes 94535 | tf_op jit(solution)/shard_map/middle0/pallas_call | solution.py:38
  122.2 4.0 %middle1.1 = (bf16[256,512]{1,0:T(8,128)(2,1)}, f32[256,1024]{1,0:T(8,128)}, bf16[256,1024]{1,0:T(8,128)(2,1)}) custom-call(s32[4]{0:T(128)} %pad_add_fusion.ids.ids_ref, f32[256,512]{1,0:T(8,128)} %get-tuple-element.124.keep, bf16[256,512]{1,0:T(8,128)(2,1)} %copy-done.29, bf16[16,2,32,1024]{3,2,1,0:T(8,128)(2,1)} %bitcast.218, ...), custom_call_target="tpu_custom_call" | custom-call | flops 5368709 | bytes 94535 | tf_op jit(solution)/shard_map/middle1/pallas_call | solution.py:38
  126.3 1.4 collective-permute-start.24
  128.7 1.6 maximum_multiply_fusion.refs_2_.refs_3_.refs_1_.refs_0_
  130.3 16.2 %feed_forward_own.1 = (bf16[512,2048]{1,0:T(8,128)(2,1)}, bf16[512,2048]{1,0:T(8,128)(2,1)}, bf16[512,1024]{1,0:T(8,128)(2,1)}, bf16[512,1024]{1,0:T(8,128)(2,1)}) custom-call(s32[4]{0:T(128)} %pad_add_fusion.ids.ids_ref, bf16[256,1024]{1,0:T(8,128)(2,1)} %get-tuple-element.121.refs_0_, bf16[256,1024]{1,0:T(8,128)(2,1)} %get-tuple-element.126.refs_1_, ...), custom_call_target="tpu_custom_call" | custom-call | flops 171798688 | bytes 398458 | tf_op jit(solution)/shard_map/feed_forward_own/pallas_call | solution.py:38
  147.3 11.0 %feed_forward_away0.1 = (bf16[256,2048]{1,0:T(8,128)(2,1)}, bf16[256,2048]{1,0:T(8,128)(2,1)}, bf16[256,1024]{1,0:T(8,128)(2,1)}, bf16[256,1024]{1,0:T(8,128)(2,1)}) custom-call(s32[4]{0:T(128)} %pad_add_fusion.ids.ids_ref, bf16[256,1024]{1,0:T(8,128)(2,1)} %copy-done.4, bf16[2,512,1024]{2,1,0:T(8,128)(2,1)} %maximum_multiply_fusion.refs_2_.refs_3_.refs_1_.refs_0_, ...), custom_call_target="tpu_custom_call" | custom-call | flops 85899344 | bytes 283115 | tf_op jit(solution)/shard_map/feed_forward_away0/pallas_call | solution.py:38
  159.1 10.5 %feed_forward_away1.1 = (bf16[256,2048]{1,0:T(8,128)(2,1)}, bf16[256,2048]{1,0:T(8,128)(2,1)}, bf16[256,1024]{1,0:T(8,128)(2,1)}, bf16[256,1024]{1,0:T(8,128)(2,1)}) custom-call(s32[4]{0:T(128)} %pad_add_fusion.ids.ids_ref, bf16[256,1024]{1,0:T(8,128)(2,1)} %copy-done.5, bf16[2,512,1024]{2,1,0:T(8,128)(2,1)} %maximum_multiply_fusion.refs_2_.refs_3_.refs_1_.refs_0_, ...), custom_call_target="tpu_custom_call" | custom-call | flops 85899344 | bytes 283115 | tf_op jit(solution)/shard_map/feed_forward_away1/pallas_call | solution.py:38
  169.6 9.7 %grad_down.1 = bf16[1024,2048]{1,0:T(8,128)(2,1)} custom-call(s32[4]{0:T(128)} %pad_add_fusion.ids.ids_ref, bf16[2,512,1024]{2,1,0:T(8,128)(2,1)} %maximum_multiply_fusion.refs_2_.refs_3_.refs_1_.refs_0_, bf16[2,512,1024]{2,1,0:T(8,128)(2,1)} %maximum_multiply_fusion.refs_2_.refs_3_.refs_1_.refs_0_, ...), custom_call_target="tpu_custom_call" | custom-call | flops 85899344 | bytes 293601 | tf_op jit(solution)/shard_map/grad_down/pallas_call | solution.py:38
  182.4 9.8 %grad_up.1 = bf16[1024,2048]{1,0:T(8,128)(2,1)} custom-call(s32[4]{0:T(128)} %pad_add_fusion.ids.ids_ref, bf16[256,1024]{1,0:T(8,128)(2,1)} %get-tuple-element.121.refs_0_, bf16[256,1024]{1,0:T(8,128)(2,1)} %get-tuple-element.126.refs_1_, bf16[256,1024]{1,0:T(8,128)(2,1)} %copy-done.4, bf16[256,1024]{1,0:T(8,128)(2,1)} %copy-done.5, ...), custom_call_target="tpu_custom_call" | custom-call | flops 85899344 | bytes 209715 | tf_op jit(solution)/shard_map/grad_up/pallas_call | solution.py:38
  192.3 3.0 collective-permute-done.25.refs_0_
  196.0 5.1 %middle_back0.1 = (f32[256,1024]{1,0:T(8,128)}, bf16[256,1024]{1,0:T(8,128)(2,1)}, bf16[256,512]{1,0:T(8,128)(2,1)}, f32[2,1024]{1,0:T(2,128)}) custom-call(s32[4]{0:T(128)} %pad_add_fusion.ids.ids_ref, bf16[512,1024]{1,0:T(8,128)(2,1)} %get-tuple-element.131.part, bf16[256,1024]{1,0:T(8,128)(2,1)} %copy-done.11, f32[256,1024]{1,0:T(8,128)} %get-tuple-element.120.refs_1_, ...), custom_call_target="tpu_custom_call" | custom-call | flops 5368709 | bytes 173260 | tf_op jit(solution)/shard_map/middle_back0/pallas_call | solution.py:38
  203.7 2.8 collective-permute-done.26.refs_0_
  207.3 4.9 %middle_back1.1 = (f32[256,1024]{1,0:T(8,128)}, bf16[256,1024]{1,0:T(8,128)(2,1)}, bf16[256,512]{1,0:T(8,128)(2,1)}, f32[2,1024]{1,0:T(2,128)}) custom-call(s32[4]{0:T(128)} %pad_add_fusion.ids.ids_ref, bf16[512,1024]{1,0:T(8,128)(2,1)} %get-tuple-element.131.part, bf16[256,1024]{1,0:T(8,128)(2,1)} %copy-done.10, f32[256,1024]{1,0:T(8,128)} %get-tuple-element.149.refs_1_, ...), custom_call_target="tpu_custom_call" | custom-call | flops 5368709 | bytes 173260 | tf_op jit(solution)/shard_map/middle_back1/pallas_call | solution.py:38
  212.2 4.0 %grad_attn_out.1 = (bf16[8,64,512]{2,1,0:T(8,128)(2,1)}, bf16[8,64,512]{2,1,0:T(8,128)(2,1)}) custom-call(s32[4]{0:T(128)} %pad_add_fusion.ids.ids_ref, bf16[256,1024]{1,0:T(8,128)(2,1)} %get-tuple-element.147.refs_0_, bf16[256,1024]{1,0:T(8,128)(2,1)} %get-tuple-element.150.refs_1_, bf16[256,512]{1,0:T(8,128)(2,1)} %get-tuple-element.152.refs_2_, ...), custom_call_target="tpu_custom_call" | custom-call | flops 10737418 | bytes 52428 | tf_op jit(solution)/shard_map/grad_attn_out/pallas_call | solution.py:38
  216.2 1.4 collective-permute-start.30
  218.2 5.7 %back_probs0.1 = (bf16[2560,512]{1,0:T(8,128)(2,1)}, bf16[512,512]{1,0:T(8,128)(2,1)}, f32[8,1,512]{2,1,0:T(1,128)}) custom-call(s32[4]{0:T(128)} %pad_add_fusion.ids.ids_ref, bf16[1024,512]{1,0:T(8,128)(2,1)} %get-tuple-element.110.q, bf16[2560,512]{1,0:T(8,128)(2,1)} %get-tuple-element.111.k, bf16[2560,512]{1,0:T(8,128)(2,1)} %values.1.v, ...), custom_call_target="tpu_custom_call" | custom-call | flops 10066329 | bytes 200212 | tf_op jit(solution)/shard_map/back_probs0/pallas_call | solution.py:38
  224.7 3.2 collective-permute-done.32
  229.4 2.2 collective-permute-start.35
  233.9 5.6 %back_probs1.1 = (bf16[2560,512]{1,0:T(8,128)(2,1)}, bf16[512,512]{1,0:T(8,128)(2,1)}, f32[8,1,512]{2,1,0:T(1,128)}) custom-call(s32[4]{0:T(128)} %pad_add_fusion.ids.ids_ref, bf16[1024,512]{1,0:T(8,128)(2,1)} %get-tuple-element.110.q, bf16[2560,512]{1,0:T(8,128)(2,1)} %get-tuple-element.111.k, ...), custom_call_target="tpu_custom_call", output_to_operand_aliasing={{0}: (7, {})} | custom-call | flops 10066329 | bytes 252641 | tf_op jit(solution)/shard_map/back_probs1/pallas_call | solution.py:38
  240.9 7.9 %grad_values.1 = (bf16[8,64,512]{2,1,0:T(8,128)(2,1)}, bf16[8,64,512]{2,1,0:T(8,128)(2,1)}) custom-call(s32[4]{0:T(128)} %pad_add_fusion.ids.ids_ref, bf16[2560,1024]{1,0:T(8,128)(2,1)} %get-tuple-element.108.src.refs_0_, bf16[2560,512]{1,0:T(8,128)(2,1)} %get-tuple-element.161.refs_1_.gv), custom_call_target="tpu_custom_call" | custom-call | flops 53687092 | bytes 178257 | tf_op jit(solution)/shard_map/grad_values/pallas_call | solution.py:38
  249.9 8.8 %back_scores0.1 = (bf16[2560,512]{1,0:T(8,128)(2,1)}, bf16[1024,512]{1,0:T(8,128)(2,1)}, f32[256,512]{1,0:T(8,128)}, bf16[1,256,512]{2,1,0:T(8,128)(2,1)}) custom-call(s32[4]{0:T(128)} %pad_add_fusion.ids.ids_ref, bf16[1024,512]{1,0:T(8,128)(2,1)} %get-tuple-element.110.q, bf16[2560,512]{1,0:T(8,128)(2,1)} %get-tuple-element.111.k, ...), custom_call_target="tpu_custom_call" | custom-call | flops 13421772 | bytes 226426 | tf_op jit(solution)/shard_map/back_scores0/pallas_call | solution.py:38
  261.7 1.6 collective-permute-start.39
  264.3 8.5 %back_scores1.1 = (bf16[2560,512]{1,0:T(8,128)(2,1)}, bf16[1024,512]{1,0:T(8,128)(2,1)}, f32[256,512]{1,0:T(8,128)}, bf16[1,256,512]{2,1,0:T(8,128)(2,1)}) custom-call(s32[4]{0:T(128)} %pad_add_fusion.ids.ids_ref, bf16[1024,512]{1,0:T(8,128)(2,1)} %get-tuple-element.110.q, ...), custom_call_target="tpu_custom_call", output_to_operand_aliasing={{0}: (7, {}), {1}: (8, {})} | custom-call | flops 13421772 | bytes 299827 | tf_op jit(solution)/shard_map/back_scores1/pallas_call | solution.py:38
  272.8 12.9 %grad_query_keys.1 = (bf16[8,64,1024]{2,1,0:T(8,128)(2,1)}, bf16[8,64,1024]{2,1,0:T(8,128)(2,1)}) custom-call(s32[4]{0:T(128)} %pad_add_fusion.ids.ids_ref, bf16[2560,1024]{1,0:T(8,128)(2,1)} %get-tuple-element.108.src.refs_0_, bf16[2560,512]{1,0:T(8,128)(2,1)} %get-tuple-element.173.refs_1_.gk, bf16[1024,1024]{1,0:T(8,128)(2,1)} %get-tuple-element.109.nlat.refs_2_, ...), custom_call_target="tpu_custom_call" | custom-call | flops 75161928 | bytes 262144 | tf_op jit(solution)/shard_map/grad_query_keys/pallas_call | solution.py:38
  288.6 1.6 copy-done
  290.2 1.7 convert_select_fusion
  292.1 5.9 %collective-permute-start.55 = (bf16[64,256]{1,0:T(8,128)(2,1)S(1)}, bf16[64,256]{1,0:T(8,128)(2,1)S(1)}, u32[]{:S(2)}, u32[]{:S(2)}) collective-permute-start(bf16[64,256]{1,0:T(8,128)(2,1)S(1)} %get-tuple-element.234), channel_id=1, source_target_pairs={{8,0},{10,2},{12,4},{14,6},{16,8},{18,10},{20,12},{22,14},{24,16},... | collective-permute-start | bytes 98312 | tf_op jit(solution)/shard_map/ppermute | solution.py:495
  300.2 3.3 collective-permute-start.52
  303.4 13.0 %source_back0.1 = (f32[16,128,1024]{2,1,0:T(8,128)}, f32[16,32,1024]{2,1,0:T(8,128)}, f32[4,1024]{1,0:T(4,128)}) custom-call(s32[4]{0:T(128)} %pad_add_fusion.ids.ids_ref, s32[16]{0:T(128)} %compare_convert_fusion.live, bf16[2560,512]{1,0:T(8,128)(2,1)} %get-tuple-element.173.refs_1_.gk, bf16[2560,512]{1,0:T(8,128)(2,1)} %get-tuple-element.161.refs_1_.gv, ...), custom_call_target="tpu_custom_call" | custom-call | flops 53687092 | bytes 435650 | tf_op jit(solution)/shard_map/source_back0/pallas_call | solution.py:38
  317.8 12.9 %source_back1.1 = (f32[16,128,1024]{2,1,0:T(8,128)}, f32[16,32,1024]{2,1,0:T(8,128)}, f32[4,1024]{1,0:T(4,128)}) custom-call(s32[4]{0:T(128)} %pad_add_fusion.ids.ids_ref, s32[16]{0:T(128)} %compare_convert_fusion.live, bf16[2560,512]{1,0:T(8,128)(2,1)} %get-tuple-element.173.refs_1_.gk, ...), custom_call_target="tpu_custom_call", output_to_operand_aliasing={{0}: (14, {}), {1}: (15, {})} | custom-call | flops 53687092 | bytes 645365 | tf_op jit(solution)/shard_map/source_back1/pallas_call | solution.py:38
  331.8 2.9 collective-permute-start.61
  334.7 1.5 collective-permute-start.59
  338.2 1.8 collective-permute-start.46
  340.1 1.4 collective-permute-start.45
  341.7 1.7 collective-permute-start.57
  343.5 10.3 %collective-permute-done.57 = f32[6,1024]{1,0:T(8,128)S(1)} collective-permute-done((f32[6,1024]{1,0:T(8,128)S(1)}, f32[6,1024]{1,0:T(8,128)S(1)}, u32[]{:S(2)}, u32[]{:S(2)}) %collective-permute-start.57) | collective-permute-done | bytes 24608 | tf_op jit(solution)/shard_map/ppermute | solution.py:510
  353.9 2.1 collective-permute-start.65
  355.9 2.0 collective-permute-start.64
  358.8 1.7 collective-permute-start.49
  363.2 3.7 collective-permute-done.48
  369.1 1.8 convert_bitcast_fusion
  370.9 1.8 convert_element_type.485
  (242 shorter events, 54.2 us)
Async XLA Ops:
  7.2 123.1 %all-gather.3.cloned.1.call-start = ((), (), s32[]{:S(2)}) async-start(), calls=%async_computation.2 | async-start | bytes 4456448 | tf_op jit(solution)/shard_map/all_gather | solution.py:556
  7.9 122.4 %all-gather.5.cloned.1.call-start = ((), (), s32[]{:S(2)}) async-start(), calls=%async_computation.3 | async-start | bytes 4456448 | tf_op jit(solution)/shard_map/all_gather | solution.py:557
  8.7 360.4 %reduce-scatter.5.cloned.1.call-start = ((), (), s32[]{:S(2)}) async-start(), calls=%async_computation.5 | async-start | bytes 4456448 | tf_op jit(solution)/shard_map/reduce_scatter | solution.py:763
  10.5 8.8 %collective-permute-start.2 = (bf16[64,512]{1,0:T(8,128)(2,1)S(1)}, bf16[64,512]{1,0:T(8,128)(2,1)S(1)}, u32[]{:S(2)}, u32[]{:S(2)}) collective-permute-start(bf16[64,512]{1,0:T(8,128)(2,1)S(1)} %get-tuple-element.260), channel_id=1, source_target_pairs={{24,0},{26,2},{28,4},{30,6},{0,8},{2,10},{4,12},{6,14},{8,16},{10,... | collective-permute-start | bytes 196616 | tf_op jit(solution)/shard_map/ppermute | solution.py:495
  13.6 8.5 %collective-permute-start.1 = (bf16[64,512]{1,0:T(8,128)(2,1)S(1)}, bf16[64,512]{1,0:T(8,128)(2,1)S(1)}, u32[]{:S(2)}, u32[]{:S(2)}) collective-permute-start(bf16[64,512]{1,0:T(8,128)(2,1)S(1)} %get-tuple-element.260), channel_id=1, source_target_pairs={{16,0},{18,2},{20,4},{22,6},{24,8},{26,10},{28,12},{30,14},{0,16},... | collective-permute-start | bytes 196616 | tf_op jit(solution)/shard_map/ppermute | solution.py:495
  18.3 6.4 %collective-permute-start.12 = (bf16[64,512]{1,0:T(8,128)(2,1)S(1)}, bf16[64,512]{1,0:T(8,128)(2,1)S(1)}, u32[]{:S(2)}, u32[]{:S(2)}) collective-permute-start(bf16[64,512]{1,0:T(8,128)(2,1)S(1)} %pad_maximum_fusion.4), channel_id=1, source_target_pairs={{24,0},{26,2},{28,4},{30,6},{0,8},{2,10},{4,12},{6,14},{8,16},{10,... | collective-permute-start | bytes 196616 | tf_op jit(solution)/shard_map/ppermute | solution.py:495
  19.0 9.5 %collective-permute-start.11 = (bf16[64,512]{1,0:T(8,128)(2,1)S(1)}, bf16[64,512]{1,0:T(8,128)(2,1)S(1)}, u32[]{:S(2)}, u32[]{:S(2)}) collective-permute-start(bf16[64,512]{1,0:T(8,128)(2,1)S(1)} %pad_maximum_fusion.4), channel_id=1, source_target_pairs={{16,0},{18,2},{20,4},{22,6},{24,8},{26,10},{28,12},{30,14},{0,16},... | collective-permute-start | bytes 196616 | tf_op jit(solution)/shard_map/ppermute | solution.py:495
  19.3 9.2 %collective-permute-start.10 = (bf16[64,512]{1,0:T(8,128)(2,1)S(1)}, bf16[64,512]{1,0:T(8,128)(2,1)S(1)}, u32[]{:S(2)}, u32[]{:S(2)}) collective-permute-start(bf16[64,512]{1,0:T(8,128)(2,1)S(1)} %pad_maximum_fusion.4), channel_id=1, source_target_pairs={{8,0},{10,2},{12,4},{14,6},{16,8},{18,10},{20,12},{22,14},{24,16},... | collective-permute-start | bytes 196616 | tf_op jit(solution)/shard_map/ppermute | solution.py:495
  28.6 10.6 %collective-permute-start.18 = (bf16[4,64,512]{2,1,0:T(8,128)(2,1)S(1)}, bf16[4,64,512]{2,1,0:T(8,128)(2,1)S(1)}, u32[]{:S(2)}, u32[]{:S(2)}) collective-permute-start(bf16[4,64,512]{2,1,0:T(8,128)(2,1)S(1)} %pad_maximum_fusion.1.refs_0_), channel_id=1, source_target_pairs={{5,0},{4,1},{7,2},{6,3},{1,4},{0,5},{3,6},{2,7},{13,8},{12,9},{15,... | collective-permute-start | bytes 786440 | tf_op jit(solution)/shard_map/ppermute | solution.py:510
  32.0 13.4 %collective-permute-start.16 = (bf16[4,64,512]{2,1,0:T(8,128)(2,1)S(1)}, bf16[4,64,512]{2,1,0:T(8,128)(2,1)S(1)}, u32[]{:S(2)}, u32[]{:S(2)}) collective-permute-start(bf16[4,64,512]{2,1,0:T(8,128)(2,1)S(1)} %pad_maximum_fusion.1.refs_0_), channel_id=1, source_target_pairs={{1,0},{0,1},{3,2},{2,3},{5,4},{4,5},{7,6},{6,7},{9,8},{8,9},{11,10... | collective-permute-start | bytes 786440 | tf_op jit(solution)/shard_map/ppermute | solution.py:510
  32.5 17.9 %collective-permute-start.8 = (bf16[4,64,512]{2,1,0:T(8,128)(2,1)S(1)}, bf16[4,64,512]{2,1,0:T(8,128)(2,1)S(1)}, u32[]{:S(2)}, u32[]{:S(2)}) collective-permute-start(bf16[4,64,512]{2,1,0:T(8,128)(2,1)S(1)} %pad_maximum_fusion.refs_0_), channel_id=1, source_target_pairs={{5,0},{4,1},{7,2},{6,3},{1,4},{0,5},{3,6},{2,7},{13,8},{12,9},{15,... | collective-permute-start | bytes 786440 | tf_op jit(solution)/shard_map/ppermute | solution.py:510
  33.8 19.0 %collective-permute-start.6 = (bf16[4,64,512]{2,1,0:T(8,128)(2,1)S(1)}, bf16[4,64,512]{2,1,0:T(8,128)(2,1)S(1)}, u32[]{:S(2)}, u32[]{:S(2)}) collective-permute-start(bf16[4,64,512]{2,1,0:T(8,128)(2,1)S(1)} %pad_maximum_fusion.refs_0_), channel_id=1, source_target_pairs={{1,0},{0,1},{3,2},{2,3},{5,4},{4,5},{7,6},{6,7},{9,8},{8,9},{11,10... | collective-permute-start | bytes 786440 | tf_op jit(solution)/shard_map/ppermute | solution.py:510
  34.1 18.9 %collective-permute-start.4 = (bf16[4,64,512]{2,1,0:T(8,128)(2,1)S(1)}, bf16[4,64,512]{2,1,0:T(8,128)(2,1)S(1)}, u32[]{:S(2)}, u32[]{:S(2)}) collective-permute-start(bf16[4,64,512]{2,1,0:T(8,128)(2,1)S(1)} %pad_maximum_fusion.refs_0_), channel_id=1, source_target_pairs={{4,0},{5,1},{6,2},{7,3},{0,4},{1,5},{2,6},{3,7},{12,8},{13,9},{14,... | collective-permute-start | bytes 786440 | tf_op jit(solution)/shard_map/ppermute | solution.py:510
  39.2 22.2 %collective-permute-start.14 = (bf16[4,64,512]{2,1,0:T(8,128)(2,1)S(1)}, bf16[4,64,512]{2,1,0:T(8,128)(2,1)S(1)}, u32[]{:S(2)}, u32[]{:S(2)}) collective-permute-start(bf16[4,64,512]{2,1,0:T(8,128)(2,1)S(1)} %pad_maximum_fusion.1.refs_0_), channel_id=1, source_target_pairs={{4,0},{5,1},{6,2},{7,3},{0,4},{1,5},{2,6},{3,7},{12,8},{13,9},{14,... | collective-permute-start | bytes 786440 | tf_op jit(solution)/shard_map/ppermute | solution.py:510
  45.4 16.0 %collective-permute-start.3 = (bf16[4,64,512]{2,1,0:T(8,128)(2,1)S(1)}, bf16[4,64,512]{2,1,0:T(8,128)(2,1)S(1)}, u32[]{:S(2)}, u32[]{:S(2)}) collective-permute-start(bf16[4,64,512]{2,1,0:T(8,128)(2,1)S(1)} %pad_maximum_fusion.refs_0_), channel_id=1, source_target_pairs={{2,0},{0,2},{6,4},{4,6},{10,8},{8,10},{14,12},{12,14},{18,16},{16,... | collective-permute-start | bytes 786440 | tf_op jit(solution)/shard_map/ppermute | solution.py:495
  50.5 11.4 %collective-permute-start.9 = (bf16[4,64,512]{2,1,0:T(8,128)(2,1)S(1)}, bf16[4,64,512]{2,1,0:T(8,128)(2,1)S(1)}, u32[]{:S(2)}, u32[]{:S(2)}) collective-permute-start(bf16[4,64,512]{2,1,0:T(8,128)(2,1)S(1)} %collective-permute-done.8.refs_6_), channel_id=1, source_target_pairs={{2,0},{0,2},{6,4},{4,6},{10,8},{8,10},{14,12},{12,14},{18,16},{16,... | collective-permute-start | bytes 786440 | tf_op jit(solution)/shard_map/ppermute | solution.py:495
  52.8 9.2 %collective-permute-start.7 = (bf16[4,64,512]{2,1,0:T(8,128)(2,1)S(1)}, bf16[4,64,512]{2,1,0:T(8,128)(2,1)S(1)}, u32[]{:S(2)}, u32[]{:S(2)}) collective-permute-start(bf16[4,64,512]{2,1,0:T(8,128)(2,1)S(1)} %collective-permute-done.6.refs_4_), channel_id=1, source_target_pairs={{2,0},{0,2},{6,4},{4,6},{10,8},{8,10},{14,12},{12,14},{18,16},{16,... | collective-permute-start | bytes 786440 | tf_op jit(solution)/shard_map/ppermute | solution.py:495
  53.0 20.9 %collective-permute-start.5 = (bf16[4,64,512]{2,1,0:T(8,128)(2,1)S(1)}, bf16[4,64,512]{2,1,0:T(8,128)(2,1)}, u32[]{:S(2)}, u32[]{:S(2)}) collective-permute-start(bf16[4,64,512]{2,1,0:T(8,128)(2,1)S(1)} %collective-permute-done.4.refs_2_), channel_id=1, source_target_pairs={{2,0},{0,2},{6,4},{4,6},{10,8},{8,10},{14,12},{12,14},{18,16},{16,... | collective-permute-start | bytes 786440 | tf_op jit(solution)/shard_map/ppermute | solution.py:495
  61.4 27.6 %collective-permute-start.13 = (bf16[4,64,512]{2,1,0:T(8,128)(2,1)S(1)}, bf16[4,64,512]{2,1,0:T(8,128)(2,1)S(1)}, u32[]{:S(2)}, u32[]{:S(2)}) collective-permute-start(bf16[4,64,512]{2,1,0:T(8,128)(2,1)S(1)} %pad_maximum_fusion.1.refs_0_), channel_id=1, source_target_pairs={{2,0},{0,2},{6,4},{4,6},{10,8},{8,10},{14,12},{12,14},{18,16},{16,... | collective-permute-start | bytes 786440 | tf_op jit(solution)/shard_map/ppermute | solution.py:495
  61.4 27.6 %collective-permute-start.19 = (bf16[4,64,512]{2,1,0:T(8,128)(2,1)S(1)}, bf16[4,64,512]{2,1,0:T(8,128)(2,1)S(1)}, u32[]{:S(2)}, u32[]{:S(2)}) collective-permute-start(bf16[4,64,512]{2,1,0:T(8,128)(2,1)S(1)} %collective-permute-done.18.refs_6_), channel_id=1, source_target_pairs={{2,0},{0,2},{6,4},{4,6},{10,8},{8,10},{14,12},{12,14},{18,16},{16,... | collective-permute-start | bytes 786440 | tf_op jit(solution)/shard_map/ppermute | solution.py:495
  61.9 27.1 %collective-permute-start.17 = (bf16[4,64,512]{2,1,0:T(8,128)(2,1)S(1)}, bf16[4,64,512]{2,1,0:T(8,128)(2,1)S(1)}, u32[]{:S(2)}, u32[]{:S(2)}) collective-permute-start(bf16[4,64,512]{2,1,0:T(8,128)(2,1)S(1)} %collective-permute-done.16.refs_4_), channel_id=1, source_target_pairs={{2,0},{0,2},{6,4},{4,6},{10,8},{8,10},{14,12},{12,14},{18,16},{16,... | collective-permute-start | bytes 786440 | tf_op jit(solution)/shard_map/ppermute | solution.py:495
  62.7 26.3 %collective-permute-start.15 = (bf16[4,64,512]{2,1,0:T(8,128)(2,1)S(1)}, bf16[4,64,512]{2,1,0:T(8,128)(2,1)}, u32[]{:S(2)}, u32[]{:S(2)}) collective-permute-start(bf16[4,64,512]{2,1,0:T(8,128)(2,1)S(1)} %collective-permute-done.14.refs_2_), channel_id=1, source_target_pairs={{2,0},{0,2},{6,4},{4,6},{10,8},{8,10},{14,12},{12,14},{18,16},{16,... | collective-permute-start | bytes 786440 | tf_op jit(solution)/shard_map/ppermute | solution.py:495
  87.6 13.7 %collective-permute-start.20 = (f32[16,2,512]{2,1,0:T(2,128)}, f32[16,2,512]{2,1,0:T(2,128)S(1)}, u32[]{:S(2)}, u32[]{:S(2)}) collective-permute-start(f32[16,2,512]{2,1,0:T(2,128)} %get-tuple-element.117), channel_id=1, source_target_pairs={{1,0},{0,1},{3,2},{2,3},{5,4},{4,5},{7,6},{6,7},{9,8},{8,9},{11,10... | collective-permute-start | bytes 196616 | tf_op jit(solution)/shard_map/ppermute | solution.py:498
  107.4 8.2 %collective-permute-start.21 = (bf16[256,512]{1,0:T(8,128)(2,1)}, bf16[256,512]{1,0:T(8,128)(2,1)S(1)}, u32[]{:S(2)}, u32[]{:S(2)}) collective-permute-start(bf16[256,512]{1,0:T(8,128)(2,1)} %bitcast.260), channel_id=1, source_target_pairs={{0,1},{1,0},{2,3},{3,2},{4,5},{5,4},{6,7},{7,6},{8,9},{9,8},{10,11... | collective-permute-start | bytes 786440 | tf_op jit(solution)/shard_map/ppermute | solution.py:501
  113.6 8.0 %collective-permute-start.22 = (bf16[256,512]{1,0:T(8,128)(2,1)}, bf16[256,512]{1,0:T(8,128)(2,1)S(1)}, u32[]{:S(2)}, u32[]{:S(2)}) collective-permute-start(bf16[256,512]{1,0:T(8,128)(2,1)} %bitcast.259), channel_id=1, source_target_pairs={{0,1},{1,0},{2,3},{3,2},{4,5},{5,4},{6,7},{7,6},{8,9},{9,8},{10,11... | collective-permute-start | bytes 786440 | tf_op jit(solution)/shard_map/ppermute | solution.py:501
  120.3 26.2 %collective-permute-start.23 = (bf16[256,1024]{1,0:T(8,128)(2,1)}, bf16[256,1024]{1,0:T(8,128)(2,1)S(1)}, u32[]{:S(2)}, u32[]{:S(2)}) collective-permute-start(bf16[256,1024]{1,0:T(8,128)(2,1)} %get-tuple-element.121.refs_0_), channel_id=1, source_target_pairs={{1,0},{0,1},{3,2},{2,3},{5,4},{4,5},{7,6},{6,7},{9,8},{8,9},{11,10... | collective-permute-start | bytes 1572872 | tf_op jit(solution)/shard_map/ppermute | solution.py:498
  126.3 32.0 %collective-permute-start.24 = (bf16[256,1024]{1,0:T(8,128)(2,1)}, bf16[256,1024]{1,0:T(8,128)(2,1)S(1)}, u32[]{:S(2)}, u32[]{:S(2)}) collective-permute-start(bf16[256,1024]{1,0:T(8,128)(2,1)} %get-tuple-element.126.refs_1_), channel_id=1, source_target_pairs={{1,0},{0,1},{3,2},{2,3},{5,4},{4,5},{7,6},{6,7},{9,8},{8,9},{11,10... | collective-permute-start | bytes 1572872 | tf_op jit(solution)/shard_map/ppermute | solution.py:498
  179.4 191.5 %reduce-scatter.3.cloned.1.call-start = ((), (), s32[]{:S(2)}) async-start(), calls=%async_computation.4 | async-start | bytes 4456448 | tf_op jit(solution)/shard_map/reduce_scatter | solution.py:764
  180.4 14.8 %collective-permute-start.25 = (bf16[256,1024]{1,0:T(8,128)(2,1)S(1)}, bf16[256,1024]{1,0:T(8,128)(2,1)S(1)}, u32[]{:S(2)}, u32[]{:S(2)}) collective-permute-start(bf16[256,1024]{1,0:T(8,128)(2,1)S(1)} %copy-done.40), channel_id=1, source_target_pairs={{0,1},{1,0},{2,3},{3,2},{4,5},{5,4},{6,7},{7,6},{8,9},{9,8},{10,11... | collective-permute-start | bytes 1572872 | tf_op jit(solution)/shard_map/ppermute | solution.py:501
  181.2 25.3 %collective-permute-start.26 = (bf16[256,1024]{1,0:T(8,128)(2,1)S(1)}, bf16[256,1024]{1,0:T(8,128)(2,1)S(1)}, u32[]{:S(2)}, u32[]{:S(2)}) collective-permute-start(bf16[256,1024]{1,0:T(8,128)(2,1)S(1)} %copy-done.38), channel_id=1, source_target_pairs={{0,1},{1,0},{2,3},{3,2},{4,5},{5,4},{6,7},{7,6},{8,9},{9,8},{10,11... | collective-permute-start | bytes 1572872 | tf_op jit(solution)/shard_map/ppermute | solution.py:501
  201.1 16.4 %collective-permute-start.31 = (bf16[256,512]{1,0:T(8,128)(2,1)}, bf16[256,512]{1,0:T(8,128)(2,1)S(1)}, u32[]{:S(2)}, u32[]{:S(2)}) collective-permute-start(bf16[256,512]{1,0:T(8,128)(2,1)} %get-tuple-element.159.grad_keep), channel_id=1, source_target_pairs={{1,0},{0,1},{3,2},{2,3},{5,4},{4,5},{7,6},{6,7},{9,8},{8,9},{11,10... | collective-permute-start | bytes 786440 | tf_op jit(solution)/shard_map/ppermute | solution.py:498
  206.5 79.3 %collective-permute-start.28 = (bf16[256,1024]{1,0:T(8,128)(2,1)S(1)}, bf16[256,1024]{1,0:T(8,128)(2,1)S(1)}, u32[]{:S(2)}, u32[]{:S(2)}) collective-permute-start(bf16[256,1024]{1,0:T(8,128)(2,1)S(1)} %copy-done.37), channel_id=1, source_target_pairs={{0,1},{1,0},{2,3},{3,2},{4,5},{5,4},{6,7},{7,6},{8,9},{9,8},{10,11... | collective-permute-start | bytes 1572872 | tf_op jit(solution)/shard_map/ppermute | solution.py:501
  216.2 17.0 %collective-permute-start.30 = (bf16[256,512]{1,0:T(8,128)(2,1)}, bf16[256,512]{1,0:T(8,128)(2,1)S(1)}, u32[]{:S(2)}, u32[]{:S(2)}) collective-permute-start(bf16[256,512]{1,0:T(8,128)(2,1)} %get-tuple-element.157.grad_keep), channel_id=1, source_target_pairs={{1,0},{0,1},{3,2},{2,3},{5,4},{4,5},{7,6},{6,7},{9,8},{8,9},{11,10... | collective-permute-start | bytes 786440 | tf_op jit(solution)/shard_map/ppermute | solution.py:498
  217.5 11.7 %collective-permute-start.29 = (bf16[8,64,512]{2,1,0:T(8,128)(2,1)}, bf16[8,64,512]{2,1,0:T(8,128)(2,1)S(1)}, u32[]{:S(2)}, u32[]{:S(2)}) collective-permute-start(bf16[8,64,512]{2,1,0:T(8,128)(2,1)} %get-tuple-element.155), channel_id=1, source_target_pairs={{2,0},{0,2},{6,4},{4,6},{10,8},{8,10},{14,12},{12,14},{18,16},{16,... | collective-permute-start | bytes 1572872 | tf_op jit(solution)/shard_map/ppermute | solution.py:495
  229.4 30.1 %collective-permute-start.35 = (bf16[4,64,256]{2,1,0:T(8,128)(2,1)S(1)}, bf16[4,64,256]{2,1,0:T(8,128)(2,1)S(1)}, u32[]{:S(2)}, u32[]{:S(2)}) collective-permute-start(bf16[4,64,256]{2,1,0:T(8,128)(2,1)S(1)} %get-tuple-element.240), channel_id=1, source_target_pairs={{0,4},{1,5},{2,6},{3,7},{4,0},{5,1},{6,2},{7,3},{8,12},{9,13},{10,... | collective-permute-start | bytes 393224 | tf_op jit(solution)/shard_map/ppermute | solution.py:510
  231.7 28.7 %collective-permute-start.37 = (bf16[4,64,256]{2,1,0:T(8,128)(2,1)S(1)}, bf16[4,64,256]{2,1,0:T(8,128)(2,1)S(1)}, u32[]{:S(2)}, u32[]{:S(2)}) collective-permute-start(bf16[4,64,256]{2,1,0:T(8,128)(2,1)S(1)} %get-tuple-element.247), channel_id=1, source_target_pairs={{0,5},{1,4},{2,7},{3,6},{4,1},{5,0},{6,3},{7,2},{8,13},{9,12},{10,... | collective-permute-start | bytes 393224 | tf_op jit(solution)/shard_map/ppermute | solution.py:510
  232.5 29.1 %collective-permute-start.36 = (bf16[4,64,256]{2,1,0:T(8,128)(2,1)S(1)}, bf16[4,64,256]{2,1,0:T(8,128)(2,1)S(1)}, u32[]{:S(2)}, u32[]{:S(2)}) collective-permute-start(bf16[4,64,256]{2,1,0:T(8,128)(2,1)S(1)} %get-tuple-element.248), channel_id=1, source_target_pairs={{0,1},{1,0},{2,3},{3,2},{4,5},{5,4},{6,7},{7,6},{8,9},{9,8},{10,11... | collective-permute-start | bytes 393224 | tf_op jit(solution)/shard_map/ppermute | solution.py:510
  239.6 19.2 %collective-permute-start.34 = (f32[8,1,512]{2,1,0:T(1,128)}, f32[8,1,512]{2,1,0:T(1,128)S(1)}, u32[]{:S(2)}, u32[]{:S(2)}) collective-permute-start(f32[8,1,512]{2,1,0:T(1,128)} %get-tuple-element.171), channel_id=1, source_target_pairs={{1,0},{0,1},{3,2},{2,3},{5,4},{4,5},{7,6},{6,7},{9,8},{8,9},{11,10... | collective-permute-start | bytes 49160 | tf_op jit(solution)/shard_map/ppermute | solution.py:498
  259.5 27.5 %collective-permute-start.27 = (bf16[256,1024]{1,0:T(8,128)(2,1)S(1)}, bf16[256,1024]{1,0:T(8,128)(2,1)S(1)}, u32[]{:S(2)}, u32[]{:S(2)}) collective-permute-start(bf16[256,1024]{1,0:T(8,128)(2,1)S(1)} %copy-done.36), channel_id=1, source_target_pairs={{0,1},{1,0},{2,3},{3,2},{4,5},{5,4},{6,7},{7,6},{8,9},{9,8},{10,11... | collective-permute-start | bytes 1572872 | tf_op jit(solution)/shard_map/ppermute | solution.py:501
  260.4 39.7 %collective-permute-start.42 = (bf16[256,512]{1,0:T(8,128)(2,1)}, bf16[256,512]{1,0:T(8,128)(2,1)S(1)}, u32[]{:S(2)}, u32[]{:S(2)}) collective-permute-start(bf16[256,512]{1,0:T(8,128)(2,1)} %bitcast.257), channel_id=1, source_target_pairs={{0,1},{1,0},{2,3},{3,2},{4,5},{5,4},{6,7},{7,6},{8,9},{9,8},{10,11... | collective-permute-start | bytes 786440 | tf_op jit(solution)/shard_map/ppermute | solution.py:501
  261.7 30.3 %collective-permute-start.39 = (bf16[4,64,256]{2,1,0:T(8,128)(2,1)S(1)}, bf16[4,64,256]{2,1,0:T(8,128)(2,1)S(1)}, u32[]{:S(2)}, u32[]{:S(2)}) collective-permute-start(bf16[4,64,256]{2,1,0:T(8,128)(2,1)S(1)} %get-tuple-element.238), channel_id=1, source_target_pairs={{0,4},{1,5},{2,6},{3,7},{4,0},{5,1},{6,2},{7,3},{8,12},{9,13},{10,... | collective-permute-start | bytes 393224 | tf_op jit(solution)/shard_map/ppermute | solution.py:510
  263.4 34.6 %collective-permute-start.41 = (bf16[4,64,256]{2,1,0:T(8,128)(2,1)S(1)}, bf16[4,64,256]{2,1,0:T(8,128)(2,1)S(1)}, u32[]{:S(2)}, u32[]{:S(2)}) collective-permute-start(bf16[4,64,256]{2,1,0:T(8,128)(2,1)S(1)} %get-tuple-element.241), channel_id=1, source_target_pairs={{0,5},{1,4},{2,7},{3,6},{4,1},{5,0},{6,3},{7,2},{8,13},{9,12},{10,... | collective-permute-start | bytes 393224 | tf_op jit(solution)/shard_map/ppermute | solution.py:510
  285.8 12.2 %collective-permute-start.40 = (bf16[4,64,256]{2,1,0:T(8,128)(2,1)S(1)}, bf16[4,64,256]{2,1,0:T(8,128)(2,1)S(1)}, u32[]{:S(2)}, u32[]{:S(2)}) collective-permute-start(bf16[4,64,256]{2,1,0:T(8,128)(2,1)S(1)} %get-tuple-element.242), channel_id=1, source_target_pairs={{0,1},{1,0},{2,3},{3,2},{4,5},{5,4},{6,7},{7,6},{8,9},{9,8},{10,11... | collective-permute-start | bytes 393224 | tf_op jit(solution)/shard_map/ppermute | solution.py:510
  286.9 11.7 %collective-permute-start.38 = (bf16[8,64,1024]{2,1,0:T(8,128)(2,1)}, bf16[8,64,1024]{2,1,0:T(8,128)(2,1)S(1)}, u32[]{:S(2)}, u32[]{:S(2)}) collective-permute-start(bf16[8,64,1024]{2,1,0:T(8,128)(2,1)} %get-tuple-element.179), channel_id=1, source_target_pairs={{2,0},{0,2},{6,4},{4,6},{10,8},{8,10},{14,12},{12,14},{18,16},{16,... | collective-permute-start | bytes 3145736 | tf_op jit(solution)/shard_map/ppermute | solution.py:495
  292.1 38.6 %collective-permute-start.55 = (bf16[64,256]{1,0:T(8,128)(2,1)S(1)}, bf16[64,256]{1,0:T(8,128)(2,1)S(1)}, u32[]{:S(2)}, u32[]{:S(2)}) collective-permute-start(bf16[64,256]{1,0:T(8,128)(2,1)S(1)} %get-tuple-element.234), channel_id=1, source_target_pairs={{8,0},{10,2},{12,4},{14,6},{16,8},{18,10},{20,12},{22,14},{24,16},... | collective-permute-start | bytes 98312 | tf_op jit(solution)/shard_map/ppermute | solution.py:495
  298.0 33.7 %collective-permute-start.54 = (bf16[64,256]{1,0:T(8,128)(2,1)S(1)}, bf16[64,256]{1,0:T(8,128)(2,1)S(1)}, u32[]{:S(2)}, u32[]{:S(2)}) collective-permute-start(bf16[64,256]{1,0:T(8,128)(2,1)S(1)} %get-tuple-element.235), channel_id=1, source_target_pairs={{16,0},{18,2},{20,4},{22,6},{24,8},{26,10},{28,12},{30,14},{0,16},... | collective-permute-start | bytes 98312 | tf_op jit(solution)/shard_map/ppermute | solution.py:495
  298.0 33.8 %collective-permute-start.53 = (bf16[64,256]{1,0:T(8,128)(2,1)S(1)}, bf16[64,256]{1,0:T(8,128)(2,1)S(1)}, u32[]{:S(2)}, u32[]{:S(2)}) collective-permute-start(bf16[64,256]{1,0:T(8,128)(2,1)S(1)} %get-tuple-element.236), channel_id=1, source_target_pairs={{24,0},{26,2},{28,4},{30,6},{0,8},{2,10},{4,12},{6,14},{8,16},{10,... | collective-permute-start | bytes 98312 | tf_op jit(solution)/shard_map/ppermute | solution.py:495
  298.7 17.8 %collective-permute-start.43 = (bf16[256,512]{1,0:T(8,128)(2,1)S(1)}, bf16[256,512]{1,0:T(8,128)(2,1)S(1)}, u32[]{:S(2)}, u32[]{:S(2)}) collective-permute-start(bf16[256,512]{1,0:T(8,128)(2,1)S(1)} %bitcast.258), channel_id=1, source_target_pairs={{0,1},{1,0},{2,3},{3,2},{4,5},{5,4},{6,7},{7,6},{8,9},{9,8},{10,11... | collective-permute-start | bytes 786440 | tf_op jit(solution)/shard_map/ppermute | solution.py:501
  300.2 34.5 %collective-permute-start.52 = (bf16[64,256]{1,0:T(8,128)(2,1)S(1)}, bf16[64,256]{1,0:T(8,128)(2,1)S(1)}, u32[]{:S(2)}, u32[]{:S(2)}) collective-permute-start(bf16[64,256]{1,0:T(8,128)(2,1)S(1)} %get-tuple-element.231), channel_id=1, source_target_pairs={{8,0},{10,2},{12,4},{14,6},{16,8},{18,10},{20,12},{22,14},{24,16},... | collective-permute-start | bytes 98312 | tf_op jit(solution)/shard_map/ppermute | solution.py:495
  316.5 18.2 %collective-permute-start.51 = (bf16[64,256]{1,0:T(8,128)(2,1)S(1)}, bf16[64,256]{1,0:T(8,128)(2,1)S(1)}, u32[]{:S(2)}, u32[]{:S(2)}) collective-permute-start(bf16[64,256]{1,0:T(8,128)(2,1)S(1)} %get-tuple-element.232), channel_id=1, source_target_pairs={{16,0},{18,2},{20,4},{22,6},{24,8},{26,10},{28,12},{30,14},{0,16},... | collective-permute-start | bytes 98312 | tf_op jit(solution)/shard_map/ppermute | solution.py:495
  331.7 6.5 %collective-permute-start.62 = (f32[6,1024]{1,0:T(8,128)S(1)}, f32[6,1024]{1,0:T(8,128)S(1)}, u32[]{:S(2)}, u32[]{:S(2)}) collective-permute-start(f32[6,1024]{1,0:T(8,128)S(1)} %maximum_add_fusion.1), channel_id=1, source_target_pairs={{7,0},{6,1},{5,2},{4,3},{3,4},{2,5},{1,6},{0,7},{15,8},{14,9},{13,... | collective-permute-start | bytes 73736 | tf_op jit(solution)/shard_map/ppermute | solution.py:510
  331.8 8.3 %collective-permute-start.61 = (f32[6,1024]{1,0:T(8,128)S(1)}, f32[6,1024]{1,0:T(8,128)S(1)}, u32[]{:S(2)}, u32[]{:S(2)}) collective-permute-start(f32[6,1024]{1,0:T(8,128)S(1)} %maximum_add_fusion.1), channel_id=1, source_target_pairs={{3,0},{2,1},{1,2},{0,3},{7,4},{6,5},{5,6},{4,7},{11,8},{10,9},{9,1... | collective-permute-start | bytes 73736 | tf_op jit(solution)/shard_map/ppermute | solution.py:510
  334.7 6.8 %collective-permute-start.60 = (f32[6,1024]{1,0:T(8,128)S(1)}, f32[6,1024]{1,0:T(8,128)S(1)}, u32[]{:S(2)}, u32[]{:S(2)}) collective-permute-start(f32[6,1024]{1,0:T(8,128)S(1)} %maximum_add_fusion.1), channel_id=1, source_target_pairs={{6,0},{7,1},{4,2},{5,3},{2,4},{3,5},{0,6},{1,7},{14,8},{15,9},{12,... | collective-permute-start | bytes 73736 | tf_op jit(solution)/shard_map/ppermute | solution.py:510
  334.7 7.1 %collective-permute-start.59 = (f32[6,1024]{1,0:T(8,128)S(1)}, f32[6,1024]{1,0:T(8,128)S(1)}, u32[]{:S(2)}, u32[]{:S(2)}) collective-permute-start(f32[6,1024]{1,0:T(8,128)S(1)} %maximum_add_fusion.1), channel_id=1, source_target_pairs={{5,0},{4,1},{7,2},{6,3},{1,4},{0,5},{3,6},{2,7},{13,8},{12,9},{15,... | collective-permute-start | bytes 73736 | tf_op jit(solution)/shard_map/ppermute | solution.py:510
  336.5 7.0 %collective-permute-start.58 = (f32[6,1024]{1,0:T(8,128)S(1)}, f32[6,1024]{1,0:T(8,128)S(1)}, u32[]{:S(2)}, u32[]{:S(2)}) collective-permute-start(f32[6,1024]{1,0:T(8,128)S(1)} %maximum_add_fusion.1), channel_id=1, source_target_pairs={{1,0},{0,1},{3,2},{2,3},{5,4},{4,5},{7,6},{6,7},{9,8},{8,9},{11,10... | collective-permute-start | bytes 73736 | tf_op jit(solution)/shard_map/ppermute | solution.py:510
  338.2 19.6 %collective-permute-start.46 = (bf16[4,64,512]{2,1,0:T(8,128)(2,1)S(1)}, bf16[4,64,512]{2,1,0:T(8,128)(2,1)S(1)}, u32[]{:S(2)}, u32[]{:S(2)}) collective-permute-start(bf16[4,64,512]{2,1,0:T(8,128)(2,1)S(1)} %get-tuple-element.221), channel_id=1, source_target_pairs={{0,5},{1,4},{2,7},{3,6},{4,1},{5,0},{6,3},{7,2},{8,13},{9,12},{10,... | collective-permute-start | bytes 786440 | tf_op jit(solution)/shard_map/ppermute | solution.py:510
  340.1 18.6 %collective-permute-start.45 = (bf16[4,64,512]{2,1,0:T(8,128)(2,1)S(1)}, bf16[4,64,512]{2,1,0:T(8,128)(2,1)S(1)}, u32[]{:S(2)}, u32[]{:S(2)}) collective-permute-start(bf16[4,64,512]{2,1,0:T(8,128)(2,1)S(1)} %get-tuple-element.222), channel_id=1, source_target_pairs={{0,1},{1,0},{2,3},{3,2},{4,5},{5,4},{6,7},{7,6},{8,9},{9,8},{10,11... | collective-permute-start | bytes 786440 | tf_op jit(solution)/shard_map/ppermute | solution.py:510
  341.5 17.2 %collective-permute-start.44 = (bf16[4,64,512]{2,1,0:T(8,128)(2,1)S(1)}, bf16[4,64,512]{2,1,0:T(8,128)(2,1)S(1)}, u32[]{:S(2)}, u32[]{:S(2)}) collective-permute-start(bf16[4,64,512]{2,1,0:T(8,128)(2,1)S(1)} %get-tuple-element.220), channel_id=1, source_target_pairs={{0,4},{1,5},{2,6},{3,7},{4,0},{5,1},{6,2},{7,3},{8,12},{9,13},{10,... | collective-permute-start | bytes 786440 | tf_op jit(solution)/shard_map/ppermute | solution.py:510
  341.7 12.1 %collective-permute-start.57 = (f32[6,1024]{1,0:T(8,128)S(1)}, f32[6,1024]{1,0:T(8,128)S(1)}, u32[]{:S(2)}, u32[]{:S(2)}) collective-permute-start(f32[6,1024]{1,0:T(8,128)S(1)} %maximum_add_fusion.1), channel_id=1, source_target_pairs={{4,0},{5,1},{6,2},{7,3},{0,4},{1,5},{2,6},{3,7},{12,8},{13,9},{14,... | collective-permute-start | bytes 73736 | tf_op jit(solution)/shard_map/ppermute | solution.py:510
  343.5 10.3 %collective-permute-start.56 = (f32[6,1024]{1,0:T(8,128)S(1)}, f32[6,1024]{1,0:T(8,128)S(1)}, u32[]{:S(2)}, u32[]{:S(2)}) collective-permute-start(f32[6,1024]{1,0:T(8,128)S(1)} %maximum_add_fusion.1), channel_id=1, source_target_pairs={{2,0},{0,2},{6,4},{4,6},{10,8},{8,10},{14,12},{12,14},{18,16},{16,... | collective-permute-start | bytes 73736 | tf_op jit(solution)/shard_map/ppermute | solution.py:495
  353.9 7.7 %collective-permute-start.65 = (f32[6,1024]{1,0:T(8,128)S(1)}, f32[6,1024]{1,0:T(8,128)S(1)}, u32[]{:S(2)}, u32[]{:S(2)}) collective-permute-start(f32[6,1024]{1,0:T(8,128)S(1)} %add_add_fusion.1), channel_id=1, source_target_pairs={{24,0},{26,2},{28,4},{30,6},{0,8},{2,10},{4,12},{6,14},{8,16},{10,... | collective-permute-start | bytes 73736 | tf_op jit(solution)/shard_map/ppermute | solution.py:495
  355.9 6.0 %collective-permute-start.64 = (f32[6,1024]{1,0:T(8,128)S(1)}, f32[6,1024]{1,0:T(8,128)S(1)}, u32[]{:S(2)}, u32[]{:S(2)}) collective-permute-start(f32[6,1024]{1,0:T(8,128)S(1)} %add_add_fusion.1), channel_id=1, source_target_pairs={{16,0},{18,2},{20,4},{22,6},{24,8},{26,10},{28,12},{30,14},{0,16},... | collective-permute-start | bytes 73736 | tf_op jit(solution)/shard_map/ppermute | solution.py:495
  360.5 6.4 %collective-permute-start.48 = (bf16[64,512]{1,0:T(8,128)(2,1)S(1)}, bf16[64,512]{1,0:T(8,128)(2,1)S(1)}, u32[]{:S(2)}, u32[]{:S(2)}) collective-permute-start(bf16[64,512]{1,0:T(8,128)(2,1)S(1)} %get-tuple-element.217), channel_id=1, source_target_pairs={{16,0},{18,2},{20,4},{22,6},{24,8},{26,10},{28,12},{30,14},{0,16},... | collective-permute-start | bytes 196616 | tf_op jit(solution)/shard_map/ppermute | solution.py:495
  361.5 6.1 %collective-permute-start.47 = (bf16[64,512]{1,0:T(8,128)(2,1)S(1)}, bf16[64,512]{1,0:T(8,128)(2,1)S(1)}, u32[]{:S(2)}, u32[]{:S(2)}) collective-permute-start(bf16[64,512]{1,0:T(8,128)(2,1)S(1)} %get-tuple-element.218), channel_id=1, source_target_pairs={{24,0},{26,2},{28,4},{30,6},{0,8},{2,10},{4,12},{6,14},{8,16},{10,... | collective-permute-start | bytes 196616 | tf_op jit(solution)/shard_map/ppermute | solution.py:495
  (49 other events, 429.9 us)
Sparse Core Ops, SparseCore 0:
  10.2 66.3 all-gather.2
  78.7 50.8 all-gather.4
  179.5 76.6 reduce-scatter.4
  260.4 72.2 reduce-scatter.2
